TPU v7x, 256 devices: a whole 4x4x8 slice. The times are simulated.
256 devices in a mesh: pipe: 2 (over x_hi), seg: 32 (over x_lo, z, core), dp: 4 (over y).
Axes of the slice: x: 4 (x_hi: 2, x_lo: 2; x = x_hi * 2 + x_lo), y: 4, z: 8, core: 2. Of those that a mesh axis runs over, the one named last changes fastest.
Arguments:
- inputs: bfloat16 [2, 4, 4096, 4096], P('pipe', 'dp', 'seg'), may hold values from -8 to 8
- mixed: bfloat16 [2, 4, 4096, 4096], P('pipe', 'dp', 'seg'), may hold values from -6 to 6
- gate_in: bfloat16 [2, 4, 4096, 4096], P('pipe', 'dp', 'seg'), may hold values from -6 to 6
- entry_states: float32 [2, 4, 32, 64, 64, 128], P('pipe', 'dp', 'seg'), may hold values from -6 to 6
- out_grad: bfloat16 [4, 4096, 4096], P('dp', 'seg'), may hold values from -6 to 6
- doc_lengths: int32 [4, 6], P('dp'), may hold values from 1 to 2048, 4096 in all within a row
- proj_weight: bfloat16 [2, 4096, 320], P('pipe', ('seg', 'dp')), may hold values from -0.05078125 to 0.05078125
- decay_rate: float32 [2, 64], P('pipe'), may hold values from 7.324219e-05 to 0.1
- dt_bias: float32 [2, 64], P('pipe'), may hold values from -1 to 1
- skip_gain: float32 [2, 64], P('pipe'), may hold values from 0.5 to 1.5
Outputs:
- input_grad: bfloat16 [2, 4, 4096, 4096], P('pipe', 'dp', 'seg')
- mixed_grad: bfloat16 [2, 4, 4096, 4096], P('pipe', 'dp', 'seg')
- gate_grad: bfloat16 [2, 4, 4096, 4096], P('pipe', 'dp', 'seg')
- weight_grad: float32 [2, 4096, 320], P('pipe', ('seg', 'dp'))
All inputs are finite; a program needn't handle non-finite values.
Results may differ from a plain program's by a relative error of at most 0.009.
Values may be sent and summed in bfloat16 or wider, within the bound.
A program may use at most 320 MiB of HBM per device.

v0:
```python
import jax
import jax.numpy as jnp
from jax import lax
from jax.sharding import PartitionSpec as P

highest = lax.Precision.HIGHEST


def swapped(value, axis, bit):
    mask = 2**bit
    pairs = [(source, source ^ mask) for source in range(lax.axis_size(axis))]
    return lax.ppermute(value, axis, pairs)


def passed_along(value, axis, by):
    count = lax.axis_size(axis)
    pairs = [(i, i + by) for i in range(count) if 0 <= i + by < count]
    return lax.ppermute(value, axis, pairs)


def block_states(xs_f, b_mat, dt_step, log_decay, counts):
    last_log = log_decay[-1]
    kept_mask = (counts == counts[-1]).astype(jnp.float32)
    weighting = jnp.exp(last_log[None, :] - log_decay) * kept_mask[:, None] * dt_step
    states = jnp.einsum("sh,shp,sn->hpn", weighting, xs_f, b_mat, precision=highest)
    passing = jnp.exp(last_log) * (counts[-1] == 0).astype(jnp.float32)
    return (states, passing)


def block_passing(dt_step, rates, counts):
    log_decay = jnp.cumsum(-dt_step * rates[None, :], axis=0)
    return jnp.exp(log_decay[-1]) * (counts[-1] == 0).astype(jnp.float32)


def block_scan(start_state, xs_f, b_mat, c_mat, dt_step, rates, counts):
    log_decay = jnp.cumsum(-dt_step * rates[None, :], axis=0)
    positions = jnp.arange(xs_f.shape[0], dtype=jnp.int32)
    causal = (positions[:, None] >= positions[None, :]) & (counts[:, None] == counts[None, :])
    gap_log = jnp.where(causal[:, :, None], log_decay[:, None, :] - log_decay[None, :, :], 0.0)
    decay_mat = jnp.exp(gap_log) * causal[:, :, None].astype(jnp.float32)
    scores = jnp.dot(c_mat, b_mat.T, precision=highest)
    mixing = decay_mat * scores[:, :, None] * dt_step[None, :, :]
    inner_out = jnp.einsum("tsh,shp->thp", mixing, xs_f, precision=highest)
    entry_weight = jnp.exp(log_decay) * (counts == 0).astype(jnp.float32)[:, None]
    carried = jnp.einsum("tn,hpn->thp", c_mat, start_state, precision=highest)
    states, passing = block_states(xs_f, b_mat, dt_step, log_decay, counts)
    return (
        inner_out + entry_weight[:, :, None] * carried,
        states + passing[:, None, None] * start_state,
    )


def entry_adjoint(c_mat, dt_step, rates, counts, grad_y):
    log_decay = jnp.cumsum(-dt_step * rates[None, :], axis=0)
    entry_weight = jnp.exp(log_decay) * (counts == 0).astype(jnp.float32)[:, None]
    return jnp.einsum("th,tn,thp->hpn", entry_weight, c_mat, grad_y, precision=highest)


def block_grads(start_state, exit_adj, xs_f, b_mat, c_mat, dt_step, rates, counts, grad_y):

    def local_fn(state_in, xs_in, b_in, c_in, dt_in):
        return block_scan(state_in, xs_in, b_in, c_in, dt_in, rates, counts)

    results, pullback = jax.vjp(local_fn, start_state, xs_f, b_mat, c_mat, dt_step)
    gradients = pullback((grad_y, exit_adj))
    return (results[0], gradients[1], gradients[2], gradients[3], gradients[4])


def layer_tail(
    xs_f,
    gate_in,
    grad_in,
    weights,
    dt_raw,
    skip_gain,
    y_ssd,
    grad_y,
    grad_xs,
    grad_b,
    grad_c,
    grad_dt,
):
    rows_all = gate_in.shape[0]
    gate_f = gate_in.astype(jnp.float32)
    gate_sig = jax.nn.sigmoid(gate_f)
    y_full = (y_ssd + skip_gain[None, :, None] * xs_f).reshape(rows_all, -1)
    grad_gate = (grad_in * y_full * gate_sig * (1.0 + gate_f * (1.0 - gate_sig))).astype(
        jnp.bfloat16
    )
    grad_mixed = (
        (grad_xs + skip_gain[None, :, None] * grad_y).reshape(rows_all, -1).astype(jnp.bfloat16)
    )
    grad_proj = jnp.concatenate([grad_b, grad_c, grad_dt * jax.nn.sigmoid(dt_raw)], axis=1).astype(
        jnp.bfloat16
    )
    back_term = jnp.einsum("te,de->td", grad_proj, weights, preferred_element_type=jnp.float32)
    grad_x = (grad_in + back_term).astype(jnp.bfloat16)
    return (grad_x, grad_mixed, grad_gate, grad_proj)


def combine_pairs(earlier, later):
    return (earlier[0] * later[0], later[0][..., None, None] * earlier[1] + later[1])


def later_adjoints(element, seg_idx, ones_head, zeros_state):
    levels = lax.axis_size("seg").bit_length() - 1
    total = element
    below = (ones_head, zeros_state)
    for level in range(levels):
        other = swapped((total[0], total[1]), "seg", level)
        partner_after = seg_idx // (1 << level) % 2 == 0
        joined = combine_pairs(other, below)
        below = (
            jnp.where(partner_after, joined[0], below[0]),
            jnp.where(partner_after, joined[1], below[1]),
        )
        high_first = combine_pairs(other, total)
        low_first = combine_pairs(total, other)
        total = (
            jnp.where(partner_after, high_first[0], low_first[0]),
            jnp.where(partner_after, high_first[1], low_first[1]),
        )
    return below[1]


def local(
    inputs,
    mixed,
    gate_in,
    entry_states,
    out_grad,
    doc_lengths,
    proj_weight,
    decay_rate,
    dt_bias,
    skip_gain,
):
    weights = lax.all_gather(proj_weight, ("seg", "dp"), axis=1, tiled=True)[0]
    rates = decay_rate[0]
    dt_shift = dt_bias[0]
    skip_vec = skip_gain[0]
    x_local = inputs[0]
    xs_local = mixed[0]
    gate_local = gate_in[0]
    entry_local = entry_states[0][:, 0]
    batches = x_local.shape[0]
    rows_seg = x_local.shape[1]
    width = x_local.shape[2]
    head_count = rates.shape[0]
    head_size = xs_local.shape[2] // head_count
    state_dim = (weights.shape[1] - head_count) // 2
    proj_cols = weights.shape[1]
    section_idx = lax.axis_index("pipe")
    seg_idx = lax.axis_index("seg")
    positions = seg_idx * rows_seg + jnp.arange(rows_seg, dtype=jnp.int32)
    doc_ends = jnp.cumsum(doc_lengths, axis=1)
    starts = doc_ends[:, :-1]
    resets = jnp.any(positions[None, :, None] == starts[:, None, :], axis=2).astype(jnp.int32)
    counts = jnp.cumsum(resets, axis=1)
    projected = jnp.einsum("btd,de->bte", x_local, weights, preferred_element_type=jnp.float32)
    b_all = projected[:, :, :state_dim]
    c_all = projected[:, :, state_dim : 2 * state_dim]
    raw_all = projected[:, :, 2 * state_dim :] + dt_shift[None, None, :]
    dt_all = jax.nn.softplus(raw_all)
    xs_all = xs_local.astype(jnp.float32).reshape(batches, rows_seg, head_count, head_size)
    passings = jax.vmap(lambda da, ca: block_passing(da, rates, ca))(dt_all, counts)
    ones_head = jnp.ones((head_count,), jnp.float32)
    zeros_state = jnp.zeros((head_count, head_size, state_dim), jnp.float32)
    received = jnp.zeros((rows_seg, width), jnp.bfloat16)
    grad_inputs = jnp.zeros_like(x_local)
    grad_mixes = jnp.zeros_like(x_local)
    grad_gates = jnp.zeros_like(x_local)
    proj_grads = jnp.zeros((batches, rows_seg, proj_cols), jnp.bfloat16)
    for step_idx in range(batches + 1):
        batch_idx = step_idx - 1 + section_idx
        active = (batch_idx >= 0) & (batch_idx < batches)
        slot_idx = jnp.clip(batch_idx, 0, batches - 1)

        def select(array):
            return lax.dynamic_index_in_dim(array, slot_idx, 0, keepdims=False)

        incoming = jnp.where(section_idx == 1, select(out_grad), received)
        grad_in = incoming.astype(jnp.float32)
        gate_pick = select(gate_local)
        gate_act = jax.nn.silu(gate_pick.astype(jnp.float32))
        grad_y = (grad_in * gate_act).reshape(rows_seg, head_count, head_size)
        c_pick = select(c_all)
        dt_pick = select(dt_all)
        count_pick = select(counts)
        own_adj = entry_adjoint(c_pick, dt_pick, rates, count_pick, grad_y)
        exit_adj = later_adjoints((select(passings), own_adj), seg_idx, ones_head, zeros_state)

        def working(operand):
            xs_pick = select(xs_all)
            y_ssd, grad_xs, grad_b, grad_c, grad_dt = block_grads(
                select(entry_local),
                exit_adj,
                xs_pick,
                select(b_all),
                c_pick,
                dt_pick,
                rates,
                count_pick,
                grad_y,
            )
            return layer_tail(
                xs_pick,
                gate_pick,
                grad_in,
                weights,
                select(raw_all),
                skip_vec,
                y_ssd,
                grad_y,
                grad_xs,
                grad_b,
                grad_c,
                grad_dt,
            )

        def resting(operand):
            blank = jnp.zeros((rows_seg, width), jnp.bfloat16)
            return (blank, blank, blank, jnp.zeros((rows_seg, proj_cols), jnp.bfloat16))

        grad_x, grad_mixed, grad_gate, grad_proj = lax.cond(active, working, resting, 0)
        grad_inputs = jnp.where(
            active, lax.dynamic_update_index_in_dim(grad_inputs, grad_x, slot_idx, 0), grad_inputs
        )
        grad_mixes = jnp.where(
            active, lax.dynamic_update_index_in_dim(grad_mixes, grad_mixed, slot_idx, 0), grad_mixes
        )
        grad_gates = jnp.where(
            active, lax.dynamic_update_index_in_dim(grad_gates, grad_gate, slot_idx, 0), grad_gates
        )
        proj_grads = jnp.where(
            active, lax.dynamic_update_index_in_dim(proj_grads, grad_proj, slot_idx, 0), proj_grads
        )
        if step_idx < batches:
            received = passed_along(grad_x, "pipe", -1)
    weight_total = jnp.einsum(
        "btd,bte->de", x_local, proj_grads, preferred_element_type=jnp.float32
    )
    weight_shard = lax.psum_scatter(
        weight_total[None], ("seg", "dp"), scatter_dimension=1, tiled=True
    )
    return (grad_inputs[None], grad_mixes[None], grad_gates[None], weight_shard)


def solution(mesh):
    in_specs = (
        P("pipe", "dp", "seg", None),
        P("pipe", "dp", "seg", None),
        P("pipe", "dp", "seg", None),
        P("pipe", "dp", "seg", None, None, None),
        P("dp", "seg", None),
        P("dp", None),
        P("pipe", ("seg", "dp"), None),
        P("pipe", None),
        P("pipe", None),
        P("pipe", None),
    )
    out_specs = (
        P("pipe", "dp", "seg", None),
        P("pipe", "dp", "seg", None),
        P("pipe", "dp", "seg", None),
        P("pipe", ("seg", "dp"), None),
    )
    return jax.shard_map(local, mesh=mesh, in_specs=in_specs, out_specs=out_specs, check_vma=False)
```

profile of v0, /device:TPU:1, one launch (start us, length us, event | category | flops | bytes accessed | tf_op | source)
XLA Modules:
  0.0 2359.1 jit_solution(5416243080608511109)
XLA Ops:
  9.4 1.9 copy.281
  11.2 2.6 copy.282
  13.8 2.8 multiply_multiply_fusion.4
  16.6 357.1 %all-gather.2.cloned.1.call-done = bf16[1,4096,320]{2,1,0:T(8,128)(2,1)} async-done(((bf16[1,32,320]{2,1,0:T(8,128)(2,1)}), bf16[1,4096,320]{2,1,0:T(8,128)(2,1)}) %all-gather.2.cloned.1.call-update) | async-done | bytes 2621456 | tf_op jit(solution)/shard_map/all_gather | solution.py:138
  373.7 3.1 convolution_bitcast_fusion.1
  377.4 3.1 fusion.160
  383.6 1.7 collective-permute-done
  385.5 4.1 add_select_fusion.15
  389.6 3.1 collective-permute-start.5
  392.8 45.9 %collective-permute-done.1 = f32[64]{0:T(128)S(1)} collective-permute-done((f32[64]{0:T(128)S(1)}, f32[64]{0:T(128)S(1)}, u32[]{:S(2)}, u32[]{:S(2)}) %collective-permute-start.1) | collective-permute-done | bytes 288 | tf_op jit(solution)/shard_map/ppermute | solution.py:12
  438.7 4.0 add_select_fusion.14
  442.7 4.5 collective-permute-start.6
  447.3 90.3 %collective-permute-done.2 = f32[64]{0:T(128)S(1)} collective-permute-done((f32[64]{0:T(128)S(1)}, f32[64]{0:T(128)S(1)}, u32[]{:S(2)}, u32[]{:S(2)}) %collective-permute-start.2) | collective-permute-done | bytes 288 | tf_op jit(solution)/shard_map/ppermute | solution.py:12
  537.6 4.1 add_select_fusion.13
  541.7 4.5 collective-permute-start.7
  547.2 90.1 %collective-permute-done.3 = f32[64]{0:T(128)S(1)} collective-permute-done((f32[64]{0:T(128)S(1)}, f32[64]{0:T(128)S(1)}, u32[]{:S(2)}, u32[]{:S(2)}) %collective-permute-start.3) | collective-permute-done | bytes 288 | tf_op jit(solution)/shard_map/ppermute | solution.py:12
  637.3 4.0 add_select_fusion.12
  641.3 2.3 collective-permute-start.8
  646.2 1.6 copy.277
  647.8 2.8 fusion.162
  650.8 37.3 %collective-permute-done.8 = f32[64,64,128]{2,1,0:T(8,128)} collective-permute-done((f32[64,64,128]{2,1,0:T(8,128)}, f32[64,64,128]{2,1,0:T(8,128)}, u32[]{:S(2)}, u32[]{:S(2)}) %collective-permute-start.8) | collective-permute-done | bytes 2097184 | tf_op jit(solution)/shard_map/ppermute | solution.py:12
  688.1 1.6 broadcast_in_dim.86
  689.7 10.0 conditional.2
  701.0 131.3 %collective-permute-done.9 = bf16[128,4096]{0,1:T(8,128)(2,1)S(1)} collective-permute-done((bf16[128,4096]{0,1:T(8,128)(2,1)}, bf16[128,4096]{0,1:T(8,128)(2,1)S(1)}, u32[]{:S(2)}, u32[]{:S(2)}) %collective-permute-start.9) | collective-permute-done | bytes 1048608 | tf_op jit(solution)/shard_map/ppermute | solution.py:18
  832.3 3.6 fusion.157
  835.9 1.9 fusion.158
  837.9 3.5 collective-permute-start.10
  841.4 3.8 collective-permute-done.10
  846.5 46.8 %collective-permute-done.11 = f32[64,64,128]{2,1,0:T(8,128)S(1)} collective-permute-done((f32[64,64,128]{2,1,0:T(8,128)S(1)}, f32[64,64,128]{2,1,0:T(8,128)S(1)}, u32[]{:S(2)}, u32[]{:S(2)}) %collective-permute-start.11) | collective-permute-done | bytes 2097184 | tf_op jit(solution)/shard_map/ppermute | solution.py:12
  894.7 4.3 collective-permute-start.12
  899.0 90.2 %collective-permute-done.12 = f32[64,64,128]{2,1,0:T(8,128)S(1)} collective-permute-done((f32[64,64,128]{2,1,0:T(8,128)S(1)}, f32[64,64,128]{2,1,0:T(8,128)S(1)}, u32[]{:S(2)}, u32[]{:S(2)}) %collective-permute-start.12) | collective-permute-done | bytes 2097184 | tf_op jit(solution)/shard_map/ppermute | solution.py:12
  990.5 2.0 collective-permute-start.13
  992.5 93.3 %collective-permute-done.13 = f32[64,64,128]{2,1,0:T(8,128)S(1)} collective-permute-done((f32[64,64,128]{2,1,0:T(8,128)S(1)}, f32[64,64,128]{2,1,0:T(8,128)S(1)}, u32[]{:S(2)}, u32[]{:S(2)}) %collective-permute-start.13) | collective-permute-done | bytes 2097184 | tf_op jit(solution)/shard_map/ppermute | solution.py:12
  1085.8 1.9 add_select_fusion.8
  1087.8 47.0 %collective-permute-done.14 = f32[64,64,128]{2,1,0:T(8,128)} collective-permute-done((f32[64,64,128]{2,1,0:T(8,128)}, f32[64,64,128]{2,1,0:T(8,128)}, u32[]{:S(2)}, u32[]{:S(2)}) %collective-permute-start.14) | collective-permute-done | bytes 2097184 | tf_op jit(solution)/shard_map/ppermute | solution.py:12
  1134.8 95.1 %conditional.3 = (bf16[128,4096]{0,1:T(8,128)(2,1)}, bf16[128,320]{0,1:T(8,128)(2,1)S(1)}, bf16[128,4096]{0,1:T(8,128)(2,1)}, bf16[128,4096]{0,1:T(8,128)(2,1)}) conditional(s32[]{:T(128)} %convert_element_type.224, () %tuple.47, (f32[128,64]{0,1:T(8,128)S(1)}, f32[1,64]{1,0:T(1,128)S(1)}, s32[128]{0:T(128)S(1)}, f32[1,128,64,64]{1,3,2,0:T(8,128)}, ...), branch_computations={%region_16.17_spmd, %region_17.27_spmd} | conditional | flops 6099624960 | bytes 144681568 | solution.py:225
  1135.0 5.5 fusion.102
  1140.5 3.7 fusion.97
  1146.3 11.9 fusion.87
  1158.2 1.5 copy.274
  1160.4 4.2 multiply_reduce_fusion.3
  1169.7 1.7 add_add_fusion.1
  1171.3 1.5 copy.266
  1172.8 8.9 fusion.96
  1182.5 2.6 reduce_window_sum.87
  1185.0 1.5 copy.271
  1187.8 5.2 fusion.133
  1193.3 3.6 fusion.132
  1197.1 2.0 copy.297
  1199.1 1.4 copy-done.14
  1200.4 4.0 fusion.77
  1204.4 2.4 copy.333
  1206.9 2.3 copy.298
  1209.2 11.3 fusion.94
  1220.5 3.1 copy.276
  1223.5 3.8 fusion.93
  1227.3 2.3 copy.335
  1229.9 3.2 convolution_bitcast_fusion
  1233.1 14.4 copy.303
  1249.4 1.3 select_bitcast_fusion.2
  1250.8 1.3 copy.304
  1252.1 1.7 select_bitcast_fusion
  1253.8 1.3 copy.305
  1256.5 1093.8 %all-reduce.5.cloned.1.call-done = f32[1,4096,320]{2,0,1:T(1,128)} async-done(((f32[1,4096,320]{2,0,1:T(1,128)}), f32[1,4096,320]{2,0,1:T(1,128)}) %all-reduce.5.cloned.1.call-update) | async-done | bytes 5242896
  (200 shorter events, 32.1 us)
Async XLA Ops:
  7.2 366.5 %copy-start = (bf16[1,1,128,4096]{3,2,1,0:T(8,128)(2,1)S(1)}, bf16[1,1,128,4096]{3,2,1,0:T(8,128)(2,1)}, u32[]{:S(2)}) copy-start(bf16[1,1,128,4096]{3,2,1,0:T(8,128)(2,1)} %param.14) | copy-start | bytes 3145732
  7.2 366.5 %all-gather.2.cloned.1.call-start = ((), (), s32[]{:S(2)}) async-start(), calls=%async_computation | async-start | bytes 3170304 | tf_op jit(solution)/shard_map/all_gather | solution.py:138
  7.9 2342.4 %all-reduce.5.cloned.1.call-start = ((), (), s32[]{:S(2)}) async-start(), calls=%async_computation.1 | async-start | bytes 12582912
  9.2 680.4 %copy-start.44 = (s32[1,128]{1,0:T(1,128)}, s32[1,128]{1,0:T(1,128)S(1)}, u32[]{:S(2)}) copy-start(s32[1,128]{1,0:T(1,128)S(1)} %reduce_window_sum.92) | copy-start | bytes 1540
  16.6 360.8 %copy-start.8 = (f32[128,64,64]{0,2,1:T(8,128)}, f32[128,64,64]{0,2,1:T(8,128)S(1)}, u32[]{:S(2)}) copy-start(f32[128,64,64]{0,2,1:T(8,128)S(1)} %multiply_multiply_fusion.4) | copy-start | bytes 6291460
  16.6 360.3 %copy-start.42 = (f32[1,64]{1,0:T(1,128)S(1)}, f32[1,64]{1,0:T(1,128)}, u32[]{:S(2)}) copy-start(f32[1,64]{1,0:T(1,128)} %param.21) | copy-start | bytes 772
  16.6 360.3 %copy-start.72 = (f32[1,64]{1,0:T(1,128)S(1)}, f32[1,64]{1,0:T(1,128)}, u32[]{:S(2)}) copy-start(f32[1,64]{1,0:T(1,128)} %param.22) | copy-start | bytes 772
  380.6 4.9 collective-permute-start.4
  383.5 6.1 copy-start.66
  383.5 1.8 collective-permute-start
  385.3 265.4 %copy-start.48 = (f32[64]{0:T(128)}, f32[64]{0:T(128)S(1)}, u32[]{:S(2)}) copy-start(f32[64]{0:T(128)S(1)} %collective-permute-done) | copy-start | bytes 772
  389.6 49.1 %collective-permute-start.5 = (f32[64,64,128]{2,1,0:T(8,128)}, f32[64,64,128]{2,1,0:T(8,128)}, u32[]{:S(2)}, u32[]{:S(2)}) collective-permute-start(f32[64,64,128]{2,1,0:T(8,128)} %add_select_fusion.15), channel_id=1, source_target_pairs={{0,8},{4,12},{8,0},{12,4},{16,24},{20,28},{24,16},{28,20},{32,40},... | collective-permute-start | bytes 6291464 | tf_op jit(solution)/shard_map/ppermute | solution.py:12
  392.7 54.5 %copy-start.64 = (f32[64]{0:T(128)}, f32[64]{0:T(128)S(1)}, u32[]{:S(2)}) copy-start(f32[64]{0:T(128)S(1)} %fusion.198) | copy-start | bytes 772
  392.7 46.0 %collective-permute-start.1 = (f32[64]{0:T(128)S(1)}, f32[64]{0:T(128)S(1)}, u32[]{:S(2)}, u32[]{:S(2)}) collective-permute-start(f32[64]{0:T(128)S(1)} %fusion.198), channel_id=1, source_target_pairs={{0,8},{4,12},{8,0},{12,4},{16,24},{20,28},{24,16},{28,20},{32,40},... | collective-permute-start | bytes 776 | tf_op jit(solution)/shard_map/ppermute | solution.py:12
  438.7 212.0 %copy-start.58 = (f32[64]{0:T(128)}, f32[64]{0:T(128)S(1)}, u32[]{:S(2)}) copy-start(f32[64]{0:T(128)S(1)} %collective-permute-done.1) | copy-start | bytes 772
  442.7 94.9 %collective-permute-start.6 = (f32[64,64,128]{2,1,0:T(8,128)}, f32[64,64,128]{2,1,0:T(8,128)S(1)}, u32[]{:S(2)}, u32[]{:S(2)}) collective-permute-start(f32[64,64,128]{2,1,0:T(8,128)} %add_select_fusion.14), channel_id=1, source_target_pairs={{0,16},{4,20},{8,24},{12,28},{16,0},{20,4},{24,8},{28,12},{32,48},... | collective-permute-start | bytes 6291464 | tf_op jit(solution)/shard_map/ppermute | solution.py:12
  447.2 99.0 %copy-start.68 = (f32[64]{0:T(128)}, f32[64]{0:T(128)S(1)}, u32[]{:S(2)}) copy-start(f32[64]{0:T(128)S(1)} %mul.1146) | copy-start | bytes 772
  447.2 90.4 %collective-permute-start.2 = (f32[64]{0:T(128)S(1)}, f32[64]{0:T(128)S(1)}, u32[]{:S(2)}, u32[]{:S(2)}) collective-permute-start(f32[64]{0:T(128)S(1)} %mul.1146), channel_id=1, source_target_pairs={{0,16},{4,20},{8,24},{12,28},{16,0},{20,4},{24,8},{28,12},{32,48},... | collective-permute-start | bytes 776 | tf_op jit(solution)/shard_map/ppermute | solution.py:12
  537.6 113.1 %copy-start.60 = (f32[64]{0:T(128)}, f32[64]{0:T(128)S(1)}, u32[]{:S(2)}) copy-start(f32[64]{0:T(128)S(1)} %collective-permute-done.2) | copy-start | bytes 772
  541.7 95.6 %collective-permute-start.7 = (f32[64,64,128]{2,1,0:T(8,128)}, f32[64,64,128]{2,1,0:T(8,128)}, u32[]{:S(2)}, u32[]{:S(2)}) collective-permute-start(f32[64,64,128]{2,1,0:T(8,128)} %add_select_fusion.13), channel_id=1, source_target_pairs={{0,32},{4,36},{8,40},{12,44},{16,48},{20,52},{24,56},{28,60},{32,0... | collective-permute-start | bytes 6291464 | tf_op jit(solution)/shard_map/ppermute | solution.py:12
  546.3 95.0 %copy-start.70 = (f32[64]{0:T(128)}, f32[64]{0:T(128)S(1)}, u32[]{:S(2)}) copy-start(f32[64]{0:T(128)S(1)} %mul.1147) | copy-start | bytes 772
  546.3 91.0 %collective-permute-start.3 = (f32[64]{0:T(128)S(1)}, f32[64]{0:T(128)S(1)}, u32[]{:S(2)}, u32[]{:S(2)}) collective-permute-start(f32[64]{0:T(128)S(1)} %mul.1147), channel_id=1, source_target_pairs={{0,32},{4,36},{8,40},{12,44},{16,48},{20,52},{24,56},{28,60},{32,0... | collective-permute-start | bytes 776 | tf_op jit(solution)/shard_map/ppermute | solution.py:12
  547.2 96.4 %copy-start.22 = (bf16[1,1,128,4096]{3,2,1,0:T(8,128)(2,1)S(1)}, bf16[1,1,128,4096]{3,2,1,0:T(8,128)(2,1)}, u32[]{:S(2)}) copy-start(bf16[1,1,128,4096]{3,2,1,0:T(8,128)(2,1)} %param.16) | copy-start | bytes 3145732
  637.3 13.4 copy-start.62
  641.3 46.8 %collective-permute-start.8 = (f32[64,64,128]{2,1,0:T(8,128)}, f32[64,64,128]{2,1,0:T(8,128)}, u32[]{:S(2)}, u32[]{:S(2)}) collective-permute-start(f32[64,64,128]{2,1,0:T(8,128)} %add_select_fusion.12), channel_id=1, source_target_pairs={{0,64},{4,68},{8,72},{12,76},{16,80},{20,84},{24,88},{28,92},{32,9... | collective-permute-start | bytes 6291464 | tf_op jit(solution)/shard_map/ppermute | solution.py:12
  647.8 41.8 %copy-start.1 = (f32[1,1,1,64,64,128]{5,4,3,2,1,0:T(8,128)S(1)}, f32[1,1,1,64,64,128]{5,4,3,2,1,0:T(8,128)}, u32[]{:S(2)}) copy-start(f32[1,1,1,64,64,128]{5,4,3,2,1,0:T(8,128)} %param.17) | copy-start | bytes 6291460
  647.8 41.8 %copy-start.2 = (f32[1,1,128,4096]{2,3,1,0:T(8,128)S(1)}, f32[1,1,128,4096]{2,3,1,0:T(8,128)}, u32[]{:S(2)}) copy-start(f32[1,1,128,4096]{2,3,1,0:T(8,128)} %copy.277) | copy-start | bytes 6291460
  650.8 38.9 %copy-start.50 = (f32[64]{0:T(128)}, f32[64]{0:T(128)S(1)}, u32[]{:S(2)}) copy-start(f32[64]{0:T(128)S(1)} %get-tuple-element.1070) | copy-start | bytes 772
  650.8 38.9 %copy-start.52 = (f32[64]{0:T(128)}, f32[64]{0:T(128)S(1)}, u32[]{:S(2)}) copy-start(f32[64]{0:T(128)S(1)} %get-tuple-element.1071) | copy-start | bytes 772
  650.8 38.9 %copy-start.54 = (f32[64]{0:T(128)}, f32[64]{0:T(128)S(1)}, u32[]{:S(2)}) copy-start(f32[64]{0:T(128)S(1)} %get-tuple-element.1072) | copy-start | bytes 772
  650.8 38.9 %copy-start.56 = (f32[64]{0:T(128)}, f32[64]{0:T(128)S(1)}, u32[]{:S(2)}) copy-start(f32[64]{0:T(128)S(1)} %get-tuple-element.1073) | copy-start | bytes 772
  699.7 136.2 %copy-start.29 = (f32[128,64]{0,1:T(8,128)S(1)}, f32[128,64]{0,1:T(8,128)}, u32[]{:S(2)}) copy-start(f32[128,64]{0,1:T(8,128)} %copy-done.28) | copy-start | bytes 98308
  699.7 132.6 %collective-permute-start.9 = (bf16[128,4096]{0,1:T(8,128)(2,1)}, bf16[128,4096]{0,1:T(8,128)(2,1)S(1)}, u32[]{:S(2)}, u32[]{:S(2)}) collective-permute-start(bf16[128,4096]{0,1:T(8,128)(2,1)} %get-tuple-element.1050), channel_id=1, source_target_pairs={{128,0},{129,1},{130,2},{131,3},{132,4},{133,5},{134,6},{135,7},{1... | collective-permute-start | bytes 3145736 | tf_op jit(solution)/shard_map/ppermute | solution.py:18
  835.9 9.2 copy-start.49
  835.9 9.2 copy-start.67
  837.8 55.5 %copy-start.59 = (f32[64]{0:T(128)S(1)}, f32[64]{0:T(128)}, u32[]{:S(2)}) copy-start(f32[64]{0:T(128)} %copy-done.58) | copy-start | bytes 772
  837.9 55.5 %copy-start.65 = (f32[64]{0:T(128)S(1)}, f32[64]{0:T(128)}, u32[]{:S(2)}) copy-start(f32[64]{0:T(128)} %copy-done.64) | copy-start | bytes 772
  837.9 7.3 collective-permute-start.10
  846.5 142.7 %copy-start.61 = (f32[64]{0:T(128)S(1)}, f32[64]{0:T(128)}, u32[]{:S(2)}) copy-start(f32[64]{0:T(128)} %copy-done.60) | copy-start | bytes 772
  846.5 142.7 %copy-start.69 = (f32[64]{0:T(128)S(1)}, f32[64]{0:T(128)}, u32[]{:S(2)}) copy-start(f32[64]{0:T(128)} %copy-done.68) | copy-start | bytes 772
  846.5 46.8 %collective-permute-start.11 = (f32[64,64,128]{2,1,0:T(8,128)S(1)}, f32[64,64,128]{2,1,0:T(8,128)S(1)}, u32[]{:S(2)}, u32[]{:S(2)}) collective-permute-start(f32[64,64,128]{2,1,0:T(8,128)S(1)} %add_select_fusion.11), channel_id=1, source_target_pairs={{0,8},{4,12},{8,0},{12,4},{16,24},{20,28},{24,16},{28,20},{32,40},... | collective-permute-start | bytes 6291464 | tf_op jit(solution)/shard_map/ppermute | solution.py:12
  894.7 191.1 %copy-start.63 = (f32[64]{0:T(128)S(1)}, f32[64]{0:T(128)}, u32[]{:S(2)}) copy-start(f32[64]{0:T(128)} %copy-done.62) | copy-start | bytes 772
  894.7 191.1 %copy-start.71 = (f32[64]{0:T(128)S(1)}, f32[64]{0:T(128)}, u32[]{:S(2)}) copy-start(f32[64]{0:T(128)} %copy-done.70) | copy-start | bytes 772
  894.7 94.5 %collective-permute-start.12 = (f32[64,64,128]{2,1,0:T(8,128)S(1)}, f32[64,64,128]{2,1,0:T(8,128)S(1)}, u32[]{:S(2)}, u32[]{:S(2)}) collective-permute-start(f32[64,64,128]{2,1,0:T(8,128)S(1)} %add_select_fusion.10), channel_id=1, source_target_pairs={{0,16},{4,20},{8,24},{12,28},{16,0},{20,4},{24,8},{28,12},{32,48},... | collective-permute-start | bytes 6291464 | tf_op jit(solution)/shard_map/ppermute | solution.py:12
  990.5 144.3 %copy-start.30 = (f32[128,64]{0,1:T(8,128)S(1)}, f32[128,64]{0,1:T(8,128)}, u32[]{:S(2)}) copy-start(f32[128,64]{0,1:T(8,128)} %get-tuple-element.1099) | copy-start | bytes 98308
  990.5 144.3 %copy-start.43 = (f32[1,64]{1,0:T(1,128)S(1)}, f32[1,64]{1,0:T(1,128)}, u32[]{:S(2)}) copy-start(f32[1,64]{1,0:T(1,128)} %param.21) | copy-start | bytes 772
  990.5 144.3 %copy-start.45 = (s32[1,128]{1,0:T(1,128)S(1)}, s32[1,128]{1,0:T(1,128)}, u32[]{:S(2)}) copy-start(s32[1,128]{1,0:T(1,128)} %copy-done.44) | copy-start | bytes 1540
  990.5 144.3 %copy-start.51 = (f32[64]{0:T(128)S(1)}, f32[64]{0:T(128)}, u32[]{:S(2)}) copy-start(f32[64]{0:T(128)} %copy-done.50) | copy-start | bytes 772
  990.5 144.3 %copy-start.53 = (f32[64]{0:T(128)S(1)}, f32[64]{0:T(128)}, u32[]{:S(2)}) copy-start(f32[64]{0:T(128)} %copy-done.52) | copy-start | bytes 772
  990.5 144.3 %copy-start.55 = (f32[64]{0:T(128)S(1)}, f32[64]{0:T(128)}, u32[]{:S(2)}) copy-start(f32[64]{0:T(128)} %copy-done.54) | copy-start | bytes 772
  990.5 144.3 %copy-start.57 = (f32[64]{0:T(128)S(1)}, f32[64]{0:T(128)}, u32[]{:S(2)}) copy-start(f32[64]{0:T(128)} %copy-done.56) | copy-start | bytes 772
  990.5 95.3 %collective-permute-start.13 = (f32[64,64,128]{2,1,0:T(8,128)S(1)}, f32[64,64,128]{2,1,0:T(8,128)S(1)}, u32[]{:S(2)}, u32[]{:S(2)}) collective-permute-start(f32[64,64,128]{2,1,0:T(8,128)S(1)} %add_select_fusion.9), channel_id=1, source_target_pairs={{0,32},{4,36},{8,40},{12,44},{16,48},{20,52},{24,56},{28,60},{32,0... | collective-permute-start | bytes 6291464 | tf_op jit(solution)/shard_map/ppermute | solution.py:12
  1087.8 47.0 %collective-permute-start.14 = (f32[64,64,128]{2,1,0:T(8,128)}, f32[64,64,128]{2,1,0:T(8,128)}, u32[]{:S(2)}, u32[]{:S(2)}) collective-permute-start(f32[64,64,128]{2,1,0:T(8,128)} %add_select_fusion.8), channel_id=1, source_target_pairs={{0,64},{4,68},{8,72},{12,76},{16,80},{20,84},{24,88},{28,92},{32,9... | collective-permute-start | bytes 6291464 | tf_op jit(solution)/shard_map/ppermute | solution.py:12
  1135.0 5.5 copy-start.5
  1146.2 12.0 copy-start.40
  1172.8 14.8 copy-start.34
  1187.7 5.3 copy-start.33
  1187.7 5.5 copy-start.6
  1187.7 5.5 copy-start.13
  1187.7 5.5 copy-start.36
  1204.4 4.7 copy-start.39
  1204.4 4.7 copy-start.41
  1204.4 4.7 copy-start.47
  1204.4 4.7 copy-start.73
  (18 other events, 46.8 us)
Sparse Core Ops, SparseCore 0:
  9.9 363.8 all-gather.1
  1247.7 1102.5 all-reduce.4
where the time goes:
time: 2370 us; the launch traced here: 2360 us
  waiting for transfers between devices  2130 us (90%)
  matrix products  65.5 us (3%)
  local copies, waits for them, and re-layouts  60.7 us (3%)
  other arithmetic  52.1 us (2%)
  starting transfers between devices  27.7 us (1%)
    unnamed x3, waiting for transfers between devices  1090 us
    ppermute x14, waiting for transfers between devices, swapped(): return lax.ppermute(value, axis, pairs)  546 us
    all_gather x1, waiting for transfers between devices, local(): weights = lax.all_gather(proj_weight, ('seg', 'dp'), axis=1, tiled=True)[0]  357 us
    ppermute x1, waiting for transfers between devices, passed_along(): return lax.ppermute(value, axis, pairs)  131 us
  transfers between devices with their start and end apart: 17, of which 14 were waited for; matrix products, arithmetic and copies ran while one was open for 1% of the time, Pallas kernels for 0%

commit v1 on v0

v1 whole, which is shorter than its diff:
```python
import functools

import jax
import jax.numpy as jnp
from jax import lax
from jax.experimental import pallas as pl
from jax.experimental.pallas import tpu as pltpu
from jax.sharding import PartitionSpec as P

MESH = pl.DeviceIdType.MESH
F32 = jnp.float32
BF16 = jnp.bfloat16
HIGH = lax.Precision.HIGHEST
LANES = 128
NEG = -1e30
VMEM_BYTES = 56 * 1024 * 1024
VMEM = pl.BlockSpec(memory_space=pltpu.VMEM)
SMEM = pl.BlockSpec(memory_space=pltpu.SMEM)
NN = (((1,), (0,)), ((), ()))
NT = (((1,), (1,)), ((), ()))
TN = (((0,), (0,)), ((), ()))


def dot(a, b, dims=NN, precision=None):
    return lax.dot_general(a, b, dims, precision=precision, preferred_element_type=F32)


def iota(axis, shape=(LANES, LANES)):
    return lax.broadcasted_iota(jnp.int32, shape, axis)


def tile_at(j):
    return pl.ds(pl.multiple_of(j * LANES, LANES), LANES)


def split_two(value):
    high = value.astype(BF16)
    low = (value - high.astype(F32)).astype(BF16)
    return high, low


def split_three(value):
    high = value.astype(BF16)
    rest = value - high.astype(F32)
    mid = rest.astype(BF16)
    low = (rest - mid.astype(F32)).astype(BF16)
    return high, mid, low


def pass_rows(value):
    high, mid, low = split_three(value)
    row = iota(0, (16, LANES))
    zero = jnp.zeros((16, LANES), F32)
    out = jnp.where(row == 0, high.astype(F32), zero)
    out = jnp.where(row == 1, mid.astype(F32), out)
    out = jnp.where(row == 2, low.astype(F32), out)
    return out.astype(BF16)


def pass_value(rows):
    return jnp.sum(rows.astype(F32), axis=0, keepdims=True)


def place():
    seg = lax.axis_index("seg")
    chip = seg // 2
    core = seg - 2 * chip
    return lax.axis_index("pipe"), seg, chip, core, lax.axis_index("dp")


def greet(devices):
    barrier = pltpu.get_barrier_semaphore()
    for count, device_of in devices:
        def one(k, carry, device_of=device_of):
            pl.semaphore_signal(barrier, inc=1, device_id=device_of(k), device_id_type=MESH)
            return carry

        lax.fori_loop(0, count, one, 0)
    pl.semaphore_wait(barrier, sum(count for count, _ in devices))


def remote(src, dst, send_sem, recv_sem, device):
    return pltpu.make_async_remote_copy(
        src_ref=src, dst_ref=dst, send_sem=send_sem, recv_sem=recv_sem,
        device_id=device, device_id_type=MESH,
    )


def each(count, body):
    def step(k, carry):
        body(k)
        return carry

    lax.fori_loop(0, count, step, 0)


def gather_kernel(n_chip, n_dp, w_ref, own_ref, one_ref, shard, pipe_sems, sems_a, sems_b):
    pipe, seg, chip, core, dp = place()

    def chip_device(k):
        return {"seg": lax.rem(chip + 1 + k, n_chip) * 2 + core}

    def dp_device(k):
        return {"dp": lax.rem(dp + 1 + k, n_dp)}

    def sibling(k):
        return {"seg": seg + 1 - 2 * core}

    def partner(k):
        return {"pipe": 1 - pipe}

    greet([(n_chip - 1, chip_device), (n_dp - 1, dp_device), (1, sibling), (1, partner)])

    def gather(src, dst, sems):
        chip_send, chip_recv, dp_send, dp_recv, core_sems = sems
        dst[chip, core, dp] = src[...]

        def chip_copy(k):
            block = dst.at[chip, core, dp]
            return remote(block, block, chip_send.at[k], chip_recv.at[k], chip_device(k))

        def dp_copy(k):
            block = dst.at[:, core, dp]
            return remote(block, block, dp_send.at[k], dp_recv.at[k], dp_device(k))

        each(n_chip - 1, lambda k: chip_copy(k).start())
        each(n_chip - 1, lambda k: chip_copy(k).wait_recv())
        each(n_dp - 1, lambda k: dp_copy(k).start())
        each(n_dp - 1, lambda k: dp_copy(k).wait_recv())
        block = dst.at[:, core]
        last = remote(block, block, core_sems.at[0], core_sems.at[1], sibling(0))
        last.start()
        last.wait()
        each(n_chip - 1, lambda k: chip_copy(k).wait_send())
        each(n_dp - 1, lambda k: dp_copy(k).wait_send())

    shard_copy = remote(w_ref, shard, pipe_sems.at[0], pipe_sems.at[1], partner(0))

    @pl.when(pipe == 1)
    def _():
        shard_copy.start()

    gather(w_ref, own_ref, sems_a)

    @pl.when(pipe == 1)
    def _():
        shard_copy.wait_send()

    @pl.when(pipe == 0)
    def _():
        shard_copy.wait_recv()
        gather(shard, one_ref, sems_b)


def gather_sems(n_chip, n_dp):
    dma = pltpu.SemaphoreType.DMA
    return (dma((n_chip - 1,)), dma((n_chip - 1,)), dma((n_dp - 1,)), dma((n_dp - 1,)), dma((2,)))


def gather_weights(w, n_chip, n_dp):
    rows, cols = w.shape
    full = jax.ShapeDtypeStruct((n_chip, 2, n_dp, rows, cols), BF16)
    own, one = pl.pallas_call(
        functools.partial(gather_kernel, n_chip, n_dp),
        out_shape=(full, full),
        in_specs=[VMEM],
        out_specs=(VMEM, VMEM),
        scratch_shapes=[
            pltpu.VMEM((rows, cols), BF16),
            pltpu.SemaphoreType.DMA((2,)),
            gather_sems(n_chip, n_dp),
            gather_sems(n_chip, n_dp),
        ],
        compiler_params=pltpu.CompilerParams(
            collective_id=1, has_side_effects=True, vmem_limit_bytes=VMEM_BYTES
        ),
    )(w)
    return own.reshape(-1, cols), one.reshape(-1, cols)


def prep_kernel(
    x_ref, w_ref, bias_ref, rate_ref, doc_ref, s0_ref,
    bf_ref, cf_ref, log_ref, logt_ref, dt_ref, dtt_ref, sig_ref, rho_ref, mask_ref, first_ref, kept_ref,
    s0t_ref, pad,
):
    rows = x_ref.shape[0]
    heads = bias_ref.shape[1]
    state = bf_ref.shape[1]
    projected = dot(x_ref[...], w_ref[...])
    bf_ref[...] = projected[:, :state]
    cf_ref[...] = projected[:, state : 2 * state]
    pad[...] = jnp.zeros_like(pad)
    pad[0, :, :heads] = projected[:, 2 * state :] + bias_ref[...]
    pad[1, 0:1, :heads] = rate_ref[...]
    raw = pad[0]
    rate = pad[1, 0:1, :]
    soft = jnp.maximum(raw, 0.0) + jnp.log1p(jnp.exp(-jnp.abs(raw)))
    sig = 1.0 / (1.0 + jnp.exp(-jnp.abs(raw)))
    sig = jnp.where(raw >= 0, sig, 1.0 - sig)
    small = raw < -15.0
    exp_raw = jnp.exp(jnp.minimum(raw, 0.0))
    sig = jnp.where(small, exp_raw, sig)
    soft = jnp.where(small, exp_raw, soft)
    rho = jnp.where(small, 1.0, sig / jnp.where(small, 1.0, soft))
    lower = (iota(0) >= iota(1)).astype(F32)
    log = dot(lower, -soft * rate, precision=HIGH)
    log_ref[...] = log
    logt_ref[...] = log.T
    dt_ref[...] = soft
    dtt_ref[...] = soft.T
    sig_ref[...] = sig
    rho_ref[...] = rho
    begin = lax.axis_index("seg") * rows
    count_t = jnp.zeros((rows, rows), jnp.int32)
    count_s = jnp.zeros((rows, rows), jnp.int32)
    count_last = jnp.zeros((rows, rows), jnp.int32)
    start = jnp.int32(0)
    for k in range(doc_ref.shape[1] - 1):
        start = start + doc_ref[0, k]
        offset = start - begin
        inside = offset >= 0
        count_t += (inside & (iota(0) >= offset)).astype(jnp.int32)
        count_s += (inside & (iota(1) >= offset)).astype(jnp.int32)
        count_last += jnp.broadcast_to((inside & (offset <= rows - 1)).astype(jnp.int32), (rows, rows))
    allowed = (iota(0) >= iota(1)) & (count_t == count_s)
    mask_ref[...] = jnp.where(allowed, 0.0, NEG)
    first_ref[...] = jnp.where(count_t == 0, 0.0, NEG)
    kept_ref[...] = jnp.where(count_t == count_last, 0.0, NEG)

    def turn(j, carry):
        s0t_ref[j] = s0_ref[tile_at(j), :].T.astype(BF16)
        return carry

    lax.fori_loop(0, s0t_ref.shape[0], turn, 0)


def prepare(x, w, bias, rate, docs, s0):
    rows, width = x.shape
    state = s0.shape[1]
    pairs = width // LANES
    square = jax.ShapeDtypeStruct((rows, LANES), F32)
    return pl.pallas_call(
        prep_kernel,
        out_shape=(square,) * 11 + (jax.ShapeDtypeStruct((pairs, state, LANES), BF16),),
        in_specs=[VMEM, VMEM, VMEM, VMEM, SMEM, VMEM],
        out_specs=(VMEM,) * 12,
        scratch_shapes=[pltpu.VMEM((2, rows, LANES), F32)],
        compiler_params=pltpu.CompilerParams(vmem_limit_bytes=VMEM_BYTES),
    )(x, w, bias, rate, docs, s0)


def pair_columns(ref, j):
    turned = pltpu.roll(ref[...], lax.rem(LANES - 2 * j, LANES), 1)
    shape = (turned.shape[0], LANES)
    return jnp.broadcast_to(turned[:, 0:1], shape), jnp.broadcast_to(turned[:, 1:2], shape)


def by_half(first, second):
    return jnp.where(iota(1, (1, LANES)) < LANES // 2, first, second)


def own_kernel(final, *refs):
    if final:
        out_grad_ref, later_ref, w_ref, gate_ref, cf_ref, log_ref, first_ref, msg_ref, g_ref = refs
        pipe = lax.axis_index("pipe")
        chunk = 512

        def recompute(k, carry):
            cols = pl.ds(pl.multiple_of(k * chunk, chunk), chunk)
            back = dot(later_ref[...], w_ref[cols, :], NT)
            g = out_grad_ref[:, cols].astype(F32)
            g_ref[:, cols] = jnp.where(pipe == 0, g + back, g).astype(BF16)
            return carry

        lax.fori_loop(0, out_grad_ref.shape[1] // chunk, recompute, 0)
    else:
        g_ref, gate_ref, cf_ref, log_ref, first_ref, msg_ref = refs
    ct = cf_ref[...].T.astype(BF16)
    state = ct.shape[0]

    def body(j, carry):
        cols = tile_at(j)
        gate = gate_ref[:, cols].astype(F32)
        grad_y = g_ref[:, cols].astype(F32) * gate * jax.nn.sigmoid(gate)
        log0, log1 = pair_columns(log_ref, j)
        entry = jnp.exp(by_half(log0, log1) + first_ref[...])
        msg_ref[j, 0:state] = dot(ct, (entry * grad_y).astype(BF16)).astype(BF16)
        msg_ref[j, state : state + 16] = pass_rows(entry[-1:, :])
        return carry

    lax.fori_loop(0, msg_ref.shape[0], body, 0)


def own_adjoint(final, args, pairs, state):
    shapes = [jax.ShapeDtypeStruct((pairs, state + 16, LANES), BF16)]
    if final:
        shapes.append(jax.ShapeDtypeStruct(args[0].shape, BF16))
    return pl.pallas_call(
        functools.partial(own_kernel, final),
        out_shape=tuple(shapes),
        in_specs=[VMEM] * len(args),
        out_specs=(VMEM,) * len(shapes),
        compiler_params=pltpu.CompilerParams(vmem_limit_bytes=VMEM_BYTES),
    )(*args)


def scan_kernel(n_chip, n_dp, with_x, *refs):
    if with_x:
        msg_ref, xt_ref, out_ref, group_ref = refs[:4]
        both, total, got, back, exits, other, sems, x_sems = refs[4:]
    else:
        msg_ref, out_ref = refs[:2]
        both, total, got, back, exits, other, sems = refs[2:]
    core_sems, local_sems, send, recv, back_send, back_recv = sems
    pipe, seg, chip, core, dp = place()
    state = out_ref.shape[1]
    half = n_chip

    def chip_device(k):
        return {"seg": lax.rem(chip + 1 + k, n_chip) * 2 + core}

    def sibling(k):
        return {"seg": seg + 1 - 2 * core}

    def group_place(k):
        slot = lax.rem(dp * 2 + core + 1 + k, 2 * n_dp)
        to_dp = slot // 2
        return to_dp, slot - 2 * to_dp

    def group_device(k):
        to_dp, to_core = group_place(k)
        return {"seg": chip * 2 + to_core, "dp": to_dp}

    met = [(n_chip - 1, chip_device)]
    met.append((2 * n_dp - 1, group_device) if with_x else (1, sibling))
    greet(met)

    mine = pl.ds(core * half, half)
    theirs = pl.ds((1 - core) * half, half)
    swap = remote(msg_ref.at[theirs], both.at[core], core_sems.at[0], core_sems.at[1], sibling(0))
    swap.start()
    keep = pltpu.make_async_copy(msg_ref.at[mine], both.at[core], local_sems.at[0])
    keep.start()
    if with_x:
        x_send, x_recv, x_local = x_sems

        def x_copy(k):
            to_dp, to_core = group_place(k)
            return remote(
                xt_ref.at[:, to_core, to_dp], group_ref.at[dp * 2 + core],
                x_send.at[k], x_recv.at[k], group_device(k),
            )

        each(2 * n_dp - 1, lambda k: x_copy(k).start())
        x_keep = pltpu.make_async_copy(xt_ref.at[:, core, dp], group_ref.at[dp * 2 + core], x_local.at[0])
        x_keep.start()
    keep.wait()
    swap.wait()

    def combine(j):
        pass0 = pass_value(both[0, j, state : state + 16])
        pass1 = pass_value(both[1, j, state : state + 16])
        joined = both[0, j, :state].astype(F32) + pass0 * both[1, j, :state].astype(F32)
        total[j, :state] = joined.astype(BF16)
        total[j, state : state + 16] = pass_rows(pass0 * pass1)

    def send_copy(k):
        slot = lax.rem(chip + 1 + k, n_chip)
        return remote(total.at[slot], got.at[chip], send.at[k], recv.at[chip], chip_device(k))

    def combine_send(k):
        combine(lax.rem(chip + 1 + k, n_chip))
        send_copy(k).start()

    each(n_chip - 1, combine_send)
    combine(chip)
    own_copy = pltpu.make_async_copy(total.at[chip], got.at[chip], local_sems.at[1])
    own_copy.start()
    own_copy.wait()

    def back_copy(k):
        return remote(back.at[k], exits.at[chip], back_send.at[k], back_recv.at[chip], {"seg": k * 2 + core})

    def scan(step, carry):
        k = n_chip - 1 - step

        @pl.when(k != chip)
        def _():
            remote(got.at[k], got.at[k], send.at[0], recv.at[k], sibling(0)).wait_recv()

        back[k] = carry.astype(BF16)

        @pl.when(k != chip)
        def _():
            back_copy(k).start()

        return got[k, :state].astype(F32) + pass_value(got[k, state : state + 16]) * carry

    lax.fori_loop(0, n_chip, scan, jnp.zeros((state, LANES), F32))
    own_back = pltpu.make_async_copy(back.at[chip], exits.at[chip], local_sems.at[2])
    own_back.start()
    own_back.wait()

    def finish(j):
        @pl.when(j != chip)
        def _():
            remote(back.at[j], exits.at[j], back_send.at[0], back_recv.at[j], sibling(0)).wait_recv()

        later = exits[j].astype(F32)
        pass1 = pass_value(both[1, j, state : state + 16])
        earlier = both[1, j, :state].astype(F32) + pass1 * later
        is_later = core == 1
        out_ref[core * half + j] = jnp.where(is_later, later, earlier).astype(BF16)
        other[j] = jnp.where(is_later, earlier, later).astype(BF16)

    each(n_chip, finish)
    swap_back = remote(other, out_ref.at[mine], core_sems.at[2], core_sems.at[3], sibling(0))
    swap_back.start()
    each(n_chip - 1, lambda k: send_copy(k).wait_send())

    def sent_back(k):
        @pl.when(k != chip)
        def _():
            back_copy(k).wait_send()

    each(n_chip, sent_back)
    if with_x:
        each(2 * n_dp - 1, lambda k: x_copy(k).wait())
        x_keep.wait()
    swap_back.wait()


def scan_states(msg, xt, n_chip, n_dp, collective_id):
    pairs, rows, lanes = msg.shape
    state = rows - 16
    with_x = xt is not None
    dma = pltpu.SemaphoreType.DMA
    shapes = [jax.ShapeDtypeStruct((pairs, state, lanes), BF16)]
    scratch = [
        pltpu.VMEM((2, n_chip, rows, lanes), BF16),
        pltpu.VMEM((n_chip, rows, lanes), BF16),
        pltpu.VMEM((n_chip, rows, lanes), BF16),
        pltpu.VMEM((n_chip, state, lanes), BF16),
        pltpu.VMEM((n_chip, state, lanes), BF16),
        pltpu.VMEM((n_chip, state, lanes), BF16),
        (dma((4,)), dma((3,)), dma((n_chip,)), dma((n_chip,)), dma((n_chip,)), dma((n_chip,))),
    ]
    args = [msg]
    if with_x:
        shapes.append(jax.ShapeDtypeStruct((2 * n_dp, n_chip, xt.shape[3], xt.shape[4]), BF16))
        scratch.append((dma((2 * n_dp - 1,)), dma((2 * n_dp - 1,)), dma((1,))))
        args.append(xt)
    return pl.pallas_call(
        functools.partial(scan_kernel, n_chip, n_dp, with_x),
        out_shape=tuple(shapes),
        in_specs=[VMEM] * len(args),
        out_specs=(VMEM,) * len(shapes),
        scratch_shapes=scratch,
        compiler_params=pltpu.CompilerParams(
            collective_id=collective_id, has_side_effects=True, vmem_limit_bytes=VMEM_BYTES
        ),
    )(*args)


def grads_kernel(final, *refs):
    (
        x_ref, gate_ref, g_ref, adj_ref, s0t_ref, bf_ref, cf_ref, log_ref, logt_ref, dt_ref, dtt_ref,
        sig_ref, rho_ref, mask_ref, first_ref, kept_ref, rate_ref,
    ) = refs[:17]
    refs = refs[17:]
    if final:
        skip_ref, w_ref, dproj_ref, mixed_grad_ref, gate_grad_ref, input_grad_ref = refs[:6]
        refs = refs[6:]
    else:
        dproj_ref = refs[0]
        refs = refs[1:]
    acc_scores, acc_b, acc_c, acc_y, acc_x, acc_s, acc_a, pad = refs
    for ref in (acc_scores, acc_b, acc_c, acc_y, acc_x, acc_s, acc_a):
        ref[...] = jnp.zeros_like(ref)
    scores = dot(cf_ref[...], bf_ref[...], NT, precision=HIGH)
    b_low = bf_ref[...].astype(BF16)
    c_low = cf_ref[...].astype(BF16)
    first = iota(1, (1, LANES)) < LANES // 2
    heads = rate_ref.shape[1]

    def body(j, carry):
        cols = tile_at(j)
        x_pair = x_ref[:, cols]
        gate = gate_ref[:, cols].astype(F32)
        sig = jax.nn.sigmoid(gate)
        act = gate * sig
        g = g_ref[:, cols].astype(F32)
        grad_y = g * act
        grad_low = grad_y.astype(BF16)
        zero = jnp.zeros_like(x_pair)
        x0, x1 = jnp.where(first, x_pair, zero), jnp.where(first, zero, x_pair)
        y0, y1 = jnp.where(first, grad_low, zero), jnp.where(first, zero, grad_low)
        log0, log1 = pair_columns(log_ref, j)
        dt0, dt1 = pair_columns(dt_ref, j)
        mask = mask_ref[...]
        decay0 = jnp.exp(log0 - logt_ref[pl.ds(2 * j, 1), :] + mask) * dtt_ref[pl.ds(2 * j, 1), :]
        decay1 = jnp.exp(log1 - logt_ref[pl.ds(2 * j + 1, 1), :] + mask) * dtt_ref[pl.ds(2 * j + 1, 1), :]
        mix0 = (decay0 * scores).astype(BF16)
        mix1 = (decay1 * scores).astype(BF16)
        acc_scores[...] += dot(y0, x_pair, NT) * decay0 + dot(y1, x_pair, NT) * decay1
        log_pair = jnp.where(first, log0, log1)
        entry = jnp.exp(log_pair + first_ref[...])
        s0t = s0t_ref[j]
        y = dot(mix0, x0) + dot(mix1, x1) + entry * dot(c_low, s0t)
        acc_c[...] += dot((entry * grad_y).astype(BF16), s0t, NT)
        inner = dot(mix0, y0, TN) + dot(mix1, y1, TN)
        adj = adj_ref[j]
        weight = jnp.exp(log_pair[-1:, :] - log_pair + kept_ref[...]) * jnp.where(first, dt0, dt1)
        outer = weight * dot(b_low, adj)
        x_f = x_pair.astype(F32)
        acc_b[...] += dot((x_f * weight).astype(BF16), adj, NT)
        select = (iota(1) == 2 * j + (iota(0) >= LANES // 2).astype(jnp.int32)).astype(BF16)
        select = jnp.concatenate([select, select], axis=0)

        def heads_of(value):
            return dot(jnp.concatenate(split_two(value), axis=1), select)

        acc_y[...] += heads_of(grad_low.astype(F32) * y)
        acc_x[...] += heads_of(x_f * inner)
        acc_s[...] += heads_of(x_f * outer)
        passed = entry[-1:, :] * jnp.sum(adj.astype(F32) * s0t.astype(F32), axis=0, keepdims=True)
        acc_a[...] += heads_of(jnp.broadcast_to(passed, (8, LANES)))
        if final:
            skip = skip_ref[:, cols]
            slope = sig * (1.0 + gate * (1.0 - sig))
            gate_grad_ref[:, cols] = (g * (y + skip * x_f) * slope).astype(BF16)
            mixed_grad_ref[:, cols] = (inner + outer + skip * grad_y).astype(BF16)
        return carry

    lax.fori_loop(0, adj_ref.shape[0], body, 0)
    pad[...] = jnp.zeros_like(pad)
    pad[0:1, :heads] = rate_ref[...]
    u = acc_x[...] + acc_s[...]
    last = jnp.sum(acc_s[...], axis=0, keepdims=True) + acc_a[0:1, :]
    upper = (iota(0) <= iota(1)).astype(F32)
    log_grad = dot(upper, acc_y[...] - u, precision=HIGH) + last
    raw_grad = u * rho_ref[...] - pad[0:1, :] * log_grad * sig_ref[...]
    b_grad = acc_b[...] + dot(acc_scores[...].T, cf_ref[...], precision=HIGH)
    c_grad = acc_c[...] + dot(acc_scores[...], bf_ref[...], precision=HIGH)
    dproj_ref[:, 0:LANES] = b_grad.astype(BF16)
    dproj_ref[:, LANES : 2 * LANES] = c_grad.astype(BF16)
    dproj_ref[:, 2 * LANES : 2 * LANES + heads] = raw_grad[:, :heads].astype(BF16)
    if final:
        chunk = 512
        dproj = dproj_ref[...]

        def back(k, carry):
            cols = pl.ds(pl.multiple_of(k * chunk, chunk), chunk)
            g = g_ref[:, cols].astype(F32)
            input_grad_ref[:, cols] = (g + dot(dproj, w_ref[cols, :], NT)).astype(BF16)
            return carry

        lax.fori_loop(0, g_ref.shape[1] // chunk, back, 0)


def segment_grads(final, args, proj_cols):
    rows, width = args[0].shape
    square = pltpu.VMEM((rows, LANES), F32)
    shapes = [jax.ShapeDtypeStruct((rows, proj_cols), BF16)]
    if final:
        shapes += [jax.ShapeDtypeStruct((rows, width), BF16)] * 3
    return pl.pallas_call(
        functools.partial(grads_kernel, final),
        out_shape=tuple(shapes),
        in_specs=[VMEM] * len(args),
        out_specs=(VMEM,) * len(shapes),
        scratch_shapes=[square] * 6 + [pltpu.VMEM((8, LANES), F32)] * 2,
        compiler_params=pltpu.CompilerParams(vmem_limit_bytes=VMEM_BYTES),
    )(*args)


def hand_kernel(src_ref, out_ref, sems):
    pipe = lax.axis_index("pipe")

    def partner(k):
        return {"pipe": 1 - pipe}

    greet([(1, partner)])
    copy = remote(src_ref, out_ref, sems.at[0], sems.at[1], partner(0))
    copy.start()
    copy.wait()


def hand_over(value):
    return pl.pallas_call(
        hand_kernel,
        out_shape=jax.ShapeDtypeStruct(value.shape, value.dtype),
        in_specs=[VMEM],
        out_specs=VMEM,
        scratch_shapes=[pltpu.SemaphoreType.DMA((2,))],
        compiler_params=pltpu.CompilerParams(collective_id=4, has_side_effects=True),
    )(value)


def weight_kernel(n_chip, n_dp, xg_ref, dproj_ref, out_ref, grads, part, total, got, sems):
    pipe, seg, chip, core, dp = place()
    group_send, group_recv, send, recv = sems
    members = 2 * n_dp
    me = dp * 2 + core

    def group_device(k):
        slot = lax.rem(me + 1 + k, members)
        to_dp = slot // 2
        return {"seg": chip * 2 + slot - 2 * to_dp, "dp": to_dp}

    def chip_device(k):
        return {"seg": lax.rem(chip + 1 + k, n_chip) * 2 + core}

    greet([(members - 1, group_device), (n_chip - 1, chip_device)])

    def group_copy(k):
        return remote(dproj_ref, grads.at[me], group_send.at[k], group_recv.at[k], group_device(k))

    each(members - 1, lambda k: group_copy(k).start())
    grads[me] = dproj_ref[...]

    def block(m):
        x = xg_ref[m].reshape(-1, xg_ref.shape[3])
        return dot(x, grads[m])

    total[...] = block(me)

    def add(k):
        group_copy(k).wait_recv()
        total[...] += block(lax.rem(me + members - 1 - k, members))

    each(members - 1, add)
    rows = out_ref.shape[0]

    def send_copy(k):
        slot = lax.rem(chip + 1 + k, n_chip)
        return remote(part.at[slot], got.at[k], send.at[k], recv.at[k], chip_device(k))

    def ship(k):
        slot = lax.rem(chip + 1 + k, n_chip)
        part[slot] = total[pl.ds(pl.multiple_of(slot * rows, rows), rows), :].astype(BF16)
        send_copy(k).start()

    each(n_chip - 1, ship)
    out_ref[...] = total[pl.ds(pl.multiple_of(chip * rows, rows), rows), :]

    def collect(k):
        send_copy(k).wait_recv()
        out_ref[...] += got[k].astype(F32)

    each(n_chip - 1, collect)
    each(n_chip - 1, lambda k: send_copy(k).wait_send())
    each(members - 1, lambda k: group_copy(k).wait_send())


def weight_gradient(xg, dproj, n_chip, n_dp):
    rows = xg.shape[2]
    cols = dproj.shape[1]
    dma = pltpu.SemaphoreType.DMA
    members = 2 * n_dp
    return pl.pallas_call(
        functools.partial(weight_kernel, n_chip, n_dp),
        out_shape=jax.ShapeDtypeStruct((rows, cols), F32),
        in_specs=[VMEM, VMEM],
        out_specs=VMEM,
        scratch_shapes=[
            pltpu.VMEM((members,) + dproj.shape, BF16),
            pltpu.VMEM((n_chip, rows, cols), BF16),
            pltpu.VMEM((n_chip * rows, cols), F32),
            pltpu.VMEM((n_chip - 1, rows, cols), BF16),
            (dma((members - 1,)), dma((members - 1,)), dma((n_chip - 1,)), dma((n_chip - 1,))),
        ],
        compiler_params=pltpu.CompilerParams(
            collective_id=5, has_side_effects=True, vmem_limit_bytes=VMEM_BYTES
        ),
    )(xg, dproj)


def local(
    inputs, mixed, gate_in, entry_states, out_grad, doc_lengths, proj_weight, decay_rate, dt_bias, skip_gain
):
    n_chip = lax.axis_size("seg") // 2
    n_dp = lax.axis_size("dp")
    x = inputs[0, 0]
    xs = mixed[0, 0]
    gate = gate_in[0, 0]
    rows, width = x.shape
    state = entry_states.shape[-1]
    pairs = width // LANES
    s0 = entry_states.reshape(width, state)
    g1 = out_grad[0]
    w_own, w_one = gather_weights(proj_weight[0], n_chip, n_dp)
    bf, cf, log, logt, dt, dtt, sig, rho, mask, first, kept, s0t = prepare(
        x, w_own, dt_bias, decay_rate, doc_lengths, s0
    )
    xt = x.T.reshape(n_chip, 2, n_dp, -1, rows)
    skip = jnp.repeat(skip_gain, width // skip_gain.shape[1], axis=1)
    shared = (s0t, bf, cf, log, logt, dt, dtt, sig, rho, mask, first, kept, decay_rate)
    proj_cols = proj_weight.shape[2]

    (msg,) = own_adjoint(False, (g1, gate, cf, log, first), pairs, state)
    adj, xg = scan_states(msg, xt, n_chip, n_dp, 2)
    (dproj_later,) = segment_grads(False, (xs, gate, g1, adj) + shared, proj_cols)
    received = hand_over(dproj_later)

    msg, g = own_adjoint(True, (g1, received, w_one, gate, cf, log, first), pairs, state)
    (adj,) = scan_states(msg, None, n_chip, n_dp, 3)
    dproj, mixed_grad, gate_grad, input_grad = segment_grads(
        True, (xs, gate, g, adj) + shared + (skip, w_own), proj_cols
    )
    weight_grad = weight_gradient(xg, dproj, n_chip, n_dp)
    return (
        input_grad[None, None],
        mixed_grad[None, None],
        gate_grad[None, None],
        weight_grad[None],
    )


def solution(mesh):
    in_specs = (
        P("pipe", "dp", "seg", None),
        P("pipe", "dp", "seg", None),
        P("pipe", "dp", "seg", None),
        P("pipe", "dp", "seg", None, None, None),
        P("dp", "seg", None),
        P("dp", None),
        P("pipe", ("seg", "dp"), None),
        P("pipe", None),
        P("pipe", None),
        P("pipe", None),
    )
    out_specs = (
        P("pipe", "dp", "seg", None),
        P("pipe", "dp", "seg", None),
        P("pipe", "dp", "seg", None),
        P("pipe", ("seg", "dp"), None),
    )
    return jax.shard_map(local, mesh=mesh, in_specs=in_specs, out_specs=out_specs, check_vma=False)
```

time: 2370 us -> 289 us (0.12)
  waiting for transfers between devices: 2130 us -> 0 us
  Pallas kernels: 0 us -> 284 us
  matrix products: 65.5 us -> 0 us
  local copies, waits for them, and re-layouts: 60.7 us -> 3.5 us
  other arithmetic: 52.1 us -> 0 us
  starting transfers between devices: 27.7 us -> 0 us
    unnamed x3 -> x0, waiting for transfers between devices: 1090 us -> none
    ppermute x15 -> x0, waiting for transfers between devices: 678 us -> none  [the longest x14 546 us: swapped(): return lax.ppermute(value, axis, pairs)]
    all_gather x1 -> x0, waiting for transfers between devices: 357 us -> none  [local(): weights = lax.all_gather(proj_weight, ('seg', 'dp'), axis=1, tiled=True)[0]]
    pallas_call x0 -> x10, Pallas kernels: none -> 284 us  [the longest x1 80.8 us: gather_weights(): pl.pallas_call(functools.partial(gather_kernel, n_chip, n_dp), out_shape=...]
    dot_general x15 -> x0, matrix products: 65.5 us -> none  [the longest x3 32.1 us: block_scan(): inner_out = jnp.einsum('tsh,shp->thp', mixing, xs_f, precision=highest)]
    ppermute x15 -> x0, starting transfers between devices: 27.7 us -> none  [the longest x14 26.4 us: swapped(): return lax.ppermute(value, axis, pairs)]
  transfers between devices with their start and end apart: 17 -> 0, of which waited for: 14 -> 0; matrix products, arithmetic and copies ran while one was open for 1% -> 0% of each run, Pallas kernels for 0% -> 0%
where the time goes in v1:
time: 289 us; the launch traced here: 288 us
  Pallas kernels  284 us (98%)
  local copies, waits for them, and re-layouts  3.5 us (1%)
    pallas_call x1, Pallas kernels, gather_weights(): pl.pallas_call(functools.partial(gather_kernel, n_chip, n_dp), out_shape=...  80.8 us
    pallas_call x2, Pallas kernels, scan_states(): pl.pallas_call(functools.partial(scan_kernel, n_chip, n_dp, with_x), out_...  80.3 us
    pallas_call x2, Pallas kernels, segment_grads(): pl.pallas_call(functools.partial(grads_kernel, final), out_shape=tuple(sh...  48.5 us
    pallas_call x2, Pallas kernels, own_adjoint(): pl.pallas_call(functools.partial(own_kernel, final), out_shape=tuple(shap...  29.3 us
    pallas_call x1, Pallas kernels, weight_gradient(): pl.pallas_call(functools.partial(weight_kernel, n_chip, n_dp), out_shape=...  29.3 us
    pallas_call x1, Pallas kernels, prepare(): pl.pallas_call(prep_kernel, out_shape=(square,) * 11 + (jax.ShapeDtypeStr...  8.58 us
    pallas_call x1, Pallas kernels, hand_over(): pl.pallas_call(hand_kernel, out_shape=jax.ShapeDtypeStruct(value.shape, v...  7.3 us

profile of v1, /device:TPU:1, one launch (start us, length us, event | category | flops | bytes accessed | tf_op | source)
XLA Modules:
  0.0 288.3 jit_solution(18076961302190781906)
XLA Ops:
  0.6 80.8 %shard_map.132 = (bf16[16,2,4,32,320]{4,3,2,1,0:T(8,128)(2,1)}, bf16[16,2,4,32,320]{4,3,2,1,0:T(8,128)(2,1)}) custom-call(bf16[32,320]{1,0:T(8,128)(2,1)} %bitcast.33), custom_call_target="tpu_custom_call" | custom-call | tf_op jit(solution)/shard_map/pallas_call | solution.py:163
  81.5 8.6 %shard_map.133 = (f32[128,128]{1,0:T(8,128)}, f32[128,128]{1,0:T(8,128)}, f32[128,128]{1,0:T(8,128)}, f32[128,128]{1,0:T(8,128)}, f32[128,128]{1,0:T(8,128)}, /*...) custom-call(bf16[128,4096]{1,0:T(8,128)(2,1)} %bitcast.28, ...), custom_call_target="tpu_custom_call" | custom-call | tf_op jit(solution)/shard_map/pallas_call | solution.py:242
  90.0 0.0 copy-start
  90.0 13.1 %shard_map.134.refs_0_ = bf16[32,144,128]{2,1,0:T(8,128)(2,1)} custom-call(bf16[128,4096]{1,0:T(8,128)(2,1)} %bitcast.22, bf16[128,4096]{1,0:T(8,128)(2,1)} %bitcast.16, f32[128,128]{1,0:T(8,128)} %get-tuple-element.27.refs_2_.refs_6_.refs_4_, f32[128,128]{1,0:T(8,128)} %get-tuple-element.28.refs_3_.refs_7_.refs_5_, ...), custom_call_target="tpu_custom_call" | custom-call | tf_op jit(solution)/shard_map/pallas_call | solution.py:298
  103.2 0.0 copy-done
  103.2 1.3 copy.14
  104.5 40.0 %shard_map.135 = (bf16[32,128,128]{2,1,0:T(8,128)(2,1)}, bf16[8,16,32,128]{3,2,1,0:T(8,128)(2,1)}) custom-call(bf16[32,144,128]{2,1,0:T(8,128)(2,1)} %shard_map.134.refs_0_, bf16[16,2,4,32,128]{4,3,2,1,0:T(8,128)(2,1)} %bitcast.27), custom_call_target="tpu_custom_call" | custom-call | tf_op jit(solution)/shard_map/pallas_call | solution.py:453
  144.5 22.2 %shard_map.136.src_ref = bf16[128,320]{1,0:T(8,128)(2,1)} custom-call(bf16[128,4096]{1,0:T(8,128)(2,1)} %bitcast.25, bf16[128,4096]{1,0:T(8,128)(2,1)} %bitcast.17, bf16[128,4096]{1,0:T(8,128)(2,1)} %bitcast.23, bf16[32,128,128]{2,1,0:T(8,128)(2,1)} %get-tuple-element.30.refs_3_, bf16[32,128,128]{2,1,0:T(8,128)(2,1)} %get-tuple-element.31.refs_4_, ...), custom_call_target="tpu_custom_call" | custom-call | tf_op jit(solution)/shard_map/pallas_call | solution.py:567
  166.7 7.3 %shard_map.137.refs_1_ = bf16[128,320]{1,0:T(8,128)(2,1)} custom-call(bf16[128,320]{1,0:T(8,128)(2,1)} %shard_map.136.src_ref), custom_call_target="tpu_custom_call" | custom-call | tf_op jit(solution)/shard_map/pallas_call | solution.py:590
  174.0 16.2 %shard_map.138 = (bf16[32,144,128]{2,1,0:T(8,128)(2,1)}, bf16[128,4096]{1,0:T(8,128)(2,1)}) custom-call(bf16[128,4096]{1,0:T(8,128)(2,1)} %bitcast.24, bf16[128,320]{1,0:T(8,128)(2,1)} %shard_map.137.refs_1_, bf16[4096,320]{1,0:T(8,128)(2,1)} %bitcast.30, bf16[128,4096]{1,0:T(8,128)(2,1)} %bitcast.18, f32[128,128]{1,0:T(8,128)} %get-tuple-element.27.refs_2_.refs_6_.refs_4_, ...), custom_call_target="tpu_custom_call" | custom-call | tf_op jit(solution)/shard_map/pallas_call | solution.py:298
  190.2 0.0 copy-start.1
  190.2 40.3 %shard_map.139.refs_3_ = bf16[32,128,128]{2,1,0:T(8,128)(2,1)} custom-call(bf16[32,144,128]{2,1,0:T(8,128)(2,1)} %get-tuple-element.42.refs_0_), custom_call_target="tpu_custom_call" | custom-call | tf_op jit(solution)/shard_map/pallas_call | solution.py:453
  230.5 0.0 copy-done.1
  230.5 0.1 broadcast_in_dim.17
  230.6 0.7 broadcast_in_dim.18.refs_17_
  231.3 26.3 %shard_map.140 = (bf16[128,320]{1,0:T(8,128)(2,1)}, bf16[128,4096]{1,0:T(8,128)(2,1)}, bf16[128,4096]{1,0:T(8,128)(2,1)}, bf16[128,4096]{1,0:T(8,128)(2,1)}) custom-call(bf16[128,4096]{1,0:T(8,128)(2,1)} %bitcast.26, bf16[128,4096]{1,0:T(8,128)(2,1)} %bitcast.19, bf16[128,4096]{1,0:T(8,128)(2,1)} %get-tuple-element.41.refs_2_, ...), custom_call_target="tpu_custom_call" | custom-call | tf_op jit(solution)/shard_map/pallas_call | solution.py:567
  257.6 29.3 %shard_map.141 = f32[32,320]{1,0:T(8,128)} custom-call(bf16[8,16,32,128]{3,2,1,0:T(8,128)(2,1)} %get-tuple-element.46.xg_ref, bf16[128,320]{1,0:T(8,128)(2,1)} %get-tuple-element.47.dproj_ref), custom_call_target="tpu_custom_call" | custom-call | tf_op jit(solution)/shard_map/pallas_call | solution.py:661
  286.9 1.4 copy.16
Async XLA Ops:
  90.0 13.1 %copy-start = (bf16[1,1,128,4096]{3,2,1,0:T(8,128)(2,1)S(1)}, bf16[1,1,128,4096]{3,2,1,0:T(8,128)(2,1)}, u32[]{:S(2)}) copy-start(bf16[1,1,128,4096]{3,2,1,0:T(8,128)(2,1)} %param.10) | copy-start | bytes 3145732
  190.2 40.3 %copy-start.1 = (f32[1,64]{1,0:T(1,128)S(1)}, f32[1,64]{1,0:T(1,128)}, u32[]{:S(2)}) copy-start(f32[1,64]{1,0:T(1,128)} %param.19) | copy-start | bytes 772

commit v2 on v1

v2 whole, which is shorter than its diff:
```python
import functools

import jax
import jax.numpy as jnp
from jax import lax
from jax.experimental import pallas as pl
from jax.experimental.pallas import tpu as pltpu
from jax.sharding import PartitionSpec as P

MESH = pl.DeviceIdType.MESH
F32 = jnp.float32
BF16 = jnp.bfloat16
HIGH = lax.Precision.HIGHEST
LANES = 128
NEG = -1e30
UNROLL = 4
VMEM_BYTES = 56 * 1024 * 1024
VMEM = pl.BlockSpec(memory_space=pltpu.VMEM)
SMEM = pl.BlockSpec(memory_space=pltpu.SMEM)
NN = (((1,), (0,)), ((), ()))
NT = (((1,), (1,)), ((), ()))
TN = (((0,), (0,)), ((), ()))


def dot(a, b, dims=NN, precision=None):
    return lax.dot_general(a, b, dims, precision=precision, preferred_element_type=F32)


def iota(axis, shape=(LANES, LANES)):
    return lax.broadcasted_iota(jnp.int32, shape, axis)


def tile_at(j):
    return pl.ds(pl.multiple_of(j * LANES, LANES), LANES)


def split_two(value):
    high = value.astype(BF16)
    low = (value - high.astype(F32)).astype(BF16)
    return high, low


def split_three(value):
    high = value.astype(BF16)
    rest = value - high.astype(F32)
    mid = rest.astype(BF16)
    low = (rest - mid.astype(F32)).astype(BF16)
    return high, mid, low


def pass_rows(value):
    high, mid, low = split_three(value)
    row = iota(0, (16, LANES))
    zero = jnp.zeros((16, LANES), F32)
    out = jnp.where(row == 0, high.astype(F32), zero)
    out = jnp.where(row == 1, mid.astype(F32), out)
    out = jnp.where(row == 2, low.astype(F32), out)
    return out.astype(BF16)


def pass_value(rows):
    return jnp.sum(rows.astype(F32), axis=0, keepdims=True)


def place():
    seg = lax.axis_index("seg")
    chip = seg // 2
    core = seg - 2 * chip
    return lax.axis_index("pipe"), seg, chip, core, lax.axis_index("dp")


def greet(devices):
    barrier = pltpu.get_barrier_semaphore()
    for count, device_of in devices:
        def one(k, carry, device_of=device_of):
            pl.semaphore_signal(barrier, inc=1, device_id=device_of(k), device_id_type=MESH)
            return carry

        lax.fori_loop(0, count, one, 0)
    pl.semaphore_wait(barrier, sum(count for count, _ in devices))


def remote(src, dst, send_sem, recv_sem, device):
    return pltpu.make_async_remote_copy(
        src_ref=src, dst_ref=dst, send_sem=send_sem, recv_sem=recv_sem,
        device_id=device, device_id_type=MESH,
    )


def each(count, body, unroll=1):
    def step(k, carry):
        body(k)
        return carry

    lax.fori_loop(0, count, step, 0, unroll=unroll)


class Around:
    def __init__(self, n_chip, n_dp):
        self.n_chip, self.n_dp = n_chip, n_dp
        self.pipe, self.seg, self.chip, self.core, self.dp = place()

    def chip_slot(self, k):
        return lax.rem(self.chip + 1 + k, self.n_chip)

    def chip_device(self, k):
        return {"seg": self.chip_slot(k) * 2 + self.core}

    def dp_slot(self, k):
        return lax.rem(self.dp + 1 + k, self.n_dp)

    def dp_device(self, k):
        return {"dp": self.dp_slot(k)}

    def sibling(self, k=0):
        return {"seg": self.seg + 1 - 2 * self.core}

    def partner(self, k=0):
        return {"pipe": 1 - self.pipe}

    def greet(self, with_pipe):
        met = [(self.n_chip - 1, self.chip_device), (self.n_dp - 1, self.dp_device), (1, self.sibling)]
        greet(met + ([(1, self.partner)] if with_pipe else []))


class Gather:
    def __init__(self, near, dst, sems):
        self.near, self.dst = near, dst
        self.chip_send, self.chip_recv, self.dp_send, self.dp_recv, self.core_sems = sems

    def chip_copy(self, k):
        near = self.near
        block = self.dst.at[near.chip, near.core, near.dp]
        return remote(block, block, self.chip_send.at[k], self.chip_recv.at[k], near.chip_device(k))

    def dp_copy(self, k):
        block = self.dst.at[:, self.near.core, self.near.dp]
        return remote(block, block, self.dp_send.at[k], self.dp_recv.at[k], self.near.dp_device(k))

    def core_copy(self):
        block = self.dst.at[:, self.near.core]
        return remote(block, block, self.core_sems.at[0], self.core_sems.at[1], self.near.sibling())

    def start(self, src):
        near = self.near
        self.dst[near.chip, near.core, near.dp] = src[...]
        each(near.n_chip - 1, lambda k: self.chip_copy(k).start())

    def second(self):
        each(self.near.n_chip - 1, lambda k: self.chip_copy(k).wait_recv())
        each(self.near.n_dp - 1, lambda k: self.dp_copy(k).start())

    def third(self):
        each(self.near.n_dp - 1, lambda k: self.dp_copy(k).wait_recv())
        self.core_copy().start()

    def end(self):
        self.core_copy().wait()
        each(self.near.n_chip - 1, lambda k: self.chip_copy(k).wait_send())
        each(self.near.n_dp - 1, lambda k: self.dp_copy(k).wait_send())


def gather_sems(n_chip, n_dp):
    dma = pltpu.SemaphoreType.DMA
    return (dma((n_chip - 1,)), dma((n_chip - 1,)), dma((n_dp - 1,)), dma((n_dp - 1,)), dma((2,)))


def prep_kernel(
    n_chip, n_dp, shard_ref, x_ref, bias_ref, rate_ref, doc_ref, s0_ref,
    own_ref, bf_ref, cf_ref, log_ref, logt_ref, dt_ref, dtt_ref, sig_ref, rho_ref, mask_ref, first_ref, kept_ref,
    s0t_ref, xt_ref, pad, projected, sems,
):
    near = Around(n_chip, n_dp)
    near.greet(False)
    gather = Gather(near, own_ref, sems)
    gather.start(shard_ref)
    rows = x_ref.shape[0]
    heads = bias_ref.shape[1]
    state = bf_ref.shape[1]

    def turn_state(j):
        s0t_ref[j] = s0_ref[tile_at(j), :].T.astype(BF16)

    def turn_x(chip):
        for core in range(2):
            xt_ref[chip, core] = x_ref[:, tile_at(2 * chip + core)].T

    each(s0t_ref.shape[0], turn_state, UNROLL)
    begin = near.seg * rows
    count_t = jnp.zeros((rows, rows), jnp.int32)
    count_s = jnp.zeros((rows, rows), jnp.int32)
    count_last = jnp.zeros((rows, rows), jnp.int32)
    start = jnp.int32(0)
    for k in range(doc_ref.shape[1] - 1):
        start = start + doc_ref[0, k]
        offset = jnp.broadcast_to(start - begin, (rows, rows))
        inside = offset >= 0
        count_t += (inside & (iota(0) >= offset)).astype(jnp.int32)
        count_s += (inside & (iota(1) >= offset)).astype(jnp.int32)
        count_last += (inside & (offset <= rows - 1)).astype(jnp.int32)
    allowed = (iota(0) >= iota(1)) & (count_t == count_s)
    mask_ref[...] = jnp.where(allowed, 0.0, NEG)
    first_ref[...] = jnp.where(count_t == 0, 0.0, NEG)
    kept_ref[...] = jnp.where(count_t == count_last, 0.0, NEG)
    gather.second()
    each(n_chip, turn_x, 2)
    gather.third()
    projected[...] = jnp.zeros_like(projected)

    def project(core):
        def one(chip):
            w = own_ref[chip, core].reshape(-1, projected.shape[1])
            projected[...] += dot(x_ref[:, tile_at(2 * chip + core)], w)

        each(n_chip, one, UNROLL)

    project(near.core)
    gather.end()
    project(1 - near.core)
    bf_ref[...] = projected[:, :state]
    cf_ref[...] = projected[:, state : 2 * state]
    pad[...] = jnp.zeros_like(pad)
    pad[0, 0:1, :heads] = bias_ref[...]
    pad[1, 0:1, :heads] = rate_ref[...]
    raw = projected[:, 2 * state :] + pad[0, 0:1, :]
    rate = pad[1, 0:1, :]
    soft = jnp.maximum(raw, 0.0) + jnp.log1p(jnp.exp(-jnp.abs(raw)))
    sig = 1.0 / (1.0 + jnp.exp(-jnp.abs(raw)))
    sig = jnp.where(raw >= 0, sig, 1.0 - sig)
    small = raw < -15.0
    exp_raw = jnp.exp(jnp.minimum(raw, 0.0))
    sig = jnp.where(small, exp_raw, sig)
    soft = jnp.where(small, exp_raw, soft)
    rho = jnp.where(small, 1.0, sig / jnp.where(small, 1.0, soft))
    lower = (iota(0) >= iota(1)).astype(F32)
    log = dot(lower, -soft * rate, precision=HIGH)
    log_ref[...] = log
    logt_ref[...] = log.T
    dt_ref[...] = soft
    dtt_ref[...] = soft.T
    sig_ref[...] = sig
    rho_ref[...] = rho


def prepare(shard, x, bias, rate, docs, s0, n_chip, n_dp):
    rows, width = x.shape
    state = s0.shape[1]
    pairs = width // LANES
    cols = shard.shape[1]
    square = jax.ShapeDtypeStruct((rows, LANES), F32)
    return pl.pallas_call(
        functools.partial(prep_kernel, n_chip, n_dp),
        out_shape=(jax.ShapeDtypeStruct((n_chip, 2, n_dp) + shard.shape, BF16),)
        + (square,) * 11
        + (
            jax.ShapeDtypeStruct((pairs, state, LANES), BF16),
            jax.ShapeDtypeStruct((n_chip, 2, LANES, rows), BF16),
        ),
        in_specs=[VMEM, VMEM, VMEM, VMEM, SMEM, VMEM],
        out_specs=(VMEM,) * 14,
        scratch_shapes=[
            pltpu.VMEM((2, 8, LANES), F32),
            pltpu.VMEM((rows, cols), F32),
            gather_sems(n_chip, n_dp),
        ],
        compiler_params=pltpu.CompilerParams(
            collective_id=1, has_side_effects=True, vmem_limit_bytes=VMEM_BYTES
        ),
    )(shard, x, bias, rate, docs, s0)


def pair_columns(ref, j):
    turned = pltpu.roll(ref[...], lax.rem(LANES - 2 * j, LANES), 1)
    shape = (turned.shape[0], LANES)
    return jnp.broadcast_to(turned[:, 0:1], shape), jnp.broadcast_to(turned[:, 1:2], shape)


def by_half(first, second):
    return jnp.where(iota(1, (1, LANES)) < LANES // 2, first, second)


def heads_of(value, j):
    select = (iota(1) == 2 * j + (iota(0) >= LANES // 2).astype(jnp.int32)).astype(BF16)
    high, low = split_two(value)
    return dot(high, select) + dot(low, select)


def layer_kernel(n_chip, n_dp, *refs):
    (
        shard_ref, x_ref, gate_ref, out_grad_ref, w_ref, xt_ref, s0t_ref, bf_ref, cf_ref, log_ref, logt_ref,
        dt_ref, dtt_ref, sig_ref, rho_ref, mask_ref, first_ref, kept_ref, rate_ref, skip_ref,
    ) = refs[:20]
    dproj_ref, mixed_grad_ref, gate_grad_ref, input_grad_ref, group_ref = refs[20:25]
    (
        one_shard, one_ref, later, g_ref, msg, both, total, got, back, exits, other, adj_ref, base, weights,
        x_stage, acc_scores, acc_b, acc_c, acc_y, acc_x, acc_s, acc_a, pad, sems,
    ) = refs[25:]
    (
        gather_set, shard_sems, later_sems, core_sems, local_sems, send, recv, back_send, back_recv,
        other_send, other_recv, xt_sems, xg_send, xg_recv,
    ) = sems
    near = Around(n_chip, n_dp)
    near.greet(True)
    pipe, chip, core, dp = near.pipe, near.chip, near.core, near.dp
    rows = x_ref.shape[0]
    width = x_ref.shape[1]
    state = s0t_ref.shape[1]
    half = n_chip
    chunk = 512
    heads = rate_ref.shape[1]
    proj = w_ref.shape[-1]
    w_rows = w_ref.shape[1] * w_ref.shape[2] * w_ref.shape[3]
    part = shard_ref.shape[0]

    xt_copy = remote(xt_ref.at[:, 1 - core], x_stage, xt_sems.at[0], xt_sems.at[1], near.sibling())
    xt_copy.start()

    shard_copy = remote(shard_ref, one_shard, shard_sems.at[0], shard_sems.at[1], near.partner())
    later_copy = remote(dproj_ref, later, later_sems.at[0], later_sems.at[1], near.partner())

    for ref in (acc_scores, acc_b, acc_c, acc_y, acc_x, acc_s, acc_a):
        ref[...] = jnp.zeros_like(ref)

    @pl.when(pipe == 1)
    def _():
        shard_copy.start()

        def keep(k):
            cols = pl.ds(pl.multiple_of(k * chunk, chunk), chunk)
            g_ref[:, cols] = out_grad_ref[:, cols]

        each(width // chunk, keep)
        shard_copy.wait_send()

    @pl.when(pipe == 0)
    def _():
        shard_copy.wait_recv()
        gather = Gather(near, one_ref, gather_set)
        gather.start(one_shard)
        gather.second()
        gather.third()
        gather.end()
        later_copy.wait_recv()

        def recompute(k):
            cols = pl.ds(pl.multiple_of(k * w_rows, w_rows), w_rows)
            sent = dot(later[...], one_ref[k].reshape(w_rows, proj), NT)
            g_ref[:, cols] = (out_grad_ref[:, cols].astype(F32) + sent).astype(BF16)

        each(n_chip, recompute, 2)

    ct = cf_ref[...].T.astype(BF16)

    def own(j):
        cols = tile_at(j)
        gate = gate_ref[:, cols].astype(F32)
        grad_y = g_ref[:, cols].astype(F32) * gate * jax.nn.sigmoid(gate)
        log0, log1 = pair_columns(log_ref, j)
        entry = jnp.exp(by_half(log0, log1) + first_ref[...])
        msg[j, 0:state] = dot(ct, (entry * grad_y).astype(BF16)).astype(BF16)
        msg[j, state : state + 16] = pass_rows(entry[-1:, :])

    mine = pl.ds(core * half, half)
    theirs = pl.ds((1 - core) * half, half)
    swap = remote(msg.at[theirs], both.at[core], core_sems.at[0], core_sems.at[1], near.sibling())
    keep_mine = pltpu.make_async_copy(msg.at[mine], both.at[core], local_sems.at[0])
    each(half, lambda j: own((1 - core) * half + j), UNROLL)
    swap.start()
    each(half, lambda j: own(core * half + j), UNROLL)
    keep_mine.start()
    keep_mine.wait()
    swap.wait()

    def combine(j):
        pass0 = pass_value(both[0, j, state : state + 16])
        pass1 = pass_value(both[1, j, state : state + 16])
        joined = both[0, j, :state].astype(F32) + pass0 * both[1, j, :state].astype(F32)
        total[j, :state] = joined.astype(BF16)
        total[j, state : state + 16] = pass_rows(pass0 * pass1)

    def send_copy(k):
        return remote(
            total.at[near.chip_slot(k)], got.at[chip], send.at[k], recv.at[chip], near.chip_device(k)
        )

    def combine_send(k):
        combine(near.chip_slot(k))
        send_copy(k).start()

    each(n_chip - 1, combine_send)
    combine(chip)
    got[chip] = total[chip]

    xt_copy.wait()

    def x_copy(k, src, from_core):
        to = near.dp_slot(k)
        cut = pl.ds(pl.multiple_of(to * part, part), part)
        return remote(
            src.at[:, cut], group_ref.at[dp, from_core],
            xg_send.at[from_core, k], xg_recv.at[from_core, k], near.dp_device(k),
        )

    def x_start(k):
        x_copy(k, xt_ref.at[:, core], core).start()
        x_copy(k, x_stage, 1 - core).start()

    each(n_dp - 1, x_start)
    cut = pl.ds(pl.multiple_of(dp * part, part), part)
    group_ref[dp, core] = xt_ref[:, core, cut]
    group_ref[dp, 1 - core] = x_stage[:, cut]

    scores = dot(cf_ref[...], bf_ref[...], NT, precision=HIGH)
    b_low = bf_ref[...].astype(BF16)
    c_low = cf_ref[...].astype(BF16)
    first = iota(1, (1, LANES)) < LANES // 2

    def before(j):
        cols = tile_at(j)
        x_pair = x_ref[:, cols]
        x_f = x_pair.astype(F32)
        gate = gate_ref[:, cols].astype(F32)
        sig = jax.nn.sigmoid(gate)
        g = g_ref[:, cols].astype(F32)
        grad_y = g * gate * sig
        grad_low = grad_y.astype(BF16)
        zero = jnp.zeros_like(x_pair)
        x0, x1 = jnp.where(first, x_pair, zero), jnp.where(first, zero, x_pair)
        y0, y1 = jnp.where(first, grad_low, zero), jnp.where(first, zero, grad_low)
        log0, log1 = pair_columns(log_ref, j)
        dt0, dt1 = pair_columns(dt_ref, j)
        mask = mask_ref[...]
        decay0 = jnp.exp(log0 - logt_ref[pl.ds(2 * j, 1), :] + mask) * dtt_ref[pl.ds(2 * j, 1), :]
        decay1 = jnp.exp(log1 - logt_ref[pl.ds(2 * j + 1, 1), :] + mask) * dtt_ref[pl.ds(2 * j + 1, 1), :]
        mix0 = (decay0 * scores).astype(BF16)
        mix1 = (decay1 * scores).astype(BF16)
        acc_scores[...] += dot(y0, x_pair, NT) * decay0 + dot(y1, x_pair, NT) * decay1
        log_pair = jnp.where(first, log0, log1)
        entry = jnp.exp(log_pair + first_ref[...])
        s0t = s0t_ref[j]
        y = dot(mix0, x0) + dot(mix1, x1) + entry * dot(c_low, s0t)
        acc_c[...] += dot((entry * grad_y).astype(BF16), s0t, NT)
        inner = dot(mix0, y0, TN) + dot(mix1, y1, TN)
        weights[j] = jnp.exp(log_pair[-1:, :] - log_pair + kept_ref[...]) * jnp.where(first, dt0, dt1)
        x_inner = x_f * inner
        acc_y[...] += heads_of(grad_low.astype(F32) * y - x_inner, j)
        acc_x[...] += heads_of(x_inner, j)
        skip = skip_ref[:, cols]
        slope = sig * (1.0 + gate * (1.0 - sig))
        gate_grad_ref[:, cols] = (g * (y + skip * x_f) * slope).astype(BF16)
        base[j] = inner + skip * grad_y

    each(half, before, UNROLL)

    def back_copy(k):
        return remote(
            back.at[k], exits.at[chip], back_send.at[k], back_recv.at[chip], {"seg": k * 2 + core}
        )

    def scan(step, carry):
        k = n_chip - 1 - step

        @pl.when(k != chip)
        def _():
            remote(got.at[k], got.at[k], send.at[0], recv.at[k], near.sibling()).wait_recv()

        back[k] = carry.astype(BF16)

        @pl.when(k != chip)
        def _():
            back_copy(k).start()

        return got[k, :state].astype(F32) + pass_value(got[k, state : state + 16]) * carry

    lax.fori_loop(0, n_chip, scan, jnp.zeros((state, LANES), F32))
    exits[chip] = back[chip]
    each(half, lambda j: before(half + j), UNROLL)

    def other_copy(j):
        return remote(
            other.at[j], adj_ref.at[core * half + j], other_send.at[j], other_recv.at[j], near.sibling()
        )

    def finish(j):
        @pl.when(j != chip)
        def _():
            remote(back.at[j], exits.at[j], back_send.at[0], back_recv.at[j], near.sibling()).wait_recv()

        after = exits[j].astype(F32)
        pass1 = pass_value(both[1, j, state : state + 16])
        earlier = both[1, j, :state].astype(F32) + pass1 * after
        is_later = core == 1
        adj_ref[core * half + j] = jnp.where(is_later, after, earlier).astype(BF16)
        other[j] = jnp.where(is_later, earlier, after).astype(BF16)
        other_copy(j).start()

    each(n_chip, finish)

    def after_scan(j):
        cols = tile_at(j)
        adj = adj_ref[j]
        weight = weights[j]
        x_f = x_ref[:, cols].astype(F32)
        outer = weight * dot(b_low, adj)
        acc_b[...] += dot((x_f * weight).astype(BF16), adj, NT)
        acc_s[...] += heads_of(x_f * outer, j)
        log0, log1 = pair_columns(log_ref, j)
        last = jnp.exp(by_half(log0[-8:], log1[-8:]) + first_ref[rows - 8 :, :])[-1:]
        passed = last * jnp.sum(adj.astype(F32) * s0t_ref[j].astype(F32), axis=0, keepdims=True)
        select = (iota(1) == 2 * j + (iota(0) >= LANES // 2).astype(jnp.int32)).astype(BF16)
        high, low = split_two(jnp.broadcast_to(passed, (8, LANES)))
        acc_a[...] += dot(high, select) + dot(low, select)
        mixed_grad_ref[:, cols] = (base[j] + outer).astype(BF16)

    each(half, lambda j: after_scan(core * half + j), UNROLL)
    each(half, lambda j: other_copy(j).wait())
    each(half, lambda j: after_scan((1 - core) * half + j), UNROLL)

    pad[...] = jnp.zeros_like(pad)
    pad[0:1, :heads] = rate_ref[...]
    u = acc_x[...] + acc_s[...]
    last = jnp.sum(acc_s[...], axis=0, keepdims=True) + acc_a[0:1, :]
    upper = (iota(0) <= iota(1)).astype(F32)
    log_grad = dot(upper, acc_y[...] - acc_s[...], precision=HIGH) + last
    raw_grad = u * rho_ref[...] - pad[0:1, :] * log_grad * sig_ref[...]
    b_grad = acc_b[...] + dot(acc_scores[...].T, cf_ref[...], precision=HIGH)
    c_grad = acc_c[...] + dot(acc_scores[...], bf_ref[...], precision=HIGH)
    dproj_ref[:, 0:LANES] = b_grad.astype(BF16)
    dproj_ref[:, LANES : 2 * LANES] = c_grad.astype(BF16)
    dproj_ref[:, 2 * LANES :] = raw_grad.astype(BF16)

    @pl.when(pipe == 1)
    def _():
        later_copy.start()

    def give(k):
        cols = pl.ds(pl.multiple_of(k * w_rows, w_rows), w_rows)
        sent = dot(dproj_ref[...], w_ref[k].reshape(w_rows, proj), NT)
        input_grad_ref[:, cols] = (g_ref[:, cols].astype(F32) + sent).astype(BF16)

    each(n_chip, give, 2)

    @pl.when(pipe == 1)
    def _():
        later_copy.wait_send()

    each(n_chip - 1, lambda k: send_copy(k).wait_send())

    def sent_back(k):
        @pl.when(k != chip)
        def _():
            back_copy(k).wait_send()

    each(n_chip, sent_back)

    def x_wait(k):
        x_copy(k, xt_ref.at[:, core], core).wait()
        x_copy(k, x_stage, 1 - core).wait()

    each(n_dp - 1, x_wait)


def layer_grads(args, n_chip, n_dp):
    shard, x = args[:2]
    rows, width = x.shape
    pairs = width // LANES
    state = args[6].shape[1]
    cols = shard.shape[1]
    part = shard.shape[0]
    dma = pltpu.SemaphoreType.DMA
    square = pltpu.VMEM((rows, LANES), F32)
    line = jax.ShapeDtypeStruct((rows, width), BF16)
    return pl.pallas_call(
        functools.partial(layer_kernel, n_chip, n_dp),
        out_shape=(
            jax.ShapeDtypeStruct((rows, cols), BF16), line, line, line,
            jax.ShapeDtypeStruct((n_dp, 2, n_chip, part, rows), BF16),
        ),
        in_specs=[VMEM] * len(args),
        out_specs=(VMEM,) * 5,
        scratch_shapes=[
            pltpu.VMEM(shard.shape, BF16),
            pltpu.VMEM((n_chip, 2, n_dp) + shard.shape, BF16),
            pltpu.VMEM((rows, cols), BF16),
            pltpu.VMEM((rows, width), BF16),
            pltpu.VMEM((pairs, state + 16, LANES), BF16),
            pltpu.VMEM((2, n_chip, state + 16, LANES), BF16),
            pltpu.VMEM((n_chip, state + 16, LANES), BF16),
            pltpu.VMEM((n_chip, state + 16, LANES), BF16),
            pltpu.VMEM((n_chip, state, LANES), BF16),
            pltpu.VMEM((n_chip, state, LANES), BF16),
            pltpu.VMEM((n_chip, state, LANES), BF16),
            pltpu.VMEM((pairs, state, LANES), BF16),
            pltpu.VMEM((pairs, rows, LANES), F32),
            pltpu.VMEM((pairs, rows, LANES), F32),
            pltpu.VMEM((n_chip, LANES, rows), BF16),
        ]
        + [square] * 6
        + [pltpu.VMEM((8, LANES), F32)] * 2
        + [
            (
                gather_sems(n_chip, n_dp), dma((2,)), dma((2,)), dma((2,)), dma((1,)), dma((n_chip,)),
                dma((n_chip,)), dma((n_chip,)), dma((n_chip,)), dma((n_chip,)), dma((n_chip,)), dma((2,)),
                dma((2, n_dp - 1)), dma((2, n_dp - 1)),
            )
        ],
        compiler_params=pltpu.CompilerParams(
            collective_id=2, has_side_effects=True, vmem_limit_bytes=VMEM_BYTES
        ),
    )(*args)


def weight_kernel(n_chip, n_dp, xg_ref, dproj_ref, out_ref, grads, part, total, got, sems):
    near = Around(n_chip, n_dp)
    near.greet(False)
    chip, core, dp = near.chip, near.core, near.dp
    dp_send, dp_recv, core_sems, send, recv = sems
    rows = out_ref.shape[0]
    cols = out_ref.shape[1]
    grads[core, dp] = dproj_ref[...]

    def dp_copy(k):
        return remote(dproj_ref, grads.at[core, dp], dp_send.at[k], dp_recv.at[k], near.dp_device(k))

    each(n_dp - 1, lambda k: dp_copy(k).start())
    total[...] = jnp.zeros_like(total)

    def add(from_core, k):
        total[...] += dot(xg_ref[k, from_core].reshape(-1, xg_ref.shape[4]), grads[from_core, k])

    add(core, dp)
    each(n_dp - 1, lambda k: dp_copy(k).wait_recv())
    swap = remote(grads.at[core], grads.at[core], core_sems.at[0], core_sems.at[1], near.sibling())
    swap.start()
    each(n_dp - 1, lambda k: add(core, near.dp_slot(k)))
    swap.wait()
    each(n_dp, lambda k: add(1 - core, k))

    def send_copy(k):
        return remote(part.at[near.chip_slot(k)], got.at[k], send.at[k], recv.at[k], near.chip_device(k))

    def ship(k):
        slot = near.chip_slot(k)
        part[slot] = total[pl.ds(pl.multiple_of(slot * rows, rows), rows), :].astype(BF16)
        send_copy(k).start()

    each(n_chip - 1, ship)
    out_ref[...] = total[pl.ds(pl.multiple_of(chip * rows, rows), rows), :cols]

    def collect(k):
        send_copy(k).wait_recv()
        out_ref[...] += got[k, :, :cols].astype(F32)

    each(n_chip - 1, collect)
    each(n_chip - 1, lambda k: send_copy(k).wait_send())
    each(n_dp - 1, lambda k: dp_copy(k).wait_send())


def weight_gradient(xg, dproj, proj_cols, n_chip, n_dp):
    rows = xg.shape[3]
    cols = dproj.shape[1]
    dma = pltpu.SemaphoreType.DMA
    return pl.pallas_call(
        functools.partial(weight_kernel, n_chip, n_dp),
        out_shape=jax.ShapeDtypeStruct((rows, proj_cols), F32),
        in_specs=[VMEM, VMEM],
        out_specs=VMEM,
        scratch_shapes=[
            pltpu.VMEM((2, n_dp) + dproj.shape, BF16),
            pltpu.VMEM((n_chip, rows, cols), BF16),
            pltpu.VMEM((n_chip * rows, cols), F32),
            pltpu.VMEM((n_chip - 1, rows, cols), BF16),
            (dma((n_dp - 1,)), dma((n_dp - 1,)), dma((2,)), dma((n_chip - 1,)), dma((n_chip - 1,))),
        ],
        compiler_params=pltpu.CompilerParams(
            collective_id=3, has_side_effects=True, vmem_limit_bytes=VMEM_BYTES
        ),
    )(xg, dproj)


def local(
    inputs, mixed, gate_in, entry_states, out_grad, doc_lengths, proj_weight, decay_rate, dt_bias, skip_gain
):
    n_chip = lax.axis_size("seg") // 2
    n_dp = lax.axis_size("dp")
    x = inputs[0, 0]
    width = x.shape[1]
    s0 = entry_states.reshape(width, entry_states.shape[-1])
    proj_cols = proj_weight.shape[2]
    shard = jnp.pad(proj_weight[0], ((0, 0), (0, -proj_cols % LANES)))
    w, bf, cf, log, logt, dt, dtt, sig, rho, mask, first, kept, s0t, xt = prepare(
        shard, x, dt_bias, decay_rate, doc_lengths, s0, n_chip, n_dp
    )
    skip = jnp.repeat(skip_gain, width // skip_gain.shape[1], axis=1)
    dproj, mixed_grad, gate_grad, input_grad, group = layer_grads(
        (
            shard, mixed[0, 0], gate_in[0, 0], out_grad[0], w, xt, s0t, bf, cf, log, logt, dt, dtt, sig, rho,
            mask, first, kept, decay_rate, skip,
        ),
        n_chip,
        n_dp,
    )
    weight_grad = weight_gradient(group, dproj, proj_cols, n_chip, n_dp)
    return (
        input_grad[None, None],
        mixed_grad[None, None],
        gate_grad[None, None],
        weight_grad[None],
    )


def solution(mesh):
    in_specs = (
        P("pipe", "dp", "seg", None),
        P("pipe", "dp", "seg", None),
        P("pipe", "dp", "seg", None),
        P("pipe", "dp", "seg", None, None, None),
        P("dp", "seg", None),
        P("dp", None),
        P("pipe", ("seg", "dp"), None),
        P("pipe", None),
        P("pipe", None),
        P("pipe", None),
    )
    out_specs = (
        P("pipe", "dp", "seg", None),
        P("pipe", "dp", "seg", None),
        P("pipe", "dp", "seg", None),
        P("pipe", ("seg", "dp"), None),
    )
    return jax.shard_map(local, mesh=mesh, in_specs=in_specs, out_specs=out_specs, check_vma=False)
```

time: 289 us -> 185 us (0.64)
  Pallas kernels: 284 us -> 176 us
  local copies, waits for them, and re-layouts: 3.5 us -> 7.65 us
    pallas_call x9 -> x2, Pallas kernels: 255 us -> 149 us  [the longest x1 101 us: layer_grads(): pl.pallas_call(functools.partial(layer_kernel, n_chip, n_dp), out_shape=(...]
    unnamed x5 -> x10, local copies, waits for them, and re-layouts: 1.43 us -> 4.87 us
where the time goes in v2:
time: 185 us; the launch traced here: 184 us
  Pallas kernels  176 us (95%)
  local copies, waits for them, and re-layouts  7.65 us (4%)
    pallas_call x1, Pallas kernels, layer_grads(): pl.pallas_call(functools.partial(layer_kernel, n_chip, n_dp), out_shape=(...  101 us
    pallas_call x1, Pallas kernels, prepare(): pl.pallas_call(functools.partial(prep_kernel, n_chip, n_dp), out_shape=(j...  48.3 us
    pallas_call x1, Pallas kernels, weight_gradient(): pl.pallas_call(functools.partial(weight_kernel, n_chip, n_dp), out_shape=...  26.8 us
    unnamed x10, local copies, waits for them, and re-layouts  4.87 us

profile of v2, /device:TPU:1, one launch (start us, length us, event | category | flops | bytes accessed | tf_op | source)
XLA Modules:
  0.0 184.4 jit_solution(4320030111081604541)
XLA Ops:
  0.6 1.4 pad.4.shard_ref.refs_0_
  2.0 0.7 broadcast_in_dim.17
  2.7 0.7 broadcast_in_dim.18.refs_19_
  3.4 48.3 %shard_map.132 = (bf16[16,2,4,32,384]{4,3,2,1,0:T(8,128)(2,1)}, f32[128,128]{1,0:T(8,128)}, f32[128,128]{1,0:T(8,128)}, f32[128,128]{1,0:T(8,128)}, f32[128,128]...) custom-call(bf16[32,384]{1,0:T(8,128)(2,1)} %pad.4.shard_ref.refs_0_, ...), custom_call_target="tpu_custom_call" | custom-call | tf_op jit(solution)/shard_map/pallas_call | solution.py:251
  51.8 100.9 %shard_map.133 = (bf16[128,384]{1,0:T(8,128)(2,1)}, bf16[128,4096]{1,0:T(8,128)(2,1)}, bf16[128,4096]{1,0:T(8,128)(2,1)}, bf16[128,4096]{1,0:T(8,128)(2,1)}, bf16[4,2,16,32,128]{4,3,2,1,0:T(8,128)(2,1)}) custom-call(bf16[32,384]{1,0:T(8,128)(2,1)} %pad.4.shard_ref.refs_0_, bf16[128,4096]{1,0:T(8,128)(2,1)} %bitcast.16, bf16[128,4096]{1,0:T(8,128)(2,1)} %bitcast.17, ...), custom_call_target="tpu_custom_call" | custom-call | tf_op jit(solution)/shard_map/pallas_call | solution.py:573
  152.6 0.0 copy-start.1
  152.7 0.0 copy-start
  152.7 26.8 %shard_map.134 = f32[32,320]{1,0:T(8,128)} custom-call(bf16[4,2,16,32,128]{4,3,2,1,0:T(8,128)(2,1)} %get-tuple-element.40.xg_ref, bf16[128,384]{1,0:T(8,128)(2,1)} %get-tuple-element.41.dproj_ref), custom_call_target="tpu_custom_call" | custom-call | tf_op jit(solution)/shard_map/pallas_call | solution.py:663
  179.5 0.0 copy-start.2
  179.5 2.3 %copy.18 = bf16[1,1,128,4096]{3,2,1,0:T(8,128)(2,1)} copy(bf16[1,1,128,4096]{3,2,1,0:T(8,128)(2,1)} %bitcast.15) | data formatting | bytes 2097152
  181.8 0.0 copy-done.1
  181.8 1.0 copy.19
  182.8 0.0 copy-done
  182.8 1.0 copy.20
  183.7 0.0 copy-done.2
  183.7 0.6 copy.21
Async XLA Ops:
  152.6 29.1 %copy-start.1 = (bf16[128,4096]{1,0:T(8,128)(2,1)S(1)}, bf16[128,4096]{1,0:T(8,128)(2,1)}, u32[]{:S(2)}) copy-start(bf16[128,4096]{1,0:T(8,128)(2,1)} %get-tuple-element.38) | copy-start | bytes 3145732
  152.7 30.1 %copy-start = (bf16[128,4096]{1,0:T(8,128)(2,1)S(1)}, bf16[128,4096]{1,0:T(8,128)(2,1)}, u32[]{:S(2)}) copy-start(bf16[128,4096]{1,0:T(8,128)(2,1)} %get-tuple-element.39) | copy-start | bytes 3145732
  179.5 4.3 %copy-start.2 = (f32[32,320]{1,0:T(8,128)S(1)}, f32[32,320]{1,0:T(8,128)}, u32[]{:S(2)}) copy-start(f32[32,320]{1,0:T(8,128)} %shard_map.134) | copy-start | bytes 122884

commit v3 on v2

v3 whole, which is shorter than its diff:
```python
import functools

import jax
import jax.numpy as jnp
from jax import lax
from jax.experimental import pallas as pl
from jax.experimental.pallas import tpu as pltpu
from jax.sharding import PartitionSpec as P

MESH = pl.DeviceIdType.MESH
F32 = jnp.float32
BF16 = jnp.bfloat16
HIGH = lax.Precision.HIGHEST
LANES = 128
NEG = -1e30
UNROLL = 4
VMEM_BYTES = 56 * 1024 * 1024
VMEM = pl.BlockSpec(memory_space=pltpu.VMEM)
SMEM = pl.BlockSpec(memory_space=pltpu.SMEM)
NN = (((1,), (0,)), ((), ()))
NT = (((1,), (1,)), ((), ()))
TN = (((0,), (0,)), ((), ()))


def dot(a, b, dims=NN, precision=None):
    return lax.dot_general(a, b, dims, precision=precision, preferred_element_type=F32)


def iota(axis, shape=(LANES, LANES)):
    return lax.broadcasted_iota(jnp.int32, shape, axis)


def tile_at(j):
    return pl.ds(pl.multiple_of(j * LANES, LANES), LANES)


def split_two(value):
    high = value.astype(BF16)
    low = (value - high.astype(F32)).astype(BF16)
    return high, low


def split_three(value):
    high = value.astype(BF16)
    rest = value - high.astype(F32)
    mid = rest.astype(BF16)
    low = (rest - mid.astype(F32)).astype(BF16)
    return high, mid, low


def pass_rows(value):
    high, mid, low = split_three(value)
    row = iota(0, (16, LANES))
    zero = jnp.zeros((16, LANES), F32)
    out = jnp.where(row == 0, high.astype(F32), zero)
    out = jnp.where(row == 1, mid.astype(F32), out)
    out = jnp.where(row == 2, low.astype(F32), out)
    return out.astype(BF16)


def pass_value(rows):
    return jnp.sum(rows.astype(F32), axis=0, keepdims=True)


def place():
    seg = lax.axis_index("seg")
    chip = seg // 2
    core = seg - 2 * chip
    return lax.axis_index("pipe"), seg, chip, core, lax.axis_index("dp")


def greet(devices):
    barrier = pltpu.get_barrier_semaphore()
    for count, device_of in devices:
        def one(k, carry, device_of=device_of):
            pl.semaphore_signal(barrier, inc=1, device_id=device_of(k), device_id_type=MESH)
            return carry

        lax.fori_loop(0, count, one, 0)
    pl.semaphore_wait(barrier, sum(count for count, _ in devices))


def remote(src, dst, send_sem, recv_sem, device):
    return pltpu.make_async_remote_copy(
        src_ref=src, dst_ref=dst, send_sem=send_sem, recv_sem=recv_sem,
        device_id=device, device_id_type=MESH,
    )


def each(count, body, unroll=1):
    def step(k, carry):
        body(k)
        return carry

    lax.fori_loop(0, count, step, 0, unroll=unroll)


class Around:
    def __init__(self, n_chip, n_dp):
        self.n_chip, self.n_dp = n_chip, n_dp
        self.pipe, self.seg, self.chip, self.core, self.dp = place()

    def chip_slot(self, k):
        return lax.rem(self.chip + 1 + k, self.n_chip)

    def chip_device(self, k):
        return {"seg": self.chip_slot(k) * 2 + self.core}

    def dp_slot(self, k):
        return lax.rem(self.dp + 1 + k, self.n_dp)

    def dp_device(self, k):
        return {"dp": self.dp_slot(k)}

    def sibling(self, k=0):
        return {"seg": self.seg + 1 - 2 * self.core}

    def partner(self, k=0):
        return {"pipe": 1 - self.pipe}

    def greet(self, with_pipe):
        met = [(self.n_chip - 1, self.chip_device), (self.n_dp - 1, self.dp_device), (1, self.sibling)]
        greet(met + ([(1, self.partner)] if with_pipe else []))


class Gather:
    def __init__(self, near, dst, sems):
        self.near, self.dst = near, dst
        self.chip_send, self.chip_recv, self.dp_send, self.dp_recv, self.core_sems = sems

    def chip_copy(self, k):
        near = self.near
        block = self.dst.at[near.chip, near.core, near.dp]
        return remote(block, block, self.chip_send.at[k], self.chip_recv.at[k], near.chip_device(k))

    def dp_copy(self, k):
        block = self.dst.at[:, self.near.core, self.near.dp]
        return remote(block, block, self.dp_send.at[k], self.dp_recv.at[k], self.near.dp_device(k))

    def core_copy(self):
        block = self.dst.at[:, self.near.core]
        return remote(block, block, self.core_sems.at[0], self.core_sems.at[1], self.near.sibling())

    def start(self, src):
        near = self.near
        self.dst[near.chip, near.core, near.dp] = src[...]
        each(near.n_chip - 1, lambda k: self.chip_copy(k).start())

    def second(self):
        each(self.near.n_chip - 1, lambda k: self.chip_copy(k).wait_recv())
        each(self.near.n_dp - 1, lambda k: self.dp_copy(k).start())

    def third(self):
        each(self.near.n_dp - 1, lambda k: self.dp_copy(k).wait_recv())
        self.core_copy().start()

    def end(self):
        self.core_copy().wait()
        each(self.near.n_chip - 1, lambda k: self.chip_copy(k).wait_send())
        each(self.near.n_dp - 1, lambda k: self.dp_copy(k).wait_send())


def gather_sems(n_chip, n_dp):
    dma = pltpu.SemaphoreType.DMA
    return (dma((n_chip - 1,)), dma((n_chip - 1,)), dma((n_dp - 1,)), dma((n_dp - 1,)), dma((2,)))


def pair_columns(ref, j):
    turned = pltpu.roll(ref[...], lax.rem(LANES - 2 * j, LANES), 1)
    shape = (turned.shape[0], LANES)
    return jnp.broadcast_to(turned[:, 0:1], shape), jnp.broadcast_to(turned[:, 1:2], shape)


def by_half(first, second):
    return jnp.where(iota(1, (1, LANES)) < LANES // 2, first, second)


def heads_of(value, j):
    select = (iota(1) == 2 * j + (iota(0) >= LANES // 2).astype(jnp.int32)).astype(BF16)
    high, low = split_two(value)
    return dot(high, select) + dot(low, select)


def layer_kernel(n_chip, n_dp, *refs):
    (
        shard_ref, x_hbm, mixed_hbm, gate_hbm, out_grad_hbm, s0_hbm, rate_ref, bias_ref, skip_ref, doc_ref,
        input_out, mixed_out, gate_out, weight_out,
        x_ref, xs_ref, gate_ref, g_ref, s0_ref, shard, own_ref, one_shard, one_ref, later,
        s0t_ref, xt_ref, x_stage, group_ref, act_ref, es_ref, weights, projected, bf_ref, cf_ref,
        log_ref, logt_ref, dt_ref, dtt_ref, sig_ref, rho_ref, mask_ref, first_ref, kept_ref, small,
        msg, both, total, got, back, exits, other, adj_ref, base, dproj_ref,
        input_grad_ref, mixed_grad_ref, gate_grad_ref,
        acc_scores, acc_b, acc_c, acc_y, acc_x, acc_s, acc_a, grads, part, whole, arrived, sems,
    ) = refs
    (
        in_sems, out_sems, own_set, one_set, shard_sems, later_sems, core_send, core_recv, send, recv,
        back_send, back_recv, other_send, other_recv, xt_sems, xg_send, xg_recv,
        dp_send, dp_recv, grad_sems, sum_send, sum_recv,
    ) = sems
    rows, width = x_ref.shape
    state = bf_ref.shape[1]
    heads = rate_ref.shape[1]
    cols_w = shard_ref.shape[1]
    piece = shard_ref.shape[0]
    proj = shard.shape[1]
    w_rows = 2 * n_dp * piece
    half = n_chip

    loads = [
        pltpu.make_async_copy(src, dst, in_sems.at[i])
        for i, (src, dst) in enumerate(
            ((gate_hbm, gate_ref), (s0_hbm, s0_ref), (x_hbm, x_ref), (out_grad_hbm, g_ref), (mixed_hbm, xs_ref))
        )
    ]
    for load in loads:
        load.start()
    shard[...] = jnp.zeros_like(shard)
    shard[:, :cols_w] = shard_ref[...]

    near = Around(n_chip, n_dp)
    near.greet(True)
    pipe, chip, core, dp = near.pipe, near.chip, near.core, near.dp
    shard_copy = remote(shard, one_shard, shard_sems.at[0], shard_sems.at[1], near.partner())
    later_copy = remote(dproj_ref, later, later_sems.at[0], later_sems.at[1], near.partner())

    gather = Gather(near, own_ref, own_set)
    gather.start(shard)

    @pl.when(pipe == 1)
    def _():
        shard_copy.start()

    for ref in (acc_scores, acc_b, acc_c, acc_y, acc_x, acc_s, acc_a, small, projected, whole):
        ref[...] = jnp.zeros_like(ref)
    small[0:1, :heads] = rate_ref[...]
    small[8:9, :heads] = bias_ref[...]
    small[16:17, :heads] = skip_ref[...]
    begin = near.seg * rows
    count_t = jnp.zeros((rows, rows), jnp.int32)
    count_s = jnp.zeros((rows, rows), jnp.int32)
    count_last = jnp.zeros((rows, rows), jnp.int32)
    start = jnp.int32(0)
    for k in range(doc_ref.shape[1] - 1):
        start = start + doc_ref[0, k]
        offset = jnp.broadcast_to(start - begin, (rows, rows))
        inside = offset >= 0
        count_t += (inside & (iota(0) >= offset)).astype(jnp.int32)
        count_s += (inside & (iota(1) >= offset)).astype(jnp.int32)
        count_last += (inside & (offset <= rows - 1)).astype(jnp.int32)
    allowed = (iota(0) >= iota(1)) & (count_t == count_s)
    mask_ref[...] = jnp.where(allowed, 0.0, NEG)
    first_ref[...] = jnp.where(count_t == 0, 0.0, NEG)
    kept_ref[...] = jnp.where(count_t == count_last, 0.0, NEG)

    def activate(j):
        gate = gate_ref[:, tile_at(j)].astype(F32)
        act_ref[j] = gate * jax.nn.sigmoid(gate)

    def turn_state(j):
        s0t_ref[j] = s0_ref[tile_at(j), :].T.astype(BF16)

    def turn_x(k):
        for c in range(2):
            xt_ref[k, c] = x_ref[:, tile_at(2 * k + c)].T

    loads[0].wait()
    each(2 * half, activate, UNROLL)
    loads[1].wait()
    each(2 * half, turn_state, UNROLL)
    gather.second()
    loads[2].wait()
    each(n_chip, turn_x, 2)
    xt_copy = remote(xt_ref.at[:, 1 - core], x_stage, xt_sems.at[0], xt_sems.at[1], near.sibling())
    xt_copy.start()
    gather.third()

    def project(c):
        def one(k):
            projected[...] += dot(x_ref[:, tile_at(2 * k + c)], own_ref[k, c].reshape(-1, proj))

        each(n_chip, one, UNROLL)

    project(core)
    gather.end()
    project(1 - core)
    bf_ref[...] = projected[:, :state]
    cf_ref[...] = projected[:, state : 2 * state]
    raw = projected[:, 2 * state :] + small[8:9, :]
    soft = jnp.maximum(raw, 0.0) + jnp.log1p(jnp.exp(-jnp.abs(raw)))
    sig = 1.0 / (1.0 + jnp.exp(-jnp.abs(raw)))
    sig = jnp.where(raw >= 0, sig, 1.0 - sig)
    tiny = raw < -15.0
    exp_raw = jnp.exp(jnp.minimum(raw, 0.0))
    sig = jnp.where(tiny, exp_raw, sig)
    soft = jnp.where(tiny, exp_raw, soft)
    sig_ref[...] = sig
    rho_ref[...] = jnp.where(tiny, 1.0, sig / jnp.where(tiny, 1.0, soft))
    lower = (iota(0) >= iota(1)).astype(F32)
    log = dot(lower, -soft * small[0:1, :], precision=HIGH)
    log_ref[...] = log
    logt_ref[...] = log.T
    dt_ref[...] = soft
    dtt_ref[...] = soft.T
    first = iota(1, (1, LANES)) < LANES // 2

    def decays(j):
        log0, log1 = pair_columns(log_ref, j)
        log_pair = jnp.where(first, log0, log1)
        entry = jnp.exp(log_pair + first_ref[...])
        es_ref[j] = entry * act_ref[j]
        msg[j, state : state + 16] = pass_rows(entry[-1:, :])

    each(2 * half, decays, UNROLL)
    loads[3].wait()

    @pl.when(pipe == 0)
    def _():
        shard_copy.wait_recv()
        later_gather = Gather(near, one_ref, one_set)
        later_gather.start(one_shard)
        later_gather.second()
        later_gather.third()
        later_gather.end()
        later_copy.wait_recv()

        def recompute(k):
            cols = pl.ds(pl.multiple_of(k * w_rows, w_rows), w_rows)
            sent = dot(later[...], one_ref[k].reshape(w_rows, proj), NT)
            g_ref[:, cols] = (g_ref[:, cols].astype(F32) + sent).astype(BF16)

        each(n_chip, recompute, 4)

    ct = cf_ref[...].T.astype(BF16)

    def own(j):
        grad = (g_ref[:, tile_at(j)].astype(F32) * es_ref[j]).astype(BF16)
        msg[j, 0:state] = dot(ct, grad).astype(BF16)

    def swap_copy(slot):
        return remote(
            msg.at[(1 - core) * half + slot], both.at[core, slot],
            core_send.at[slot], core_recv.at[slot], near.sibling(),
        )

    def combine(j):
        both[core, j] = msg[core * half + j]
        pass0 = pass_value(both[0, j, state : state + 16])
        pass1 = pass_value(both[1, j, state : state + 16])
        joined = both[0, j, :state].astype(F32) + pass0 * both[1, j, :state].astype(F32)
        total[j, :state] = joined.astype(BF16)
        total[j, state : state + 16] = pass_rows(pass0 * pass1)

    def send_copy(k):
        return remote(
            total.at[near.chip_slot(k)], got.at[chip], send.at[k], recv.at[chip], near.chip_device(k)
        )

    group = 4

    def own_group(c):
        slots = [near.chip_slot(c * group + i) for i in range(group)]
        for slot in slots:
            own((1 - core) * half + slot)
        for slot in slots:
            swap_copy(slot).start()
        for slot in slots:
            own(core * half + slot)
        for slot in slots:
            swap_copy(slot).wait()
        for slot in slots:
            combine(slot)
        for i in range(group):
            @pl.when(c * group + i < n_chip - 1)
            def _(i=i):
                send_copy(c * group + i).start()

    each(n_chip // group, own_group)
    got[chip] = total[chip]

    xt_copy.wait()

    def x_copy(k, src, from_core):
        cut = pl.ds(pl.multiple_of(near.dp_slot(k) * piece, piece), piece)
        return remote(
            src.at[:, cut], group_ref.at[dp, from_core],
            xg_send.at[from_core, k], xg_recv.at[from_core, k], near.dp_device(k),
        )

    def x_start(k):
        x_copy(k, xt_ref.at[:, core], core).start()
        x_copy(k, x_stage, 1 - core).start()

    each(n_dp - 1, x_start)
    cut = pl.ds(pl.multiple_of(dp * piece, piece), piece)
    group_ref[dp, core] = xt_ref[:, core, cut]
    group_ref[dp, 1 - core] = x_stage[:, cut]

    loads[4].wait()
    scores = dot(cf_ref[...], bf_ref[...], NT, precision=HIGH)
    b_low = bf_ref[...].astype(BF16)
    c_low = cf_ref[...].astype(BF16)

    def before(j):
        cols = tile_at(j)
        x_pair = xs_ref[:, cols]
        x_f = x_pair.astype(F32)
        gate = gate_ref[:, cols].astype(F32)
        sig = jax.nn.sigmoid(gate)
        g = g_ref[:, cols].astype(F32)
        grad_y = g * act_ref[j]
        grad_low = grad_y.astype(BF16)
        zero = jnp.zeros_like(x_pair)
        x0, x1 = jnp.where(first, x_pair, zero), jnp.where(first, zero, x_pair)
        y0, y1 = jnp.where(first, grad_low, zero), jnp.where(first, zero, grad_low)
        log0, log1 = pair_columns(log_ref, j)
        dt0, dt1 = pair_columns(dt_ref, j)
        mask = mask_ref[...]
        decay0 = jnp.exp(log0 - logt_ref[pl.ds(2 * j, 1), :] + mask) * dtt_ref[pl.ds(2 * j, 1), :]
        decay1 = jnp.exp(log1 - logt_ref[pl.ds(2 * j + 1, 1), :] + mask) * dtt_ref[pl.ds(2 * j + 1, 1), :]
        mix0 = (decay0 * scores).astype(BF16)
        mix1 = (decay1 * scores).astype(BF16)
        acc_scores[...] += dot(y0, x_pair, NT) * decay0 + dot(y1, x_pair, NT) * decay1
        log_pair = jnp.where(first, log0, log1)
        entry = jnp.exp(log_pair + first_ref[...])
        s0t = s0t_ref[j]
        y = dot(mix0, x0) + dot(mix1, x1) + entry * dot(c_low, s0t)
        acc_c[...] += dot((entry * grad_y).astype(BF16), s0t, NT)
        inner = dot(mix0, y0, TN) + dot(mix1, y1, TN)
        weights[j] = jnp.exp(log_pair[-1:, :] - log_pair + kept_ref[...]) * jnp.where(first, dt0, dt1)
        x_inner = x_f * inner
        acc_y[...] += heads_of(grad_low.astype(F32) * y - x_inner, j)
        acc_x[...] += heads_of(x_inner, j)
        skip = pltpu.roll(small[16:24, :], lax.rem(LANES - 2 * j, LANES), 1)
        skip = by_half(skip[0:1, 0:1], skip[0:1, 1:2])
        slope = sig * (1.0 + gate * (1.0 - sig))
        gate_grad_ref[:, cols] = (g * (y + skip * x_f) * slope).astype(BF16)
        base[j] = inner + skip * grad_y

    each(half, before, UNROLL)

    def back_copy(k):
        return remote(
            back.at[k], exits.at[chip], back_send.at[k], back_recv.at[chip], {"seg": k * 2 + core}
        )

    def scan(step, carry):
        k = n_chip - 1 - step

        @pl.when(k != chip)
        def _():
            remote(got.at[k], got.at[k], send.at[0], recv.at[k], near.sibling()).wait_recv()

        back[k] = carry.astype(BF16)

        @pl.when(k != chip)
        def _():
            back_copy(k).start()

        return got[k, :state].astype(F32) + pass_value(got[k, state : state + 16]) * carry

    lax.fori_loop(0, n_chip, scan, jnp.zeros((state, LANES), F32))
    exits[chip] = back[chip]
    each(half, lambda j: before(half + j), UNROLL)
    gate_copy = pltpu.make_async_copy(gate_grad_ref, gate_out, out_sems.at[0])
    gate_copy.start()

    def other_copy(j):
        return remote(
            other.at[j], adj_ref.at[core * half + j], other_send.at[j], other_recv.at[j], near.sibling()
        )

    def finish(j):
        @pl.when(j != chip)
        def _():
            remote(back.at[j], exits.at[j], back_send.at[0], back_recv.at[j], near.sibling()).wait_recv()

        after = exits[j].astype(F32)
        pass1 = pass_value(both[1, j, state : state + 16])
        earlier = both[1, j, :state].astype(F32) + pass1 * after
        is_later = core == 1
        adj_ref[core * half + j] = jnp.where(is_later, after, earlier).astype(BF16)
        other[j] = jnp.where(is_later, earlier, after).astype(BF16)
        other_copy(j).start()

    each(n_chip, finish)

    def after_scan(j):
        cols = tile_at(j)
        adj = adj_ref[j]
        weight = weights[j]
        x_f = xs_ref[:, cols].astype(F32)
        outer = weight * dot(b_low, adj)
        acc_b[...] += dot((x_f * weight).astype(BF16), adj, NT)
        acc_s[...] += heads_of(x_f * outer, j)
        last = pass_value(msg[j, state : state + 16])
        passed = last * jnp.sum(adj.astype(F32) * s0t_ref[j].astype(F32), axis=0, keepdims=True)
        select = (iota(1) == 2 * j + (iota(0) >= LANES // 2).astype(jnp.int32)).astype(BF16)
        high, low = split_two(jnp.broadcast_to(passed, (8, LANES)))
        acc_a[...] += dot(high, select) + dot(low, select)
        mixed_grad_ref[:, cols] = (base[j] + outer).astype(BF16)

    each(half, lambda j: after_scan(core * half + j), UNROLL)
    each(half, lambda j: other_copy(j).wait())
    each(half, lambda j: after_scan((1 - core) * half + j), UNROLL)

    u = acc_x[...] + acc_s[...]
    last = jnp.sum(acc_s[...], axis=0, keepdims=True) + acc_a[0:1, :]
    upper = (iota(0) <= iota(1)).astype(F32)
    log_grad = dot(upper, acc_y[...] - acc_s[...], precision=HIGH) + last
    raw_grad = u * rho_ref[...] - small[0:1, :] * log_grad * sig_ref[...]
    b_grad = acc_b[...] + dot(acc_scores[...].T, cf_ref[...], precision=HIGH)
    c_grad = acc_c[...] + dot(acc_scores[...], bf_ref[...], precision=HIGH)
    dproj_ref[:, 0:LANES] = b_grad.astype(BF16)
    dproj_ref[:, LANES : 2 * LANES] = c_grad.astype(BF16)
    dproj_ref[:, 2 * LANES :] = raw_grad.astype(BF16)

    @pl.when(pipe == 1)
    def _():
        later_copy.start()

    def dp_copy(k):
        return remote(dproj_ref, grads.at[core, dp], dp_send.at[k], dp_recv.at[k], near.dp_device(k))

    each(n_dp - 1, lambda k: dp_copy(k).start())
    mixed_copy = pltpu.make_async_copy(mixed_grad_ref, mixed_out, out_sems.at[1])
    mixed_copy.start()
    grads[core, dp] = dproj_ref[...]

    def give(k):
        cols = pl.ds(pl.multiple_of(k * w_rows, w_rows), w_rows)
        sent = dot(dproj_ref[...], own_ref[k].reshape(w_rows, proj), NT)
        input_grad_ref[:, cols] = (g_ref[:, cols].astype(F32) + sent).astype(BF16)

    each(n_chip, give, 4)
    input_copy = pltpu.make_async_copy(input_grad_ref, input_out, out_sems.at[2])
    input_copy.start()

    def x_wait(k):
        x_copy(k, xt_ref.at[:, core], core).wait()
        x_copy(k, x_stage, 1 - core).wait()

    each(n_dp - 1, x_wait)

    def add(c, k):
        whole[...] += dot(group_ref[k, c].reshape(-1, rows), grads[c, k])

    each(n_dp - 1, lambda k: dp_copy(k).wait_recv())
    grad_swap = remote(grads.at[core], grads.at[core], grad_sems.at[0], grad_sems.at[1], near.sibling())
    grad_swap.start()
    each(n_dp, lambda k: add(core, k), 2)
    grad_swap.wait()
    each(n_dp, lambda k: add(1 - core, k), 2)

    def sum_copy(k):
        return remote(
            part.at[near.chip_slot(k)], arrived.at[k], sum_send.at[k], sum_recv.at[k], near.chip_device(k)
        )

    def ship(k):
        slot = near.chip_slot(k)
        part[slot] = whole[pl.ds(pl.multiple_of(slot * piece, piece), piece), :].astype(BF16)
        sum_copy(k).start()

    each(n_chip - 1, ship)
    weight_out[...] = whole[pl.ds(pl.multiple_of(chip * piece, piece), piece), :cols_w]

    @pl.when(pipe == 1)
    def _():
        shard_copy.wait_send()
        later_copy.wait_send()

    each(n_chip - 1, lambda k: send_copy(k).wait_send())

    def sent_back(k):
        @pl.when(k != chip)
        def _():
            back_copy(k).wait_send()

    each(n_chip, sent_back)
    each(n_dp - 1, lambda k: dp_copy(k).wait_send())

    def collect(k):
        sum_copy(k).wait_recv()
        weight_out[...] += arrived[k, :, :cols_w].astype(F32)

    each(n_chip - 1, collect)
    each(n_chip - 1, lambda k: sum_copy(k).wait_send())
    gate_copy.wait()
    mixed_copy.wait()
    input_copy.wait()


def layer_grads(shard, x, mixed, gate, out_grad, s0, rate, bias, skip, docs, n_chip, n_dp):
    rows, width = x.shape
    pairs = width // LANES
    state = s0.shape[1]
    piece, cols = shard.shape
    proj = cols + -cols % LANES
    dma = pltpu.SemaphoreType.DMA
    line = jax.ShapeDtypeStruct((rows, width), BF16)
    whole_line = pltpu.VMEM((rows, width), BF16)
    square = pltpu.VMEM((rows, LANES), F32)
    full_w = pltpu.VMEM((n_chip, 2, n_dp, piece, proj), BF16)
    wide = pltpu.VMEM((pairs, rows, LANES), F32)
    message = pltpu.VMEM((n_chip, state + 16, LANES), BF16)
    plain = pltpu.VMEM((n_chip, state, LANES), BF16)
    anywhere = pl.BlockSpec(memory_space=pl.ANY)
    chips, dps = dma((n_chip,)), dma((n_dp - 1,))
    return pl.pallas_call(
        functools.partial(layer_kernel, n_chip, n_dp),
        out_shape=(line, line, line, jax.ShapeDtypeStruct((piece, cols), F32)),
        in_specs=[VMEM] + [anywhere] * 5 + [VMEM] * 3 + [SMEM],
        out_specs=(anywhere, anywhere, anywhere, VMEM),
        scratch_shapes=[
            whole_line, whole_line, whole_line, whole_line,
            pltpu.VMEM((width, state), F32),
            pltpu.VMEM((piece, proj), BF16),
            full_w,
            pltpu.VMEM((piece, proj), BF16),
            full_w,
            pltpu.VMEM((rows, proj), BF16),
            pltpu.VMEM((pairs, state, LANES), BF16),
            pltpu.VMEM((n_chip, 2, LANES, rows), BF16),
            pltpu.VMEM((n_chip, LANES, rows), BF16),
            pltpu.VMEM((n_dp, 2, n_chip, piece, rows), BF16),
            wide, wide, wide,
            pltpu.VMEM((rows, proj), F32),
        ]
        + [square] * 11
        + [
            pltpu.VMEM((24, LANES), F32),
            pltpu.VMEM((pairs, state + 16, LANES), BF16),
            pltpu.VMEM((2, n_chip, state + 16, LANES), BF16),
            message, message, plain, plain, plain,
            pltpu.VMEM((pairs, state, LANES), BF16),
            wide,
            pltpu.VMEM((rows, proj), BF16),
            whole_line, whole_line, whole_line,
        ]
        + [square] * 6
        + [
            pltpu.VMEM((8, LANES), F32),
            pltpu.VMEM((2, n_dp, rows, proj), BF16),
            pltpu.VMEM((n_chip, piece, proj), BF16),
            pltpu.VMEM((n_chip * piece, proj), F32),
            pltpu.VMEM((n_chip - 1, piece, proj), BF16),
            (
                dma((5,)), dma((3,)), gather_sems(n_chip, n_dp), gather_sems(n_chip, n_dp), dma((2,)), dma((2,)),
                chips, chips, chips, chips, chips, chips, chips, chips, dma((2,)),
                dma((2, n_dp - 1)), dma((2, n_dp - 1)), dps, dps, dma((2,)), chips, chips,
            ),
        ],
        compiler_params=pltpu.CompilerParams(
            collective_id=1, has_side_effects=True, vmem_limit_bytes=VMEM_BYTES
        ),
    )(shard, x, mixed, gate, out_grad, s0, rate, bias, skip, docs)


def deliver_kernel(*refs):
    count = len(refs) // 2
    for i in range(count):
        refs[count + i][...] = refs[i][...]


def deliver(values):
    steps = 4
    specs = [
        pl.BlockSpec((value.shape[0] // steps, value.shape[1]), lambda i: (i, 0)) for value in values
    ]
    return pl.pallas_call(
        deliver_kernel,
        grid=(steps,),
        out_shape=tuple(jax.ShapeDtypeStruct(value.shape, value.dtype) for value in values),
        in_specs=specs,
        out_specs=tuple(specs),
    )(*values)


def local(
    inputs, mixed, gate_in, entry_states, out_grad, doc_lengths, proj_weight, decay_rate, dt_bias, skip_gain
):
    n_chip = lax.axis_size("seg") // 2
    n_dp = lax.axis_size("dp")
    width = inputs.shape[-1]
    s0 = entry_states.reshape(width, entry_states.shape[-1])
    outs = layer_grads(
        proj_weight[0], inputs[0, 0], mixed[0, 0], gate_in[0, 0], out_grad[0], s0,
        decay_rate, dt_bias, skip_gain, doc_lengths, n_chip, n_dp,
    )
    input_grad, mixed_grad, gate_grad, weight_grad = deliver(outs)
    return (
        input_grad[None, None],
        mixed_grad[None, None],
        gate_grad[None, None],
        weight_grad[None],
    )


def solution(mesh):
    in_specs = (
        P("pipe", "dp", "seg", None),
        P("pipe", "dp", "seg", None),
        P("pipe", "dp", "seg", None),
        P("pipe", "dp", "seg", None, None, None),
        P("dp", "seg", None),
        P("dp", None),
        P("pipe", ("seg", "dp"), None),
        P("pipe", None),
        P("pipe", None),
        P("pipe", None),
    )
    out_specs = (
        P("pipe", "dp", "seg", None),
        P("pipe", "dp", "seg", None),
        P("pipe", "dp", "seg", None),
        P("pipe", ("seg", "dp"), None),
    )
    return jax.shard_map(local, mesh=mesh, in_specs=in_specs, out_specs=out_specs, check_vma=False)
```

time: 185 us -> 159 us (0.86)
  Pallas kernels: 176 us -> 159 us
  local copies, waits for them, and re-layouts: 7.65 us -> 0 us
    pallas_call x2 -> x1, Pallas kernels: 75.1 us -> 4.16 us  [deliver(): pl.pallas_call(deliver_kernel, grid=(steps,), out_shape=tuple((jax.ShapeD...]
    pallas_call x1, Pallas kernels: 101 us -> 154 us  [layer_grads(): pl.pallas_call(functools.partial(layer_kernel, n_chip, n_dp), out_shape=(...]
    unnamed x10 -> x0, local copies, waits for them, and re-layouts: 4.87 us -> none
where the time goes in v3:
time: 159 us
  Pallas kernels  159 us (100%)
    pallas_call x1, Pallas kernels, layer_grads(): pl.pallas_call(functools.partial(layer_kernel, n_chip, n_dp), out_shape=(...  154 us
    pallas_call x1, Pallas kernels, deliver(): pl.pallas_call(deliver_kernel, grid=(steps,), out_shape=tuple((jax.ShapeD...  4.16 us

profile of v3, /device:TPU:1, one launch (start us, length us, event | category | flops | bytes accessed | tf_op | source)
XLA Modules:
  0.0 159.1 jit_solution(7176958505271799336)
XLA Ops:
  0.6 154.3 %shard_map.129 = (bf16[128,4096]{1,0:T(8,128)(2,1)}, bf16[128,4096]{1,0:T(8,128)(2,1)}, bf16[128,4096]{1,0:T(8,128)(2,1)}, f32[32,320]{1,0:T(8,128)}) custom-call(bf16[32,320]{1,0:T(8,128)(2,1)} %bitcast.15, bf16[128,4096]{1,0:T(8,128)(2,1)} %bitcast.11, bf16[128,4096]{1,0:T(8,128)(2,1)} %bitcast.12, bf16[128,4096]{1,0:T(8,128)(2,1)} %bitcast.13, ...), custom_call_target="tpu_custom_call" | custom-call | tf_op jit(solution)/shard_map/pallas_call | solution.py:609
  155.0 4.2 %shard_map.130 = (bf16[128,4096]{1,0:T(8,128)(2,1)}, bf16[128,4096]{1,0:T(8,128)(2,1)}, bf16[128,4096]{1,0:T(8,128)(2,1)}, f32[32,320]{1,0:T(8,128)}) custom-call(bf16[128,4096]{1,0:T(8,128)(2,1)} %get-tuple-element.12.refs_0_, bf16[128,4096]{1,0:T(8,128)(2,1)} %get-tuple-element.13.refs_1_, bf16[128,4096]{1,0:T(8,128)(2,1)} %get-tuple-element.14.refs_2_, ...), custom_call_target="tpu_custom_call" | custom-call | tf_op jit(solution)/shard_map/pallas_call | solution.py:670

commit v4 on v3

--- a/solution.py
+++ b/solution.py
@@ -40,28 +40,6 @@
     return high, low
 
 
-def split_three(value):
-    high = value.astype(BF16)
-    rest = value - high.astype(F32)
-    mid = rest.astype(BF16)
-    low = (rest - mid.astype(F32)).astype(BF16)
-    return high, mid, low
-
-
-def pass_rows(value):
-    high, mid, low = split_three(value)
-    row = iota(0, (16, LANES))
-    zero = jnp.zeros((16, LANES), F32)
-    out = jnp.where(row == 0, high.astype(F32), zero)
-    out = jnp.where(row == 1, mid.astype(F32), out)
-    out = jnp.where(row == 2, low.astype(F32), out)
-    return out.astype(BF16)
-
-
-def pass_value(rows):
-    return jnp.sum(rows.astype(F32), axis=0, keepdims=True)
-
-
 def place():
     seg = lax.axis_index("seg")
     chip = seg // 2
@@ -126,43 +104,124 @@
 class Gather:
     def __init__(self, near, dst, sems):
         self.near, self.dst = near, dst
-        self.chip_send, self.chip_recv, self.dp_send, self.dp_recv, self.core_sems = sems
+        self.chip_send, self.chip_recv, self.dp_send, self.dp_recv, self.core_send, self.core_recv = sems
+
+    def source(self, k):
+        near = self.near
+        return lax.rem(near.chip + 2 * near.n_chip - 1 - k, near.n_chip)
 
     def chip_copy(self, k):
         near = self.near
         block = self.dst.at[near.chip, near.core, near.dp]
         return remote(block, block, self.chip_send.at[k], self.chip_recv.at[k], near.chip_device(k))
 
-    def dp_copy(self, k):
-        block = self.dst.at[:, self.near.core, self.near.dp]
-        return remote(block, block, self.dp_send.at[k], self.dp_recv.at[k], self.near.dp_device(k))
-
-    def core_copy(self):
-        block = self.dst.at[:, self.near.core]
-        return remote(block, block, self.core_sems.at[0], self.core_sems.at[1], self.near.sibling())
+    def dp_copy(self, k, i):
+        near = self.near
+        block = self.dst.at[self.source(k), near.core, near.dp]
+        return remote(block, block, self.dp_send.at[k, i], self.dp_recv.at[k, i], near.dp_device(i))
+
+    def core_copy(self, k):
+        block = self.dst.at[self.source(k), self.near.core]
+        return remote(block, block, self.core_send.at[k], self.core_recv.at[k], self.near.sibling())
 
     def start(self, src):
         near = self.near
         self.dst[near.chip, near.core, near.dp] = src[...]
         each(near.n_chip - 1, lambda k: self.chip_copy(k).start())
-
-    def second(self):
-        each(self.near.n_chip - 1, lambda k: self.chip_copy(k).wait_recv())
-        each(self.near.n_dp - 1, lambda k: self.dp_copy(k).start())
-
-    def third(self):
-        each(self.near.n_dp - 1, lambda k: self.dp_copy(k).wait_recv())
-        self.core_copy().start()
-
-    def end(self):
-        self.core_copy().wait()
-        each(self.near.n_chip - 1, lambda k: self.chip_copy(k).wait_send())
-        each(self.near.n_dp - 1, lambda k: self.dp_copy(k).wait_send())
+        each(near.n_dp - 1, lambda i: self.dp_copy(near.n_chip - 1, i).start())
+
+    def spread(self):
+        near = self.near
+
+        def pass_on(k):
+            self.chip_copy(k).wait_recv()
+            for i in range(near.n_dp - 1):
+                self.dp_copy(k, i).start()
+
+        each(near.n_chip - 1, pass_on)
+
+    def over(self, use):
+        near = self.near
+
+        def pass_on(step):
+            k = lax.rem(step + near.n_chip - 1, near.n_chip)
+            for i in range(near.n_dp - 1):
+                self.dp_copy(k, i).wait_recv()
+            self.core_copy(k).start()
+            use(self.source(k), near.core)
+
+        each(near.n_chip, pass_on)
+
+    def end(self, use):
+        near = self.near
+
+        def take(step):
+            k = lax.rem(step + near.n_chip - 1, near.n_chip)
+            self.core_copy(k).wait()
+            use(self.source(k), 1 - near.core)
+
+        each(near.n_chip, take)
+
+    def sent(self):
+        near = self.near
+        each(near.n_chip - 1, lambda k: self.chip_copy(k).wait_send())
+
+        def one(k):
+            for i in range(near.n_dp - 1):
+                self.dp_copy(k, i).wait_send()
+
+        each(near.n_chip, one)
 
 
 def gather_sems(n_chip, n_dp):
     dma = pltpu.SemaphoreType.DMA
-    return (dma((n_chip - 1,)), dma((n_chip - 1,)), dma((n_dp - 1,)), dma((n_dp - 1,)), dma((2,)))
+    return (
+        dma((n_chip - 1,)), dma((n_chip - 1,)), dma((n_chip, n_dp - 1)), dma((n_chip, n_dp - 1)),
+        dma((n_chip,)), dma((n_chip,)),
+    )
+
+
+def packed(value):
+    piece = value.shape[0]
+    tail = value[:, 2 * LANES :]
+    top, low = tail[: piece // 2], tail[piece // 2 :]
+    beside = top + pltpu.roll(low, LANES // 2, 1)
+    return jnp.concatenate([value[:, :LANES], value[:, LANES : 2 * LANES], beside], axis=0)
+
+
+def unpacked(value, piece):
+    beside = value[2 * piece :]
+    first = iota(1, (1, LANES)) < LANES // 2
+    top = jnp.where(first, beside, 0.0)
+    low = jnp.where(first, pltpu.roll(beside, LANES // 2, 1), 0.0)
+    return value[:piece], value[piece : 2 * piece], jnp.concatenate([top, low], axis=0)
+
+
+def weight_tiles(ref, chip, core, piece):
+    block = ref[chip, core]
+    tail = block[:, 2 * piece :]
+    return (
+        block[:, :piece].reshape(-1, LANES),
+        block[:, piece : 2 * piece].reshape(-1, LANES),
+        jnp.concatenate([tail, tail], axis=1).reshape(-1, LANES),
+    )
+
+
+def in_top(piece):
+    lane = iota(1, (1, LANES))
+    return lane - lane // piece * piece < piece // 2
+
+
+def back_projected(dproj_ref, dt_low, ref, chip, core, piece):
+    w_b, w_c, w_t = weight_tiles(ref, chip, core, piece)
+    plain = dot(dproj_ref[:, :LANES], w_b, NT) + dot(dproj_ref[:, LANES : 2 * LANES], w_c, NT)
+    top = dot(dproj_ref[:, 2 * LANES :], w_t, NT)
+    low = dot(dt_low, w_t, NT)
+    return plain + jnp.where(in_top(piece), top, low)
+
+
+def lanes_turned(value):
+    return pltpu.roll(value.astype(F32), LANES // 2, 1).astype(BF16)
 
 
 def pair_columns(ref, j):
@@ -186,24 +245,23 @@
         shard_ref, x_hbm, mixed_hbm, gate_hbm, out_grad_hbm, s0_hbm, rate_ref, bias_ref, skip_ref, doc_ref,
         input_out, mixed_out, gate_out, weight_out,
         x_ref, xs_ref, gate_ref, g_ref, s0_ref, shard, own_ref, one_shard, one_ref, later,
-        s0t_ref, xt_ref, x_stage, group_ref, act_ref, es_ref, weights, projected, bf_ref, cf_ref,
+        s0t_ref, xt_ref, x_stage, group_ref, act_ref, weights, projected, bf_ref, cf_ref,
         log_ref, logt_ref, dt_ref, dtt_ref, sig_ref, rho_ref, mask_ref, first_ref, kept_ref, small,
-        msg, both, total, got, back, exits, other, adj_ref, base, dproj_ref,
+        msg, both, total, got, back, exits, other, adj_ref, base, dproj_ref, passes, chip_passes,
         input_grad_ref, mixed_grad_ref, gate_grad_ref,
-        acc_scores, acc_b, acc_c, acc_y, acc_x, acc_s, acc_a, grads, part, whole, arrived, sems,
+        acc_scores, acc_b, acc_c, acc_y, acc_x, acc_s, acc_a, grads, part, whole, arrived, spare, summed, sems,
     ) = refs
     (
-        in_sems, out_sems, own_set, one_set, shard_sems, later_sems, core_send, core_recv, send, recv,
+        in_sems, out_sems, own_set, one_set, shard_sems, later_sems, pass_sems, pass_send, pass_recv, core_send, core_recv, send, recv,
         back_send, back_recv, other_send, other_recv, xt_sems, xg_send, xg_recv,
-        dp_send, dp_recv, grad_sems, sum_send, sum_recv,
+        dp_send, dp_recv, grad_send, grad_recv, sum_send, sum_recv,
     ) = sems
     rows, width = x_ref.shape
     state = bf_ref.shape[1]
     heads = rate_ref.shape[1]
     cols_w = shard_ref.shape[1]
     piece = shard_ref.shape[0]
-    proj = shard.shape[1]
-    w_rows = 2 * n_dp * piece
+    proj = projected.shape[1]
     half = n_chip
 
     loads = [
@@ -214,8 +272,9 @@
     ]
     for load in loads:
         load.start()
-    shard[...] = jnp.zeros_like(shard)
-    shard[:, :cols_w] = shard_ref[...]
+    spare[...] = jnp.zeros_like(spare)
+    spare[:, :cols_w] = shard_ref[...].astype(F32)
+    shard[...] = packed(spare[...]).astype(BF16)
 
     near = Around(n_chip, n_dp)
     near.greet(True)
@@ -263,29 +322,31 @@
         for c in range(2):
             xt_ref[k, c] = x_ref[:, tile_at(2 * k + c)].T
 
+    gather.spread()
     loads[0].wait()
     each(2 * half, activate, UNROLL)
     loads[1].wait()
     each(2 * half, turn_state, UNROLL)
-    gather.second()
     loads[2].wait()
     each(n_chip, turn_x, 2)
+
+    def project(k, c):
+        x_tile = x_ref[:, tile_at(2 * k + c)]
+        zero = jnp.zeros_like(x_tile)
+        w_b, w_c, w_t = weight_tiles(own_ref, k, c, piece)
+        projected[:, :LANES] += dot(x_tile, w_b)
+        projected[:, LANES : 2 * LANES] += dot(x_tile, w_c)
+        projected[:, 2 * LANES : 3 * LANES] += dot(jnp.where(in_top(piece), x_tile, zero), w_t)
+        projected[:, 3 * LANES :] += dot(jnp.where(in_top(piece), zero, x_tile), w_t)
+
+    gather.over(project)
+    gather.end(project)
     xt_copy = remote(xt_ref.at[:, 1 - core], x_stage, xt_sems.at[0], xt_sems.at[1], near.sibling())
     xt_copy.start()
-    gather.third()
-
-    def project(c):
-        def one(k):
-            projected[...] += dot(x_ref[:, tile_at(2 * k + c)], own_ref[k, c].reshape(-1, proj))
-
-        each(n_chip, one, UNROLL)
-
-    project(core)
-    gather.end()
-    project(1 - core)
     bf_ref[...] = projected[:, :state]
     cf_ref[...] = projected[:, state : 2 * state]
-    raw = projected[:, 2 * state :] + small[8:9, :]
+    raw = projected[:, 2 * LANES : 3 * LANES] + pltpu.roll(projected[:, 3 * LANES :], LANES // 2, 1)
+    raw = jnp.where(iota(1) < heads, raw, 0.0) + small[8:9, :]
     soft = jnp.maximum(raw, 0.0) + jnp.log1p(jnp.exp(-jnp.abs(raw)))
     sig = 1.0 / (1.0 + jnp.exp(-jnp.abs(raw)))
     sig = jnp.where(raw >= 0, sig, 1.0 - sig)
@@ -303,38 +364,51 @@
     dtt_ref[...] = soft.T
     first = iota(1, (1, LANES)) < LANES // 2
 
-    def decays(j):
-        log0, log1 = pair_columns(log_ref, j)
-        log_pair = jnp.where(first, log0, log1)
-        entry = jnp.exp(log_pair + first_ref[...])
-        es_ref[j] = entry * act_ref[j]
-        msg[j, state : state + 16] = pass_rows(entry[-1:, :])
-
-    each(2 * half, decays, UNROLL)
+    passes[core] = jnp.broadcast_to(jnp.exp(log[rows - 1 :] + first_ref[rows - 1 :, :]), (8, LANES))
+    pass_copy = remote(passes.at[core], passes.at[core], pass_sems.at[0], pass_sems.at[1], near.sibling())
+    pass_copy.start()
+
+    def pass_row(value, j):
+        turned = pltpu.roll(value, lax.rem(LANES - 2 * j, LANES), 1)
+        return by_half(turned[0:1, 0:1], turned[0:1, 1:2])
+
     loads[3].wait()
+    pass_copy.wait()
+    chip_passes[chip] = passes[0] * passes[1]
+
+    def chip_pass_copy(k):
+        block = chip_passes.at[chip]
+        return remote(block, block, pass_send.at[k], pass_recv.at[k], near.chip_device(k))
+
+    each(n_chip - 1, lambda k: chip_pass_copy(k).start())
 
     @pl.when(pipe == 0)
     def _():
         shard_copy.wait_recv()
         later_gather = Gather(near, one_ref, one_set)
         later_gather.start(one_shard)
-        later_gather.second()
-        later_gather.third()
-        later_gather.end()
+        later_gather.spread()
+        later_gather.over(lambda k, c: None)
+        later_gather.end(lambda k, c: None)
+        later_gather.sent()
         later_copy.wait_recv()
+        dt_low = lanes_turned(later[:, 2 * LANES :])
 
         def recompute(k):
-            cols = pl.ds(pl.multiple_of(k * w_rows, w_rows), w_rows)
-            sent = dot(later[...], one_ref[k].reshape(w_rows, proj), NT)
-            g_ref[:, cols] = (g_ref[:, cols].astype(F32) + sent).astype(BF16)
-
-        each(n_chip, recompute, 4)
+            for c in range(2):
+                cols = tile_at(2 * k + c)
+                sent = back_projected(later, dt_low, one_ref, k, c, piece)
+                g_ref[:, cols] = (g_ref[:, cols].astype(F32) + sent).astype(BF16)
+
+        each(n_chip, recompute, 2)
 
     ct = cf_ref[...].T.astype(BF16)
 
     def own(j):
-        grad = (g_ref[:, tile_at(j)].astype(F32) * es_ref[j]).astype(BF16)
-        msg[j, 0:state] = dot(ct, grad).astype(BF16)
+        log0, log1 = pair_columns(log_ref, j)
+        entry = jnp.exp(jnp.where(first, log0, log1) + first_ref[...])
+        grad = (g_ref[:, tile_at(j)].astype(F32) * act_ref[j] * entry).astype(BF16)
+        msg[j] = dot(ct, grad).astype(BF16)
 
     def swap_copy(slot):
         return remote(
@@ -344,11 +418,8 @@
 
     def combine(j):
         both[core, j] = msg[core * half + j]
-        pass0 = pass_value(both[0, j, state : state + 16])
-        pass1 = pass_value(both[1, j, state : state + 16])
-        joined = both[0, j, :state].astype(F32) + pass0 * both[1, j, :state].astype(F32)
-        total[j, :state] = joined.astype(BF16)
-        total[j, state : state + 16] = pass_rows(pass0 * pass1)
+        pass0 = pass_row(passes[0], core * half + j)
+        total[j] = (both[0, j].astype(F32) + pass0 * both[1, j].astype(F32)).astype(BF16)
 
     def send_copy(k):
         return remote(
@@ -438,6 +509,8 @@
 
     each(half, before, UNROLL)
 
+    each(n_chip - 1, lambda k: chip_pass_copy(k).wait_recv())
+
     def back_copy(k):
         return remote(
             back.at[k], exits.at[chip], back_send.at[k], back_recv.at[chip], {"seg": k * 2 + core}
@@ -456,7 +529,7 @@
         def _():
             back_copy(k).start()
 
-        return got[k, :state].astype(F32) + pass_value(got[k, state : state + 16]) * carry
+        return got[k].astype(F32) + pass_row(chip_passes[k], core * half + chip) * carry
 
     lax.fori_loop(0, n_chip, scan, jnp.zeros((state, LANES), F32))
     exits[chip] = back[chip]
@@ -475,14 +548,21 @@
             remote(back.at[j], exits.at[j], back_send.at[0], back_recv.at[j], near.sibling()).wait_recv()
 
         after = exits[j].astype(F32)
-        pass1 = pass_value(both[1, j, state : state + 16])
-        earlier = both[1, j, :state].astype(F32) + pass1 * after
+        earlier = both[1, j].astype(F32) + pass_row(passes[1], core * half + j) * after
         is_later = core == 1
         adj_ref[core * half + j] = jnp.where(is_later, after, earlier).astype(BF16)
         other[j] = jnp.where(is_later, earlier, after).astype(BF16)
         other_copy(j).start()
 
-    each(n_chip, finish)
+    def near_first(i):
+        x_off = i - i // 2 * 2
+        m = i // 2
+        odd = m - m // 2 * 2
+        z_off = odd * ((m + 1) // 2) - (1 - odd) * (m // 2)
+        ring = n_chip // 2
+        my_x = chip // ring
+        z = lax.rem(chip - my_x * ring + z_off + ring, ring)
+        return lax.rem(my_x + x_off, 2) * ring + z
 
     def after_scan(j):
         cols = tile_at(j)
@@ -492,16 +572,29 @@
         outer = weight * dot(b_low, adj)
         acc_b[...] += dot((x_f * weight).astype(BF16), adj, NT)
         acc_s[...] += heads_of(x_f * outer, j)
-        last = pass_value(msg[j, state : state + 16])
+        last = pass_row(passes[core], j)
         passed = last * jnp.sum(adj.astype(F32) * s0t_ref[j].astype(F32), axis=0, keepdims=True)
         select = (iota(1) == 2 * j + (iota(0) >= LANES // 2).astype(jnp.int32)).astype(BF16)
         high, low = split_two(jnp.broadcast_to(passed, (8, LANES)))
         acc_a[...] += dot(high, select) + dot(low, select)
         mixed_grad_ref[:, cols] = (base[j] + outer).astype(BF16)
 
-    each(half, lambda j: after_scan(core * half + j), UNROLL)
-    each(half, lambda j: other_copy(j).wait())
-    each(half, lambda j: after_scan((1 - core) * half + j), UNROLL)
+    def mine_group(c):
+        slots = [near_first(c * group + i) for i in range(group)]
+        for slot in slots:
+            finish(slot)
+        for slot in slots:
+            after_scan(core * half + slot)
+
+    def other_group(c):
+        slots = [near_first(c * group + i) for i in range(group)]
+        for slot in slots:
+            other_copy(slot).wait()
+        for slot in slots:
+            after_scan((1 - core) * half + slot)
+
+    each(n_chip // group, mine_group)
+    each(n_chip // group, other_group)
 
     u = acc_x[...] + acc_s[...]
     last = jnp.sum(acc_s[...], axis=0, keepdims=True) + acc_a[0:1, :]
@@ -522,16 +615,24 @@
         return remote(dproj_ref, grads.at[core, dp], dp_send.at[k], dp_recv.at[k], near.dp_device(k))
 
     each(n_dp - 1, lambda k: dp_copy(k).start())
+
+    def grad_swap(i, slot):
+        block = grads.at[core, slot]
+        return remote(block, block, grad_send.at[i], grad_recv.at[i], near.sibling())
+
+    grads[core, dp] = dproj_ref[...]
+    grad_swap(n_dp - 1, dp).start()
     mixed_copy = pltpu.make_async_copy(mixed_grad_ref, mixed_out, out_sems.at[1])
     mixed_copy.start()
-    grads[core, dp] = dproj_ref[...]
+    dt_low = lanes_turned(dproj_ref[:, 2 * LANES :])
 
     def give(k):
-        cols = pl.ds(pl.multiple_of(k * w_rows, w_rows), w_rows)
-        sent = dot(dproj_ref[...], own_ref[k].reshape(w_rows, proj), NT)
-        input_grad_ref[:, cols] = (g_ref[:, cols].astype(F32) + sent).astype(BF16)
-
-    each(n_chip, give, 4)
+        for c in range(2):
+            cols = tile_at(2 * k + c)
+            sent = back_projected(dproj_ref, dt_low, own_ref, k, c, piece)
+            input_grad_ref[:, cols] = (g_ref[:, cols].astype(F32) + sent).astype(BF16)
+
+    each(n_chip, give, 2)
     input_copy = pltpu.make_async_copy(input_grad_ref, input_out, out_sems.at[2])
     input_copy.start()
 
@@ -544,12 +645,16 @@
     def add(c, k):
         whole[...] += dot(group_ref[k, c].reshape(-1, rows), grads[c, k])
 
-    each(n_dp - 1, lambda k: dp_copy(k).wait_recv())
-    grad_swap = remote(grads.at[core], grads.at[core], grad_sems.at[0], grad_sems.at[1], near.sibling())
-    grad_swap.start()
-    each(n_dp, lambda k: add(core, k), 2)
-    grad_swap.wait()
-    each(n_dp, lambda k: add(1 - core, k), 2)
+    def grad_slot(i):
+        return lax.rem(dp + 2 * n_dp - 1 - i, n_dp)
+
+    for i in range(n_dp - 1):
+        dp_copy(i).wait_recv()
+        grad_swap(i, grad_slot(i)).start()
+    each(n_dp, lambda i: add(core, i), 2)
+    for i in range(n_dp):
+        grad_swap(i, grad_slot(i)).wait()
+    each(n_dp, lambda i: add(1 - core, i), 2)
 
     def sum_copy(k):
         return remote(
@@ -558,17 +663,19 @@
 
     def ship(k):
         slot = near.chip_slot(k)
-        part[slot] = whole[pl.ds(pl.multiple_of(slot * piece, piece), piece), :].astype(BF16)
+        part[slot] = packed(whole[pl.ds(pl.multiple_of(slot * piece, piece), piece), :]).astype(BF16)
         sum_copy(k).start()
 
     each(n_chip - 1, ship)
-    weight_out[...] = whole[pl.ds(pl.multiple_of(chip * piece, piece), piece), :cols_w]
+    summed[...] = packed(whole[pl.ds(pl.multiple_of(chip * piece, piece), piece), :])
 
     @pl.when(pipe == 1)
     def _():
         shard_copy.wait_send()
         later_copy.wait_send()
 
+    gather.sent()
+    each(n_chip - 1, lambda k: chip_pass_copy(k).wait_send())
     each(n_chip - 1, lambda k: send_copy(k).wait_send())
 
     def sent_back(k):
@@ -581,9 +688,13 @@
 
     def collect(k):
         sum_copy(k).wait_recv()
-        weight_out[...] += arrived[k, :, :cols_w].astype(F32)
+        summed[...] += arrived[k].astype(F32)
 
     each(n_chip - 1, collect)
+    out_b, out_c, out_t = unpacked(summed[...], piece)
+    weight_out[:, :LANES] = out_b
+    weight_out[:, LANES : 2 * LANES] = out_c
+    weight_out[:, 2 * LANES :] = out_t[:, : cols_w - 2 * LANES]
     each(n_chip - 1, lambda k: sum_copy(k).wait_send())
     gate_copy.wait()
     mixed_copy.wait()
@@ -600,9 +711,9 @@
     line = jax.ShapeDtypeStruct((rows, width), BF16)
     whole_line = pltpu.VMEM((rows, width), BF16)
     square = pltpu.VMEM((rows, LANES), F32)
-    full_w = pltpu.VMEM((n_chip, 2, n_dp, piece, proj), BF16)
+    packed_rows = 2 * piece + piece // 2
+    full_w = pltpu.VMEM((n_chip, 2, n_dp, packed_rows, LANES), BF16)
     wide = pltpu.VMEM((pairs, rows, LANES), F32)
-    message = pltpu.VMEM((n_chip, state + 16, LANES), BF16)
     plain = pltpu.VMEM((n_chip, state, LANES), BF16)
     anywhere = pl.BlockSpec(memory_space=pl.ANY)
     chips, dps = dma((n_chip,)), dma((n_dp - 1,))
@@ -614,40 +725,44 @@
         scratch_shapes=[
             whole_line, whole_line, whole_line, whole_line,
             pltpu.VMEM((width, state), F32),
-            pltpu.VMEM((piece, proj), BF16),
+            pltpu.VMEM((packed_rows, LANES), BF16),
             full_w,
-            pltpu.VMEM((piece, proj), BF16),
+            pltpu.VMEM((packed_rows, LANES), BF16),
             full_w,
             pltpu.VMEM((rows, proj), BF16),
             pltpu.VMEM((pairs, state, LANES), BF16),
             pltpu.VMEM((n_chip, 2, LANES, rows), BF16),
             pltpu.VMEM((n_chip, LANES, rows), BF16),
             pltpu.VMEM((n_dp, 2, n_chip, piece, rows), BF16),
-            wide, wide, wide,
-            pltpu.VMEM((rows, proj), F32),
+            wide, wide,
+            pltpu.VMEM((rows, proj + LANES), F32),
         ]
         + [square] * 11
         + [
             pltpu.VMEM((24, LANES), F32),
-            pltpu.VMEM((pairs, state + 16, LANES), BF16),
-            pltpu.VMEM((2, n_chip, state + 16, LANES), BF16),
-            message, message, plain, plain, plain,
+            pltpu.VMEM((pairs, state, LANES), BF16),
+            pltpu.VMEM((2, n_chip, state, LANES), BF16),
+            plain, plain, plain, plain, plain,
             pltpu.VMEM((pairs, state, LANES), BF16),
             wide,
             pltpu.VMEM((rows, proj), BF16),
+            pltpu.VMEM((2, 8, LANES), F32),
+            pltpu.VMEM((n_chip, 8, LANES), F32),
             whole_line, whole_line, whole_line,
         ]
         + [square] * 6
         + [
             pltpu.VMEM((8, LANES), F32),
             pltpu.VMEM((2, n_dp, rows, proj), BF16),
-            pltpu.VMEM((n_chip, piece, proj), BF16),
+            pltpu.VMEM((n_chip, packed_rows, LANES), BF16),
             pltpu.VMEM((n_chip * piece, proj), F32),
-            pltpu.VMEM((n_chip - 1, piece, proj), BF16),
+            pltpu.VMEM((n_chip - 1, packed_rows, LANES), BF16),
+            pltpu.VMEM((piece, proj), F32),
+            pltpu.VMEM((packed_rows, LANES), F32),
             (
                 dma((5,)), dma((3,)), gather_sems(n_chip, n_dp), gather_sems(n_chip, n_dp), dma((2,)), dma((2,)),
-                chips, chips, chips, chips, chips, chips, chips, chips, dma((2,)),
-                dma((2, n_dp - 1)), dma((2, n_dp - 1)), dps, dps, dma((2,)), chips, chips,
+                dma((2,)), chips, chips, chips, chips, chips, chips, chips, chips, chips, chips, dma((2,)),
+                dma((2, n_dp - 1)), dma((2, n_dp - 1)), dps, dps, dma((n_dp,)), dma((n_dp,)), chips, chips,
             ),
         ],
         compiler_params=pltpu.CompilerParams(

time: 159 us -> 147 us (0.925)
  Pallas kernels: 159 us -> 147 us
    pallas_call x1, Pallas kernels: 154 us -> 142 us  [layer_grads(): pl.pallas_call(functools.partial(layer_kernel, n_chip, n_dp), out_shape=(...]
where the time goes in v4:
time: 147 us
  Pallas kernels  147 us (100%)
    pallas_call x1, Pallas kernels, layer_grads(): pl.pallas_call(functools.partial(layer_kernel, n_chip, n_dp), out_shape=(...  142 us
    pallas_call x1, Pallas kernels, deliver(): pl.pallas_call(deliver_kernel, grid=(steps,), out_shape=tuple((jax.ShapeD...  4.16 us

profile of v4, /device:TPU:1, one launch (start us, length us, event | category | flops | bytes accessed | tf_op | source)
XLA Modules:
  0.0 147.3 jit_solution(12173153069848006)
XLA Ops:
  0.6 142.5 %shard_map.129 = (bf16[128,4096]{1,0:T(8,128)(2,1)}, bf16[128,4096]{1,0:T(8,128)(2,1)}, bf16[128,4096]{1,0:T(8,128)(2,1)}, f32[32,320]{1,0:T(8,128)}) custom-call(bf16[32,320]{1,0:T(8,128)(2,1)} %bitcast.15, bf16[128,4096]{1,0:T(8,128)(2,1)} %bitcast.11, bf16[128,4096]{1,0:T(8,128)(2,1)} %bitcast.12, bf16[128,4096]{1,0:T(8,128)(2,1)} %bitcast.13, ...), custom_call_target="tpu_custom_call" | custom-call | tf_op jit(solution)/shard_map/pallas_call | solution.py:720
  143.1 4.2 %shard_map.130 = (bf16[128,4096]{1,0:T(8,128)(2,1)}, bf16[128,4096]{1,0:T(8,128)(2,1)}, bf16[128,4096]{1,0:T(8,128)(2,1)}, f32[32,320]{1,0:T(8,128)}) custom-call(bf16[128,4096]{1,0:T(8,128)(2,1)} %get-tuple-element.12.refs_0_, bf16[128,4096]{1,0:T(8,128)(2,1)} %get-tuple-element.13.refs_1_, bf16[128,4096]{1,0:T(8,128)(2,1)} %get-tuple-element.14.refs_2_, ...), custom_call_target="tpu_custom_call" | custom-call | tf_op jit(solution)/shard_map/pallas_call | solution.py:785

commit v5 on v4

--- a/solution.py
+++ b/solution.py
@@ -90,6 +90,9 @@
     def dp_device(self, k):
         return {"dp": self.dp_slot(k)}
 
+    def dp_at(self, way):
+        return {"dp": lax.rem(self.dp + way + self.n_dp, self.n_dp)}
+
     def sibling(self, k=0):
         return {"seg": self.seg + 1 - 2 * self.core}
 
@@ -104,7 +107,7 @@
 class Gather:
     def __init__(self, near, dst, sems):
         self.near, self.dst = near, dst
-        self.chip_send, self.chip_recv, self.dp_send, self.dp_recv, self.core_send, self.core_recv = sems
+        self.sends, self.chip_recv, self.side_recv, self.far_recv, self.core_recv = sems
 
     def source(self, k):
         near = self.near
@@ -113,72 +116,115 @@
     def chip_copy(self, k):
         near = self.near
         block = self.dst.at[near.chip, near.core, near.dp]
-        return remote(block, block, self.chip_send.at[k], self.chip_recv.at[k], near.chip_device(k))
-
-    def dp_copy(self, k, i):
+        return remote(block, block, self.sends.at[0], self.chip_recv.at[k], near.chip_device(k))
+
+    def side_copy(self, k, i):
         near = self.near
         block = self.dst.at[self.source(k), near.core, near.dp]
-        return remote(block, block, self.dp_send.at[k, i], self.dp_recv.at[k, i], near.dp_device(i))
+        return remote(block, block, self.sends.at[1], self.side_recv.at[k, i], near.dp_at(1 if i == 0 else -1))
+
+    def far_copy(self, k):
+        near = self.near
+        way = 1 - 2 * (k - k // 2 * 2)
+        block = self.dst.at[self.source(k), near.core, lax.rem(near.dp + near.n_dp - way, near.n_dp)]
+        return remote(block, block, self.sends.at[2], self.far_recv.at[k], near.dp_at(way))
 
     def core_copy(self, k):
         block = self.dst.at[self.source(k), self.near.core]
-        return remote(block, block, self.core_send.at[k], self.core_recv.at[k], self.near.sibling())
+        return remote(block, block, self.sends.at[3], self.core_recv.at[k], self.near.sibling())
+
+    def in_order(self, body):
+        count = self.near.n_chip
+        each(count, lambda step: body(lax.rem(step + count - 1, count)))
 
     def start(self, src):
         near = self.near
         self.dst[near.chip, near.core, near.dp] = src[...]
         each(near.n_chip - 1, lambda k: self.chip_copy(k).start())
-        each(near.n_dp - 1, lambda i: self.dp_copy(near.n_chip - 1, i).start())
+        for i in range(2):
+            self.side_copy(near.n_chip - 1, i).start()
 
     def spread(self):
-        near = self.near
-
         def pass_on(k):
             self.chip_copy(k).wait_recv()
-            for i in range(near.n_dp - 1):
-                self.dp_copy(k, i).start()
-
-        each(near.n_chip - 1, pass_on)
+            for i in range(2):
+                self.side_copy(k, i).start()
+
+        each(self.near.n_chip - 1, pass_on)
+
+        def further(k):
+            odd = k - k // 2 * 2
+            block = self.dst.at[0, 0, 0]
+            remote(block, block, self.sends.at[1], self.side_recv.at[k, odd], self.near.dp_at(1)).wait_recv()
+            self.far_copy(k).start()
+
+        self.in_order(further)
 
     def over(self, use):
-        near = self.near
-
-        def pass_on(step):
-            k = lax.rem(step + near.n_chip - 1, near.n_chip)
-            for i in range(near.n_dp - 1):
-                self.dp_copy(k, i).wait_recv()
+        def pass_on(k):
+            odd = k - k // 2 * 2
+            block = self.dst.at[0, 0, 0]
+            remote(block, block, self.sends.at[1], self.side_recv.at[k, 1 - odd], self.near.dp_at(1)).wait_recv()
+            self.far_copy(k).wait_recv()
             self.core_copy(k).start()
-            use(self.source(k), near.core)
-
-        each(near.n_chip, pass_on)
+            use(self.source(k), self.near.core)
+
+        self.in_order(pass_on)
 
     def end(self, use):
-        near = self.near
-
-        def take(step):
-            k = lax.rem(step + near.n_chip - 1, near.n_chip)
-            self.core_copy(k).wait()
-            use(self.source(k), 1 - near.core)
-
-        each(near.n_chip, take)
+        def take(k):
+            self.core_copy(k).wait_recv()
+            use(self.source(k), 1 - self.near.core)
+
+        self.in_order(take)
 
     def sent(self):
-        near = self.near
-        each(near.n_chip - 1, lambda k: self.chip_copy(k).wait_send())
-
-        def one(k):
-            for i in range(near.n_dp - 1):
-                self.dp_copy(k, i).wait_send()
-
-        each(near.n_chip, one)
+        near, dst = self.near, self.dst
+        regions = (
+            dst.at[pl.ds(0, near.n_chip - 1), near.core, near.dp],
+            dst.at[:, near.core, pl.ds(0, 2)],
+            dst.at[:, near.core, near.dp],
+            dst.at[:, near.core],
+        )
+        for i, region in enumerate(regions):
+            all_sent(region, self.sends.at[i], near)
 
 
 def gather_sems(n_chip, n_dp):
+    assert n_dp == 4
     dma = pltpu.SemaphoreType.DMA
-    return (
-        dma((n_chip - 1,)), dma((n_chip - 1,)), dma((n_chip, n_dp - 1)), dma((n_chip, n_dp - 1)),
-        dma((n_chip,)), dma((n_chip,)),
-    )
+    return (dma((4,)), dma((n_chip - 1,)), dma((n_chip, 2)), dma((n_chip,)), dma((n_chip,)))
+
+
+def all_sent(region, sem, near):
+    remote(region, region, sem, sem, near.sibling()).wait_send()
+
+
+def all_here(region, sem, near):
+    remote(region, region, sem, sem, near.sibling()).wait_recv()
+
+
+class LateGather:
+    def __init__(self, near, dst, sems):
+        self.near, self.dst, self.sems = near, dst, sems
+
+    def run(self, src):
+        near, dst, sems = self.near, self.dst, self.sems
+        dst[near.chip, near.core, near.dp] = src[...]
+        block = dst.at[near.chip, near.core, near.dp]
+        chips = dst.at[pl.ds(0, near.n_chip - 1), near.core, near.dp]
+        column = dst.at[:, near.core, near.dp]
+        columns = dst.at[:, near.core, pl.ds(0, near.n_dp - 1)]
+        side = dst.at[:, near.core]
+        each(near.n_chip - 1, lambda k: remote(block, block, sems.at[0], sems.at[1], near.chip_device(k)).start())
+        all_here(chips, sems.at[1], near)
+        each(near.n_dp - 1, lambda k: remote(column, column, sems.at[2], sems.at[3], near.dp_device(k)).start())
+        all_here(columns, sems.at[3], near)
+        last = remote(side, side, sems.at[4], sems.at[5], near.sibling())
+        last.start()
+        last.wait()
+        all_sent(chips, sems.at[0], near)
+        all_sent(columns, sems.at[2], near)
 
 
 def packed(value):
@@ -214,8 +260,8 @@
 
 def back_projected(dproj_ref, dt_low, ref, chip, core, piece):
     w_b, w_c, w_t = weight_tiles(ref, chip, core, piece)
-    plain = dot(dproj_ref[:, :LANES], w_b, NT) + dot(dproj_ref[:, LANES : 2 * LANES], w_c, NT)
-    top = dot(dproj_ref[:, 2 * LANES :], w_t, NT)
+    plain = dot(dproj_ref[1], w_b, NT) + dot(dproj_ref[0], w_c, NT)
+    top = dot(dproj_ref[2], w_t, NT)
     low = dot(dt_low, w_t, NT)
     return plain + jnp.where(in_top(piece), top, low)
 
@@ -252,9 +298,8 @@
         acc_scores, acc_b, acc_c, acc_y, acc_x, acc_s, acc_a, grads, part, whole, arrived, spare, summed, sems,
     ) = refs
     (
-        in_sems, out_sems, own_set, one_set, shard_sems, later_sems, pass_sems, pass_send, pass_recv, core_send, core_recv, send, recv,
-        back_send, back_recv, other_send, other_recv, xt_sems, xg_send, xg_recv,
-        dp_send, dp_recv, grad_send, grad_recv, sum_send, sum_recv,
+        in_sems, out_sems, own_set, one_set, shard_sems, later_sems, pass_sems, core_sems, core_recv,
+        send_sems, recv, back_recv, other_recv, xt_sems, xg_sems, dp_recv, grad_sems, grad_recv,
     ) = sems
     rows, width = x_ref.shape
     state = bf_ref.shape[1]
@@ -280,7 +325,13 @@
     near.greet(True)
     pipe, chip, core, dp = near.pipe, near.chip, near.core, near.dp
     shard_copy = remote(shard, one_shard, shard_sems.at[0], shard_sems.at[1], near.partner())
-    later_copy = remote(dproj_ref, later, later_sems.at[0], later_sems.at[1], near.partner())
+
+    def later_copy(i):
+        tiles = pl.ds(i, 1 + i)
+        return remote(
+            dproj_ref.at[tiles], later.at[tiles], later_sems.at[0, i], later_sems.at[1, i], near.partner()
+        )
+
 
     gather = Gather(near, own_ref, own_set)
     gather.start(shard)
@@ -322,9 +373,9 @@
         for c in range(2):
             xt_ref[k, c] = x_ref[:, tile_at(2 * k + c)].T
 
-    gather.spread()
     loads[0].wait()
     each(2 * half, activate, UNROLL)
+    gather.spread()
     loads[1].wait()
     each(2 * half, turn_state, UNROLL)
     loads[2].wait()
@@ -378,21 +429,17 @@
 
     def chip_pass_copy(k):
         block = chip_passes.at[chip]
-        return remote(block, block, pass_send.at[k], pass_recv.at[k], near.chip_device(k))
+        return remote(block, block, pass_sems.at[2], pass_sems.at[3], near.chip_device(k))
 
     each(n_chip - 1, lambda k: chip_pass_copy(k).start())
 
     @pl.when(pipe == 0)
     def _():
         shard_copy.wait_recv()
-        later_gather = Gather(near, one_ref, one_set)
-        later_gather.start(one_shard)
-        later_gather.spread()
-        later_gather.over(lambda k, c: None)
-        later_gather.end(lambda k, c: None)
-        later_gather.sent()
-        later_copy.wait_recv()
-        dt_low = lanes_turned(later[:, 2 * LANES :])
+        LateGather(near, one_ref, one_set).run(one_shard)
+        later_copy(0).wait_recv()
+        later_copy(1).wait_recv()
+        dt_low = lanes_turned(later[2])
 
         def recompute(k):
             for c in range(2):
@@ -410,10 +457,10 @@
         grad = (g_ref[:, tile_at(j)].astype(F32) * act_ref[j] * entry).astype(BF16)
         msg[j] = dot(ct, grad).astype(BF16)
 
-    def swap_copy(slot):
+    def swap_copy(c, slot):
         return remote(
             msg.at[(1 - core) * half + slot], both.at[core, slot],
-            core_send.at[slot], core_recv.at[slot], near.sibling(),
+            core_sems.at[0], core_recv.at[c], near.sibling(),
         )
 
     def combine(j):
@@ -423,7 +470,7 @@
 
     def send_copy(k):
         return remote(
-            total.at[near.chip_slot(k)], got.at[chip], send.at[k], recv.at[chip], near.chip_device(k)
+            total.at[near.chip_slot(k)], got.at[chip], send_sems.at[0], recv.at[chip], near.chip_device(k)
         )
 
     group = 4
@@ -433,11 +480,10 @@
         for slot in slots:
             own((1 - core) * half + slot)
         for slot in slots:
-            swap_copy(slot).start()
+            swap_copy(c, slot).start()
         for slot in slots:
             own(core * half + slot)
-        for slot in slots:
-            swap_copy(slot).wait()
+        all_here(both.at[core, pl.ds(0, group)], core_recv.at[c], near)
         for slot in slots:
             combine(slot)
         for i in range(group):
@@ -454,7 +500,7 @@
         cut = pl.ds(pl.multiple_of(near.dp_slot(k) * piece, piece), piece)
         return remote(
             src.at[:, cut], group_ref.at[dp, from_core],
-            xg_send.at[from_core, k], xg_recv.at[from_core, k], near.dp_device(k),
+            xg_sems.at[0], xg_sems.at[1], near.dp_device(k),
         )
 
     def x_start(k):
@@ -509,11 +555,11 @@
 
     each(half, before, UNROLL)
 
-    each(n_chip - 1, lambda k: chip_pass_copy(k).wait_recv())
+    all_here(chip_passes.at[pl.ds(0, n_chip - 1)], pass_sems.at[3], near)
 
     def back_copy(k):
         return remote(
-            back.at[k], exits.at[chip], back_send.at[k], back_recv.at[chip], {"seg": k * 2 + core}
+            back.at[k], exits.at[chip], send_sems.at[1], back_recv.at[chip], {"seg": k * 2 + core}
         )
 
     def scan(step, carry):
@@ -521,7 +567,7 @@
 
         @pl.when(k != chip)
         def _():
-            remote(got.at[k], got.at[k], send.at[0], recv.at[k], near.sibling()).wait_recv()
+            all_here(got.at[k], recv.at[k], near)
 
         back[k] = carry.astype(BF16)
 
@@ -534,25 +580,33 @@
     lax.fori_loop(0, n_chip, scan, jnp.zeros((state, LANES), F32))
     exits[chip] = back[chip]
     each(half, lambda j: before(half + j), UNROLL)
+    c_grad = acc_c[...] + dot(acc_scores[...], bf_ref[...], precision=HIGH)
+    dproj_ref[0] = c_grad.astype(BF16)
+    acc_b[...] += dot(acc_scores[...].T, cf_ref[...], precision=HIGH)
+
+    @pl.when(pipe == 1)
+    def _():
+        later_copy(0).start()
+
     gate_copy = pltpu.make_async_copy(gate_grad_ref, gate_out, out_sems.at[0])
     gate_copy.start()
 
-    def other_copy(j):
+    def other_copy(c, j):
         return remote(
-            other.at[j], adj_ref.at[core * half + j], other_send.at[j], other_recv.at[j], near.sibling()
+            other.at[j], adj_ref.at[core * half + j], core_sems.at[1], other_recv.at[c], near.sibling()
         )
 
-    def finish(j):
+    def finish(c, j):
         @pl.when(j != chip)
         def _():
-            remote(back.at[j], exits.at[j], back_send.at[0], back_recv.at[j], near.sibling()).wait_recv()
+            all_here(exits.at[j], back_recv.at[j], near)
 
         after = exits[j].astype(F32)
         earlier = both[1, j].astype(F32) + pass_row(passes[1], core * half + j) * after
         is_later = core == 1
         adj_ref[core * half + j] = jnp.where(is_later, after, earlier).astype(BF16)
         other[j] = jnp.where(is_later, earlier, after).astype(BF16)
-        other_copy(j).start()
+        other_copy(c, j).start()
 
     def near_first(i):
         x_off = i - i // 2 * 2
@@ -582,14 +636,13 @@
     def mine_group(c):
         slots = [near_first(c * group + i) for i in range(group)]
         for slot in slots:
-            finish(slot)
+            finish(c, slot)
         for slot in slots:
             after_scan(core * half + slot)
 
     def other_group(c):
         slots = [near_first(c * group + i) for i in range(group)]
-        for slot in slots:
-            other_copy(slot).wait()
+        all_here(other.at[pl.ds(0, group)], other_recv.at[c], near)
         for slot in slots:
             after_scan((1 - core) * half + slot)
 
@@ -601,30 +654,27 @@
     upper = (iota(0) <= iota(1)).astype(F32)
     log_grad = dot(upper, acc_y[...] - acc_s[...], precision=HIGH) + last
     raw_grad = u * rho_ref[...] - small[0:1, :] * log_grad * sig_ref[...]
-    b_grad = acc_b[...] + dot(acc_scores[...].T, cf_ref[...], precision=HIGH)
-    c_grad = acc_c[...] + dot(acc_scores[...], bf_ref[...], precision=HIGH)
-    dproj_ref[:, 0:LANES] = b_grad.astype(BF16)
-    dproj_ref[:, LANES : 2 * LANES] = c_grad.astype(BF16)
-    dproj_ref[:, 2 * LANES :] = raw_grad.astype(BF16)
+    dproj_ref[1] = acc_b[...].astype(BF16)
+    dproj_ref[2] = raw_grad.astype(BF16)
 
     @pl.when(pipe == 1)
     def _():
-        later_copy.start()
+        later_copy(1).start()
 
     def dp_copy(k):
-        return remote(dproj_ref, grads.at[core, dp], dp_send.at[k], dp_recv.at[k], near.dp_device(k))
+        return remote(dproj_ref, grads.at[core, dp], grad_sems.at[0], dp_recv.at[k], near.dp_device(k))
 
     each(n_dp - 1, lambda k: dp_copy(k).start())
 
     def grad_swap(i, slot):
         block = grads.at[core, slot]
-        return remote(block, block, grad_send.at[i], grad_recv.at[i], near.sibling())
+        return remote(block, block, grad_sems.at[1], grad_recv.at[i], near.sibling())
 
     grads[core, dp] = dproj_ref[...]
     grad_swap(n_dp - 1, dp).start()
     mixed_copy = pltpu.make_async_copy(mixed_grad_ref, mixed_out, out_sems.at[1])
     mixed_copy.start()
-    dt_low = lanes_turned(dproj_ref[:, 2 * LANES :])
+    dt_low = lanes_turned(dproj_ref[2])
 
     def give(k):
         for c in range(2):
@@ -636,14 +686,13 @@
     input_copy = pltpu.make_async_copy(input_grad_ref, input_out, out_sems.at[2])
     input_copy.start()
 
-    def x_wait(k):
-        x_copy(k, xt_ref.at[:, core], core).wait()
-        x_copy(k, x_stage, 1 - core).wait()
-
-    each(n_dp - 1, x_wait)
+    all_here(group_ref.at[pl.ds(0, n_dp - 1)], xg_sems.at[1], near)
 
     def add(c, k):
-        whole[...] += dot(group_ref[k, c].reshape(-1, rows), grads[c, k])
+        x = group_ref[k, c].reshape(-1, rows)
+        whole[:, :LANES] += dot(x, grads[c, k, 1])
+        whole[:, LANES : 2 * LANES] += dot(x, grads[c, k, 0])
+        whole[:, 2 * LANES :] += dot(x, grads[c, k, 2])
 
     def grad_slot(i):
         return lax.rem(dp + 2 * n_dp - 1 - i, n_dp)
@@ -653,12 +702,12 @@
         grad_swap(i, grad_slot(i)).start()
     each(n_dp, lambda i: add(core, i), 2)
     for i in range(n_dp):
-        grad_swap(i, grad_slot(i)).wait()
+        grad_swap(i, grad_slot(i)).wait_recv()
     each(n_dp, lambda i: add(1 - core, i), 2)
 
     def sum_copy(k):
         return remote(
-            part.at[near.chip_slot(k)], arrived.at[k], sum_send.at[k], sum_recv.at[k], near.chip_device(k)
+            part.at[near.chip_slot(k)], arrived.at[k], grad_sems.at[2], grad_sems.at[3], near.chip_device(k)
         )
 
     def ship(k):
@@ -672,30 +721,30 @@
     @pl.when(pipe == 1)
     def _():
         shard_copy.wait_send()
-        later_copy.wait_send()
+        later_copy(0).wait_send()
+        later_copy(1).wait_send()
 
     gather.sent()
-    each(n_chip - 1, lambda k: chip_pass_copy(k).wait_send())
-    each(n_chip - 1, lambda k: send_copy(k).wait_send())
-
-    def sent_back(k):
-        @pl.when(k != chip)
-        def _():
-            back_copy(k).wait_send()
-
-    each(n_chip, sent_back)
-    each(n_dp - 1, lambda k: dp_copy(k).wait_send())
+    first_chips = pl.ds(0, n_chip - 1)
+    all_sent(chip_passes.at[first_chips], pass_sems.at[2], near)
+    all_sent(both.at[core], core_sems.at[0], near)
+    all_sent(total.at[first_chips], send_sems.at[0], near)
+    all_sent(back.at[first_chips], send_sems.at[1], near)
+    all_sent(other, core_sems.at[1], near)
+    all_sent(group_ref.at[pl.ds(0, n_dp - 1)], xg_sems.at[0], near)
+    all_sent(grads.at[core, pl.ds(0, n_dp - 1)], grad_sems.at[0], near)
+    all_sent(grads.at[core], grad_sems.at[1], near)
 
     def collect(k):
-        sum_copy(k).wait_recv()
         summed[...] += arrived[k].astype(F32)
 
-    each(n_chip - 1, collect)
+    all_here(arrived, grad_sems.at[3], near)
+    each(n_chip - 1, collect, 5)
     out_b, out_c, out_t = unpacked(summed[...], piece)
     weight_out[:, :LANES] = out_b
     weight_out[:, LANES : 2 * LANES] = out_c
     weight_out[:, 2 * LANES :] = out_t[:, : cols_w - 2 * LANES]
-    each(n_chip - 1, lambda k: sum_copy(k).wait_send())
+    all_sent(arrived, grad_sems.at[2], near)
     gate_copy.wait()
     mixed_copy.wait()
     input_copy.wait()
@@ -714,9 +763,10 @@
     packed_rows = 2 * piece + piece // 2
     full_w = pltpu.VMEM((n_chip, 2, n_dp, packed_rows, LANES), BF16)
     wide = pltpu.VMEM((pairs, rows, LANES), F32)
+    tiles = pltpu.VMEM((proj // LANES, rows, LANES), BF16)
     plain = pltpu.VMEM((n_chip, state, LANES), BF16)
     anywhere = pl.BlockSpec(memory_space=pl.ANY)
-    chips, dps = dma((n_chip,)), dma((n_dp - 1,))
+    chips = dma((n_chip,))
     return pl.pallas_call(
         functools.partial(layer_kernel, n_chip, n_dp),
         out_shape=(line, line, line, jax.ShapeDtypeStruct((piece, cols), F32)),
@@ -729,7 +779,7 @@
             full_w,
             pltpu.VMEM((packed_rows, LANES), BF16),
             full_w,
-            pltpu.VMEM((rows, proj), BF16),
+            tiles,
             pltpu.VMEM((pairs, state, LANES), BF16),
             pltpu.VMEM((n_chip, 2, LANES, rows), BF16),
             pltpu.VMEM((n_chip, LANES, rows), BF16),
@@ -745,7 +795,7 @@
             plain, plain, plain, plain, plain,
             pltpu.VMEM((pairs, state, LANES), BF16),
             wide,
-            pltpu.VMEM((rows, proj), BF16),
+            tiles,
             pltpu.VMEM((2, 8, LANES), F32),
             pltpu.VMEM((n_chip, 8, LANES), F32),
             whole_line, whole_line, whole_line,
@@ -753,16 +803,16 @@
         + [square] * 6
         + [
             pltpu.VMEM((8, LANES), F32),
-            pltpu.VMEM((2, n_dp, rows, proj), BF16),
+            pltpu.VMEM((2, n_dp, proj // LANES, rows, LANES), BF16),
             pltpu.VMEM((n_chip, packed_rows, LANES), BF16),
             pltpu.VMEM((n_chip * piece, proj), F32),
             pltpu.VMEM((n_chip - 1, packed_rows, LANES), BF16),
             pltpu.VMEM((piece, proj), F32),
             pltpu.VMEM((packed_rows, LANES), F32),
             (
-                dma((5,)), dma((3,)), gather_sems(n_chip, n_dp), gather_sems(n_chip, n_dp), dma((2,)), dma((2,)),
-                dma((2,)), chips, chips, chips, chips, chips, chips, chips, chips, chips, chips, dma((2,)),
-                dma((2, n_dp - 1)), dma((2, n_dp - 1)), dps, dps, dma((n_dp,)), dma((n_dp,)), chips, chips,
+                dma((5,)), dma((3,)), gather_sems(n_chip, n_dp), dma((6,)), dma((2,)), dma((2, 2)), dma((4,)),
+                dma((2,)), dma((4,)), dma((2,)), chips, chips, dma((4,)), dma((2,)), dma((2,)),
+                dma((n_dp - 1,)), dma((4,)), dma((n_dp,)),
             ),
         ],
         compiler_params=pltpu.CompilerParams(
@@ -771,23 +821,37 @@
     )(shard, x, mixed, gate, out_grad, s0, rate, bias, skip, docs)
 
 
-def deliver_kernel(*refs):
-    count = len(refs) // 2
-    for i in range(count):
-        refs[count + i][...] = refs[i][...]
+def deliver_kernel(cuts, *refs):
+    count = len(cuts)
+    held, sems = refs[2 * count : 3 * count], refs[-1]
+    steps = []
+    for i, cut in enumerate(cuts):
+        size = held[i].shape[0] // cut
+        for k in range(cut):
+            rows = pl.ds(k * size, size)
+            at = len(steps)
+            load = pltpu.make_async_copy(refs[i].at[rows], held[i].at[rows], sems.at[0, at])
+            store = pltpu.make_async_copy(held[i].at[rows], refs[count + i].at[rows], sems.at[1, at])
+            steps.append((load, store))
+    for load, _ in steps:
+        load.start()
+    for load, store in steps:
+        load.wait()
+        store.start()
+    for _, store in steps:
+        store.wait()
 
 
 def deliver(values):
-    steps = 4
-    specs = [
-        pl.BlockSpec((value.shape[0] // steps, value.shape[1]), lambda i: (i, 0)) for value in values
-    ]
+    anywhere = pl.BlockSpec(memory_space=pl.ANY)
+    cuts = [2 if value.dtype == BF16 else 1 for value in values]
     return pl.pallas_call(
-        deliver_kernel,
-        grid=(steps,),
+        functools.partial(deliver_kernel, cuts),
         out_shape=tuple(jax.ShapeDtypeStruct(value.shape, value.dtype) for value in values),
-        in_specs=specs,
-        out_specs=tuple(specs),
+        in_specs=[anywhere] * len(values),
+        out_specs=(anywhere,) * len(values),
+        scratch_shapes=[pltpu.VMEM(value.shape, value.dtype) for value in values]
+        + [pltpu.SemaphoreType.DMA((2, sum(cuts)))],
     )(*values)
 
 

time: 147 us -> 144 us (0.980)
  Pallas kernels: 147 us -> 143 us
    pallas_call x1, Pallas kernels: 142 us -> 140 us  [layer_grads(): pl.pallas_call(functools.partial(layer_kernel, n_chip, n_dp), out_shape=(...]
where the time goes in v5:
time: 144 us
  Pallas kernels  143 us (99%)
    pallas_call x1, Pallas kernels, layer_grads(): pl.pallas_call(functools.partial(layer_kernel, n_chip, n_dp), out_shape=(...  140 us

profile of v5, /device:TPU:1, one launch (start us, length us, event | category | flops | bytes accessed | tf_op | source)
XLA Modules:
  0.0 143.6 jit_solution(12587643524056406936)
XLA Ops:
  0.6 140.1 %shard_map.129 = (bf16[128,4096]{1,0:T(8,128)(2,1)}, bf16[128,4096]{1,0:T(8,128)(2,1)}, bf16[128,4096]{1,0:T(8,128)(2,1)}, f32[32,320]{1,0:T(8,128)}) custom-call(bf16[32,320]{1,0:T(8,128)(2,1)} %bitcast.15, bf16[128,4096]{1,0:T(8,128)(2,1)} %bitcast.11, bf16[128,4096]{1,0:T(8,128)(2,1)} %bitcast.12, bf16[128,4096]{1,0:T(8,128)(2,1)} %bitcast.13, ...), custom_call_target="tpu_custom_call" | custom-call | tf_op jit(solution)/shard_map/pallas_call | solution.py:770
  140.8 2.8 %shard_map.130 = (bf16[128,4096]{1,0:T(8,128)(2,1)}, bf16[128,4096]{1,0:T(8,128)(2,1)}, bf16[128,4096]{1,0:T(8,128)(2,1)}, f32[32,320]{1,0:T(8,128)}) custom-call(bf16[128,4096]{1,0:T(8,128)(2,1)} %get-tuple-element.12.refs_0_, bf16[128,4096]{1,0:T(8,128)(2,1)} %get-tuple-element.13.refs_1_, bf16[128,4096]{1,0:T(8,128)(2,1)} %get-tuple-element.14.refs_2_, ...), custom_call_target="tpu_custom_call" | custom-call | tf_op jit(solution)/shard_map/pallas_call | solution.py:848

commit v6 on v5

--- a/solution.py
+++ b/solution.py
@@ -14,6 +14,7 @@
 LANES = 128
 NEG = -1e30
 UNROLL = 4
+GROUP = 4
 VMEM_BYTES = 56 * 1024 * 1024
 VMEM = pl.BlockSpec(memory_space=pltpu.VMEM)
 SMEM = pl.BlockSpec(memory_space=pltpu.SMEM)
@@ -129,13 +130,12 @@
         block = self.dst.at[self.source(k), near.core, lax.rem(near.dp + near.n_dp - way, near.n_dp)]
         return remote(block, block, self.sends.at[2], self.far_recv.at[k], near.dp_at(way))
 
-    def core_copy(self, k):
+    def core_copy(self, c, k):
         block = self.dst.at[self.source(k), self.near.core]
-        return remote(block, block, self.sends.at[3], self.core_recv.at[k], self.near.sibling())
-
-    def in_order(self, body):
-        count = self.near.n_chip
-        each(count, lambda step: body(lax.rem(step + count - 1, count)))
+        return remote(block, block, self.sends.at[3], self.core_recv.at[c], self.near.sibling())
+
+    def turn(self, step):
+        return lax.rem(step + self.near.n_chip - 1, self.near.n_chip)
 
     def start(self, src):
         near = self.near
@@ -158,25 +158,27 @@
             remote(block, block, self.sends.at[1], self.side_recv.at[k, odd], self.near.dp_at(1)).wait_recv()
             self.far_copy(k).start()
 
-        self.in_order(further)
+        each(self.near.n_chip, lambda step: further(self.turn(step)))
 
     def over(self, use):
-        def pass_on(k):
-            odd = k - k // 2 * 2
+        def pass_on(c):
+            turns = [self.turn(c * GROUP + i) for i in range(GROUP)]
             block = self.dst.at[0, 0, 0]
-            remote(block, block, self.sends.at[1], self.side_recv.at[k, 1 - odd], self.near.dp_at(1)).wait_recv()
-            self.far_copy(k).wait_recv()
-            self.core_copy(k).start()
-            use(self.source(k), self.near.core)
-
-        self.in_order(pass_on)
+            for k in turns:
+                odd = k - k // 2 * 2
+                all_here(block, self.side_recv.at[k, 1 - odd], self.near)
+                all_here(block, self.far_recv.at[k], self.near)
+                self.core_copy(c, k).start()
+            use([self.source(k) for k in turns], self.near.core)
+
+        each(self.near.n_chip // GROUP, pass_on)
 
     def end(self, use):
-        def take(k):
-            self.core_copy(k).wait_recv()
-            use(self.source(k), 1 - self.near.core)
-
-        self.in_order(take)
+        def take(c):
+            all_here(self.dst.at[pl.ds(0, GROUP), self.near.core], self.core_recv.at[c], self.near)
+            use([self.source(self.turn(c * GROUP + i)) for i in range(GROUP)], 1 - self.near.core)
+
+        each(self.near.n_chip // GROUP, take)
 
     def sent(self):
         near, dst = self.near, self.dst
@@ -193,7 +195,7 @@
 def gather_sems(n_chip, n_dp):
     assert n_dp == 4
     dma = pltpu.SemaphoreType.DMA
-    return (dma((4,)), dma((n_chip - 1,)), dma((n_chip, 2)), dma((n_chip,)), dma((n_chip,)))
+    return (dma((4,)), dma((n_chip - 1,)), dma((n_chip, 2)), dma((n_chip,)), dma((n_chip // GROUP,)))
 
 
 def all_sent(region, sem, near):
@@ -227,20 +229,21 @@
         all_sent(columns, sems.at[2], near)
 
 
+def beside(tail):
+    half = tail.shape[0] // 2
+    return tail[:half] + pltpu.roll(tail[half:], LANES // 2, 1)
+
+
+def below(value):
+    first = iota(1, (1, LANES)) < LANES // 2
+    top = jnp.where(first, value, 0.0)
+    low = jnp.where(first, pltpu.roll(value, LANES // 2, 1), 0.0)
+    return jnp.concatenate([top, low], axis=0)
+
+
 def packed(value):
-    piece = value.shape[0]
-    tail = value[:, 2 * LANES :]
-    top, low = tail[: piece // 2], tail[piece // 2 :]
-    beside = top + pltpu.roll(low, LANES // 2, 1)
-    return jnp.concatenate([value[:, :LANES], value[:, LANES : 2 * LANES], beside], axis=0)
-
-
-def unpacked(value, piece):
-    beside = value[2 * piece :]
-    first = iota(1, (1, LANES)) < LANES // 2
-    top = jnp.where(first, beside, 0.0)
-    low = jnp.where(first, pltpu.roll(beside, LANES // 2, 1), 0.0)
-    return value[:piece], value[piece : 2 * piece], jnp.concatenate([top, low], axis=0)
+    tail = beside(value[:, 2 * LANES :])
+    return jnp.concatenate([value[:, :LANES], value[:, LANES : 2 * LANES], tail], axis=0)
 
 
 def weight_tiles(ref, chip, core, piece):
@@ -295,7 +298,7 @@
         log_ref, logt_ref, dt_ref, dtt_ref, sig_ref, rho_ref, mask_ref, first_ref, kept_ref, small,
         msg, both, total, got, back, exits, other, adj_ref, base, dproj_ref, passes, chip_passes,
         input_grad_ref, mixed_grad_ref, gate_grad_ref,
-        acc_scores, acc_b, acc_c, acc_y, acc_x, acc_s, acc_a, grads, part, whole, arrived, spare, summed, sems,
+        acc_scores, acc_b, acc_c, acc_y, acc_x, acc_s, acc_a, grads, part_c, part_o, whole, arrived_c, arrived_o, spare, sems,
     ) = refs
     (
         in_sems, out_sems, own_set, one_set, shard_sems, later_sems, pass_sems, core_sems, core_recv,
@@ -340,7 +343,7 @@
     def _():
         shard_copy.start()
 
-    for ref in (acc_scores, acc_b, acc_c, acc_y, acc_x, acc_s, acc_a, small, projected, whole):
+    for ref in (acc_scores, acc_b, acc_c, acc_y, acc_x, acc_s, acc_a, small, projected):
         ref[...] = jnp.zeros_like(ref)
     small[0:1, :heads] = rate_ref[...]
     small[8:9, :heads] = bias_ref[...]
@@ -381,14 +384,23 @@
     loads[2].wait()
     each(n_chip, turn_x, 2)
 
-    def project(k, c):
-        x_tile = x_ref[:, tile_at(2 * k + c)]
-        zero = jnp.zeros_like(x_tile)
-        w_b, w_c, w_t = weight_tiles(own_ref, k, c, piece)
-        projected[:, :LANES] += dot(x_tile, w_b)
-        projected[:, LANES : 2 * LANES] += dot(x_tile, w_c)
-        projected[:, 2 * LANES : 3 * LANES] += dot(jnp.where(in_top(piece), x_tile, zero), w_t)
-        projected[:, 3 * LANES :] += dot(jnp.where(in_top(piece), zero, x_tile), w_t)
+    def project(chips, c):
+        top = in_top(piece)
+        x_tiles = [x_ref[:, tile_at(2 * k + c)] for k in chips]
+        zero = jnp.zeros_like(x_tiles[0])
+        w_b, w_c, w_t = [
+            jnp.concatenate(column, axis=0)
+            for column in zip(*[weight_tiles(own_ref, k, c, piece) for k in chips])
+        ]
+
+        def lined(tiles):
+            return jnp.concatenate(tiles, axis=1)
+
+        x_all = lined(x_tiles)
+        projected[:, :LANES] += dot(x_all, w_b)
+        projected[:, LANES : 2 * LANES] += dot(x_all, w_c)
+        projected[:, 2 * LANES : 3 * LANES] += dot(lined([jnp.where(top, x, zero) for x in x_tiles]), w_t)
+        projected[:, 3 * LANES :] += dot(lined([jnp.where(top, zero, x) for x in x_tiles]), w_t)
 
     gather.over(project)
     gather.end(project)
@@ -473,25 +485,36 @@
             total.at[near.chip_slot(k)], got.at[chip], send_sems.at[0], recv.at[chip], near.chip_device(k)
         )
 
-    group = 4
-
-    def own_group(c):
-        slots = [near.chip_slot(c * group + i) for i in range(group)]
+    group = GROUP
+    couple = 2
+
+    def couple_slots(c):
+        return [near.chip_slot(c * couple + i) for i in range(couple)]
+
+    def own_theirs(c):
+        slots = couple_slots(c)
         for slot in slots:
             own((1 - core) * half + slot)
         for slot in slots:
             swap_copy(c, slot).start()
+
+    def own_mine(c, send_count):
+        slots = couple_slots(c)
         for slot in slots:
             own(core * half + slot)
-        all_here(both.at[core, pl.ds(0, group)], core_recv.at[c], near)
+        all_here(both.at[core, pl.ds(0, couple)], core_recv.at[c], near)
         for slot in slots:
             combine(slot)
-        for i in range(group):
-            @pl.when(c * group + i < n_chip - 1)
-            def _(i=i):
-                send_copy(c * group + i).start()
-
-    each(n_chip // group, own_group)
+        for i in range(send_count):
+            send_copy(c * couple + i).start()
+
+    def own_step(c):
+        own_theirs(c + 1)
+        own_mine(c, couple)
+
+    own_theirs(0)
+    each(n_chip // couple - 1, own_step)
+    own_mine(n_chip // couple - 1, couple - 1)
     got[chip] = total[chip]
 
     xt_copy.wait()
@@ -588,6 +611,25 @@
     def _():
         later_copy(0).start()
 
+    def tiles_of(i):
+        return pl.ds(i, 1 + i)
+
+    def dp_copy(i, k):
+        return remote(
+            dproj_ref.at[tiles_of(i)], grads.at[core, dp, tiles_of(i)],
+            grad_sems.at[0, i], dp_recv.at[i, k], near.dp_device(k),
+        )
+
+    def grad_swap(i, slot):
+        block = grads.at[core, slot, tiles_of(i)]
+        return remote(block, block, grad_sems.at[1, i], grad_recv.at[i], near.sibling())
+
+    def share(i):
+        each(n_dp - 1, lambda k: dp_copy(i, k).start())
+        grads[core, dp, tiles_of(i)] = dproj_ref[tiles_of(i)]
+        grad_swap(i, dp).start()
+
+    share(0)
     gate_copy = pltpu.make_async_copy(gate_grad_ref, gate_out, out_sems.at[0])
     gate_copy.start()
 
@@ -618,33 +660,37 @@
         z = lax.rem(chip - my_x * ring + z_off + ring, ring)
         return lax.rem(my_x + x_off, 2) * ring + z
 
-    def after_scan(j):
-        cols = tile_at(j)
-        adj = adj_ref[j]
-        weight = weights[j]
-        x_f = xs_ref[:, cols].astype(F32)
+    def after_scan(pairs):
+        def lined(tiles):
+            return jnp.concatenate(tiles, axis=1)
+
+        adj = lined([adj_ref[j] for j in pairs])
+        weight = lined([weights[j] for j in pairs])
+        x_f = lined([xs_ref[:, tile_at(j)] for j in pairs]).astype(F32)
         outer = weight * dot(b_low, adj)
         acc_b[...] += dot((x_f * weight).astype(BF16), adj, NT)
-        acc_s[...] += heads_of(x_f * outer, j)
-        last = pass_row(passes[core], j)
-        passed = last * jnp.sum(adj.astype(F32) * s0t_ref[j].astype(F32), axis=0, keepdims=True)
-        select = (iota(1) == 2 * j + (iota(0) >= LANES // 2).astype(jnp.int32)).astype(BF16)
-        high, low = split_two(jnp.broadcast_to(passed, (8, LANES)))
+        lane, row = iota(1), (iota(0) >= LANES // 2).astype(jnp.int32)
+        select = jnp.concatenate([(lane == 2 * j + row).astype(BF16) for j in pairs], axis=0)
+        high, low = split_two(x_f * outer)
+        acc_s[...] += dot(high, select) + dot(low, select)
+        last = lined([pass_row(passes[core], j) for j in pairs])
+        s0t = lined([s0t_ref[j] for j in pairs])
+        passed = last * jnp.sum(adj.astype(F32) * s0t.astype(F32), axis=0, keepdims=True)
+        high, low = split_two(jnp.broadcast_to(passed, (8, passed.shape[1])))
         acc_a[...] += dot(high, select) + dot(low, select)
-        mixed_grad_ref[:, cols] = (base[j] + outer).astype(BF16)
+        for i, j in enumerate(pairs):
+            mixed_grad_ref[:, tile_at(j)] = (base[j] + outer[:, i * LANES : (i + 1) * LANES]).astype(BF16)
 
     def mine_group(c):
         slots = [near_first(c * group + i) for i in range(group)]
         for slot in slots:
             finish(c, slot)
-        for slot in slots:
-            after_scan(core * half + slot)
+        after_scan([core * half + slot for slot in slots])
 
     def other_group(c):
         slots = [near_first(c * group + i) for i in range(group)]
         all_here(other.at[pl.ds(0, group)], other_recv.at[c], near)
-        for slot in slots:
-            after_scan((1 - core) * half + slot)
+        after_scan([(1 - core) * half + slot for slot in slots])
 
     each(n_chip // group, mine_group)
     each(n_chip // group, other_group)
@@ -661,19 +707,53 @@
     def _():
         later_copy(1).start()
 
-    def dp_copy(k):
-        return remote(dproj_ref, grads.at[core, dp], grad_sems.at[0], dp_recv.at[k], near.dp_device(k))
-
-    each(n_dp - 1, lambda k: dp_copy(k).start())
-
-    def grad_swap(i, slot):
-        block = grads.at[core, slot]
-        return remote(block, block, grad_sems.at[1], grad_recv.at[i], near.sibling())
-
-    grads[core, dp] = dproj_ref[...]
-    grad_swap(n_dp - 1, dp).start()
+    share(1)
     mixed_copy = pltpu.make_async_copy(mixed_grad_ref, mixed_out, out_sems.at[1])
     mixed_copy.start()
+    all_here(group_ref.at[pl.ds(0, n_dp - 1)], xg_sems.at[1], near)
+
+    def gathered(i):
+        for k in range(n_dp - 1):
+            dp_copy(i, k).wait_recv()
+            grad_swap(i, lax.rem(dp + 2 * n_dp - 1 - k, n_dp)).start()
+
+    def summed_over(c, tile):
+        x = jnp.concatenate([group_ref[k, c].reshape(-1, rows) for k in range(n_dp)], axis=1)
+        return dot(x, jnp.concatenate([grads[c, k, tile] for k in range(n_dp)], axis=0))
+
+    def whole_tiles(i):
+        for tile in range(i, 1 + 2 * i):
+            whole[tile] = summed_over(core, tile)
+        all_here(grads.at[1 - core, :, tiles_of(i)], grad_recv.at[i], near)
+        for tile in range(i, 1 + 2 * i):
+            whole[tile] += summed_over(1 - core, tile)
+
+    def rows_of(slot):
+        return pl.ds(pl.multiple_of(slot * piece, piece), piece)
+
+    def c_rows(slot):
+        return whole[0, rows_of(slot)]
+
+    def other_rows(slot):
+        return jnp.concatenate([whole[1, rows_of(slot)], beside(whole[2, rows_of(slot)])], axis=0)
+
+    def sum_copy(i, k, part, arrived):
+        return remote(
+            part.at[near.chip_slot(k)], arrived.at[k], grad_sems.at[2, i], grad_sems.at[3, i],
+            near.chip_device(k),
+        )
+
+    def ship(i, rows_at, part, arrived):
+        def one(k):
+            slot = near.chip_slot(k)
+            part[slot] = rows_at(slot).astype(BF16)
+            sum_copy(i, k, part, arrived).start()
+
+        each(n_chip - 1, one)
+
+    gathered(0)
+    whole_tiles(0)
+    ship(0, c_rows, part_c, arrived_c)
     dt_low = lanes_turned(dproj_ref[2])
 
     def give(k):
@@ -686,37 +766,9 @@
     input_copy = pltpu.make_async_copy(input_grad_ref, input_out, out_sems.at[2])
     input_copy.start()
 
-    all_here(group_ref.at[pl.ds(0, n_dp - 1)], xg_sems.at[1], near)
-
-    def add(c, k):
-        x = group_ref[k, c].reshape(-1, rows)
-        whole[:, :LANES] += dot(x, grads[c, k, 1])
-        whole[:, LANES : 2 * LANES] += dot(x, grads[c, k, 0])
-        whole[:, 2 * LANES :] += dot(x, grads[c, k, 2])
-
-    def grad_slot(i):
-        return lax.rem(dp + 2 * n_dp - 1 - i, n_dp)
-
-    for i in range(n_dp - 1):
-        dp_copy(i).wait_recv()
-        grad_swap(i, grad_slot(i)).start()
-    each(n_dp, lambda i: add(core, i), 2)
-    for i in range(n_dp):
-        grad_swap(i, grad_slot(i)).wait_recv()
-    each(n_dp, lambda i: add(1 - core, i), 2)
-
-    def sum_copy(k):
-        return remote(
-            part.at[near.chip_slot(k)], arrived.at[k], grad_sems.at[2], grad_sems.at[3], near.chip_device(k)
-        )
-
-    def ship(k):
-        slot = near.chip_slot(k)
-        part[slot] = packed(whole[pl.ds(pl.multiple_of(slot * piece, piece), piece), :]).astype(BF16)
-        sum_copy(k).start()
-
-    each(n_chip - 1, ship)
-    summed[...] = packed(whole[pl.ds(pl.multiple_of(chip * piece, piece), piece), :])
+    gathered(1)
+    whole_tiles(1)
+    ship(1, other_rows, part_o, arrived_o)
 
     @pl.when(pipe == 1)
     def _():
@@ -732,19 +784,23 @@
     all_sent(back.at[first_chips], send_sems.at[1], near)
     all_sent(other, core_sems.at[1], near)
     all_sent(group_ref.at[pl.ds(0, n_dp - 1)], xg_sems.at[0], near)
-    all_sent(grads.at[core, pl.ds(0, n_dp - 1)], grad_sems.at[0], near)
-    all_sent(grads.at[core], grad_sems.at[1], near)
-
-    def collect(k):
-        summed[...] += arrived[k].astype(F32)
-
-    all_here(arrived, grad_sems.at[3], near)
-    each(n_chip - 1, collect, 5)
-    out_b, out_c, out_t = unpacked(summed[...], piece)
-    weight_out[:, :LANES] = out_b
-    weight_out[:, LANES : 2 * LANES] = out_c
-    weight_out[:, 2 * LANES :] = out_t[:, : cols_w - 2 * LANES]
-    all_sent(arrived, grad_sems.at[2], near)
+    for i in range(2):
+        all_sent(grads.at[core, pl.ds(0, n_dp - 1), tiles_of(i)], grad_sems.at[0, i], near)
+        all_sent(grads.at[core, :, tiles_of(i)], grad_sems.at[1, i], near)
+
+    def collected(i, rows_at, arrived):
+        all_here(arrived, grad_sems.at[3, i], near)
+        total_rows = rows_at(chip)
+        for k in range(n_chip - 1):
+            total_rows += arrived[k].astype(F32)
+        return total_rows
+
+    weight_out[:, LANES : 2 * LANES] = collected(0, c_rows, arrived_c)
+    others = collected(1, other_rows, arrived_o)
+    weight_out[:, :LANES] = others[:piece]
+    weight_out[:, 2 * LANES :] = below(others[piece:])[:, : cols_w - 2 * LANES]
+    all_sent(arrived_c, grad_sems.at[2, 0], near)
+    all_sent(arrived_o, grad_sems.at[2, 1], near)
     gate_copy.wait()
     mixed_copy.wait()
     input_copy.wait()
@@ -804,15 +860,16 @@
         + [
             pltpu.VMEM((8, LANES), F32),
             pltpu.VMEM((2, n_dp, proj // LANES, rows, LANES), BF16),
-            pltpu.VMEM((n_chip, packed_rows, LANES), BF16),
-            pltpu.VMEM((n_chip * piece, proj), F32),
-            pltpu.VMEM((n_chip - 1, packed_rows, LANES), BF16),
+            pltpu.VMEM((n_chip, piece, LANES), BF16),
+            pltpu.VMEM((n_chip, packed_rows - piece, LANES), BF16),
+            pltpu.VMEM((proj // LANES, n_chip * piece, LANES), F32),
+            pltpu.VMEM((n_chip - 1, piece, LANES), BF16),
+            pltpu.VMEM((n_chip - 1, packed_rows - piece, LANES), BF16),
             pltpu.VMEM((piece, proj), F32),
-            pltpu.VMEM((packed_rows, LANES), F32),
             (
                 dma((5,)), dma((3,)), gather_sems(n_chip, n_dp), dma((6,)), dma((2,)), dma((2, 2)), dma((4,)),
-                dma((2,)), dma((4,)), dma((2,)), chips, chips, dma((4,)), dma((2,)), dma((2,)),
-                dma((n_dp - 1,)), dma((4,)), dma((n_dp,)),
+                dma((2,)), dma((n_chip // 2,)), dma((2,)), chips, chips, dma((n_chip // GROUP,)), dma((2,)),
+                dma((2,)), dma((2, n_dp - 1)), dma((4, 2)), dma((2,)),
             ),
         ],
         compiler_params=pltpu.CompilerParams(

time: 144 us -> 132 us (0.917)
  Pallas kernels: 143 us -> 132 us
    pallas_call x1, Pallas kernels: 140 us -> 129 us  [layer_grads(): pl.pallas_call(functools.partial(layer_kernel, n_chip, n_dp), out_shape=(...]
where the time goes in v6:
time: 132 us
  Pallas kernels  132 us (100%)
    pallas_call x1, Pallas kernels, layer_grads(): pl.pallas_call(functools.partial(layer_kernel, n_chip, n_dp), out_shape=(...  129 us
    pallas_call x1, Pallas kernels, deliver(): pl.pallas_call(functools.partial(deliver_kernel, cuts), out_shape=tuple((...  2.82 us

profile of v6, /device:TPU:1, one launch (start us, length us, event | category | flops | bytes accessed | tf_op | source)
XLA Modules:
  0.0 132.2 jit_solution(16808352979533033618)
XLA Ops:
  0.6 128.8 %shard_map.129 = (bf16[128,4096]{1,0:T(8,128)(2,1)}, bf16[128,4096]{1,0:T(8,128)(2,1)}, bf16[128,4096]{1,0:T(8,128)(2,1)}, f32[32,320]{1,0:T(8,128)}) custom-call(bf16[32,320]{1,0:T(8,128)(2,1)} %bitcast.15, bf16[128,4096]{1,0:T(8,128)(2,1)} %bitcast.11, bf16[128,4096]{1,0:T(8,128)(2,1)} %bitcast.12, bf16[128,4096]{1,0:T(8,128)(2,1)} %bitcast.13, ...), custom_call_target="tpu_custom_call" | custom-call | tf_op jit(solution)/shard_map/pallas_call | solution.py:826
  129.4 2.8 %shard_map.130 = (bf16[128,4096]{1,0:T(8,128)(2,1)}, bf16[128,4096]{1,0:T(8,128)(2,1)}, bf16[128,4096]{1,0:T(8,128)(2,1)}, f32[32,320]{1,0:T(8,128)}) custom-call(bf16[128,4096]{1,0:T(8,128)(2,1)} %get-tuple-element.12.refs_0_, bf16[128,4096]{1,0:T(8,128)(2,1)} %get-tuple-element.13.refs_1_, bf16[128,4096]{1,0:T(8,128)(2,1)} %get-tuple-element.14.refs_2_, ...), custom_call_target="tpu_custom_call" | custom-call | tf_op jit(solution)/shard_map/pallas_call | solution.py:905

commit v7 on v6

--- a/solution.py
+++ b/solution.py
@@ -51,12 +51,9 @@
 def greet(devices):
     barrier = pltpu.get_barrier_semaphore()
     for count, device_of in devices:
-        def one(k, carry, device_of=device_of):
+        for k in range(count):
             pl.semaphore_signal(barrier, inc=1, device_id=device_of(k), device_id_type=MESH)
-            return carry
-
-        lax.fori_loop(0, count, one, 0)
-    pl.semaphore_wait(barrier, sum(count for count, _ in devices))
+    return lambda: pl.semaphore_wait(barrier, sum(count for count, _ in devices))
 
 
 def remote(src, dst, send_sem, recv_sem, device):
@@ -100,9 +97,10 @@
     def partner(self, k=0):
         return {"pipe": 1 - self.pipe}
 
-    def greet(self, with_pipe):
-        met = [(self.n_chip - 1, self.chip_device), (self.n_dp - 1, self.dp_device), (1, self.sibling)]
-        greet(met + ([(1, self.partner)] if with_pipe else []))
+    def greet(self):
+        return greet(
+            [(self.n_chip - 1, self.chip_device), (self.n_dp - 1, self.dp_device), (1, self.sibling), (1, self.partner)]
+        )
 
 
 class Gather:
@@ -302,7 +300,7 @@
     ) = refs
     (
         in_sems, out_sems, own_set, one_set, shard_sems, later_sems, pass_sems, core_sems, core_recv,
-        send_sems, recv, back_recv, other_recv, xt_sems, xg_sems, dp_recv, grad_sems, grad_recv,
+        send_sems, recv, back_recv, other_recv, xt_sems, xg_sems, dp_recv, grad_sems, grad_recv, sum_sems,
     ) = sems
     rows, width = x_ref.shape
     state = bf_ref.shape[1]
@@ -312,6 +310,9 @@
     proj = projected.shape[1]
     half = n_chip
 
+    near = Around(n_chip, n_dp)
+    pipe, chip, core, dp = near.pipe, near.chip, near.core, near.dp
+    all_met = near.greet()
     loads = [
         pltpu.make_async_copy(src, dst, in_sems.at[i])
         for i, (src, dst) in enumerate(
@@ -324,15 +325,12 @@
     spare[:, :cols_w] = shard_ref[...].astype(F32)
     shard[...] = packed(spare[...]).astype(BF16)
 
-    near = Around(n_chip, n_dp)
-    near.greet(True)
-    pipe, chip, core, dp = near.pipe, near.chip, near.core, near.dp
+    all_met()
     shard_copy = remote(shard, one_shard, shard_sems.at[0], shard_sems.at[1], near.partner())
 
     def later_copy(i):
-        tiles = pl.ds(i, 1 + i)
         return remote(
-            dproj_ref.at[tiles], later.at[tiles], later_sems.at[0, i], later_sems.at[1, i], near.partner()
+            dproj_ref.at[i], later.at[i], later_sems.at[0, i], later_sems.at[1, i], near.partner()
         )
 
 
@@ -450,14 +448,25 @@
         shard_copy.wait_recv()
         LateGather(near, one_ref, one_set).run(one_shard)
         later_copy(0).wait_recv()
+
+        def first_part(k):
+            for c in range(2):
+                j = 2 * k + c
+                w_c = one_ref[k, c, :, piece : 2 * piece].reshape(-1, LANES)
+                base[j] = g_ref[:, tile_at(j)].astype(F32) + dot(later[0], w_c, NT)
+
+        each(n_chip, first_part, 2)
         later_copy(1).wait_recv()
+        later_copy(2).wait_recv()
         dt_low = lanes_turned(later[2])
 
         def recompute(k):
             for c in range(2):
-                cols = tile_at(2 * k + c)
-                sent = back_projected(later, dt_low, one_ref, k, c, piece)
-                g_ref[:, cols] = (g_ref[:, cols].astype(F32) + sent).astype(BF16)
+                j = 2 * k + c
+                w_b, _, w_t = weight_tiles(one_ref, k, c, piece)
+                sent = base[j] + dot(later[1], w_b, NT)
+                sent += jnp.where(in_top(piece), dot(later[2], w_t, NT), dot(dt_low, w_t, NT))
+                g_ref[:, tile_at(j)] = sent.astype(BF16)
 
         each(n_chip, recompute, 2)
 
@@ -576,7 +585,8 @@
         gate_grad_ref[:, cols] = (g * (y + skip * x_f) * slope).astype(BF16)
         base[j] = inner + skip * grad_y
 
-    each(half, before, UNROLL)
+    early = 12
+    each(early, before, UNROLL)
 
     all_here(chip_passes.at[pl.ds(0, n_chip - 1)], pass_sems.at[3], near)
 
@@ -602,7 +612,7 @@
 
     lax.fori_loop(0, n_chip, scan, jnp.zeros((state, LANES), F32))
     exits[chip] = back[chip]
-    each(half, lambda j: before(half + j), UNROLL)
+    each(2 * half - early, lambda j: before(early + j), UNROLL)
     c_grad = acc_c[...] + dot(acc_scores[...], bf_ref[...], precision=HIGH)
     dproj_ref[0] = c_grad.astype(BF16)
     acc_b[...] += dot(acc_scores[...].T, cf_ref[...], precision=HIGH)
@@ -611,22 +621,19 @@
     def _():
         later_copy(0).start()
 
-    def tiles_of(i):
-        return pl.ds(i, 1 + i)
-
     def dp_copy(i, k):
         return remote(
-            dproj_ref.at[tiles_of(i)], grads.at[core, dp, tiles_of(i)],
+            dproj_ref.at[i], grads.at[core, dp, i],
             grad_sems.at[0, i], dp_recv.at[i, k], near.dp_device(k),
         )
 
     def grad_swap(i, slot):
-        block = grads.at[core, slot, tiles_of(i)]
+        block = grads.at[core, slot, i]
         return remote(block, block, grad_sems.at[1, i], grad_recv.at[i], near.sibling())
 
     def share(i):
         each(n_dp - 1, lambda k: dp_copy(i, k).start())
-        grads[core, dp, tiles_of(i)] = dproj_ref[tiles_of(i)]
+        grads[core, dp, i] = dproj_ref[i]
         grad_swap(i, dp).start()
 
     share(0)
@@ -695,19 +702,26 @@
     each(n_chip // group, mine_group)
     each(n_chip // group, other_group)
 
+    dproj_ref[1] = acc_b[...].astype(BF16)
+
+    @pl.when(pipe == 1)
+    def _():
+        later_copy(1).start()
+
+    share(1)
     u = acc_x[...] + acc_s[...]
     last = jnp.sum(acc_s[...], axis=0, keepdims=True) + acc_a[0:1, :]
     upper = (iota(0) <= iota(1)).astype(F32)
     log_grad = dot(upper, acc_y[...] - acc_s[...], precision=HIGH) + last
     raw_grad = u * rho_ref[...] - small[0:1, :] * log_grad * sig_ref[...]
-    dproj_ref[1] = acc_b[...].astype(BF16)
     dproj_ref[2] = raw_grad.astype(BF16)
 
     @pl.when(pipe == 1)
     def _():
-        later_copy(1).start()
-
-    share(1)
+        later_copy(2).start()
+
+    share(2)
+
     mixed_copy = pltpu.make_async_copy(mixed_grad_ref, mixed_out, out_sems.at[1])
     mixed_copy.start()
     all_here(group_ref.at[pl.ds(0, n_dp - 1)], xg_sems.at[1], near)
@@ -721,12 +735,10 @@
         x = jnp.concatenate([group_ref[k, c].reshape(-1, rows) for k in range(n_dp)], axis=1)
         return dot(x, jnp.concatenate([grads[c, k, tile] for k in range(n_dp)], axis=0))
 
-    def whole_tiles(i):
-        for tile in range(i, 1 + 2 * i):
-            whole[tile] = summed_over(core, tile)
-        all_here(grads.at[1 - core, :, tiles_of(i)], grad_recv.at[i], near)
-        for tile in range(i, 1 + 2 * i):
-            whole[tile] += summed_over(1 - core, tile)
+    def whole_tile(i):
+        whole[i] = summed_over(core, i)
+        all_here(grads.at[1 - core, :, i], grad_recv.at[i], near)
+        whole[i] += summed_over(1 - core, i)
 
     def rows_of(slot):
         return pl.ds(pl.multiple_of(slot * piece, piece), piece)
@@ -739,7 +751,7 @@
 
     def sum_copy(i, k, part, arrived):
         return remote(
-            part.at[near.chip_slot(k)], arrived.at[k], grad_sems.at[2, i], grad_sems.at[3, i],
+            part.at[near.chip_slot(k)], arrived.at[k], sum_sems.at[0, i], sum_sems.at[1, i],
             near.chip_device(k),
         )
 
@@ -752,7 +764,7 @@
         each(n_chip - 1, one)
 
     gathered(0)
-    whole_tiles(0)
+    whole_tile(0)
     ship(0, c_rows, part_c, arrived_c)
     dt_low = lanes_turned(dproj_ref[2])
 
@@ -767,14 +779,16 @@
     input_copy.start()
 
     gathered(1)
-    whole_tiles(1)
+    gathered(2)
+    whole_tile(1)
+    whole_tile(2)
     ship(1, other_rows, part_o, arrived_o)
 
     @pl.when(pipe == 1)
     def _():
         shard_copy.wait_send()
-        later_copy(0).wait_send()
-        later_copy(1).wait_send()
+        for i in range(3):
+            later_copy(i).wait_send()
 
     gather.sent()
     first_chips = pl.ds(0, n_chip - 1)
@@ -784,12 +798,12 @@
     all_sent(back.at[first_chips], send_sems.at[1], near)
     all_sent(other, core_sems.at[1], near)
     all_sent(group_ref.at[pl.ds(0, n_dp - 1)], xg_sems.at[0], near)
-    for i in range(2):
-        all_sent(grads.at[core, pl.ds(0, n_dp - 1), tiles_of(i)], grad_sems.at[0, i], near)
-        all_sent(grads.at[core, :, tiles_of(i)], grad_sems.at[1, i], near)
+    for i in range(3):
+        all_sent(grads.at[core, pl.ds(0, n_dp - 1), i], grad_sems.at[0, i], near)
+        all_sent(grads.at[core, :, i], grad_sems.at[1, i], near)
 
     def collected(i, rows_at, arrived):
-        all_here(arrived, grad_sems.at[3, i], near)
+        all_here(arrived, sum_sems.at[1, i], near)
         total_rows = rows_at(chip)
         for k in range(n_chip - 1):
             total_rows += arrived[k].astype(F32)
@@ -799,8 +813,8 @@
     others = collected(1, other_rows, arrived_o)
     weight_out[:, :LANES] = others[:piece]
     weight_out[:, 2 * LANES :] = below(others[piece:])[:, : cols_w - 2 * LANES]
-    all_sent(arrived_c, grad_sems.at[2, 0], near)
-    all_sent(arrived_o, grad_sems.at[2, 1], near)
+    all_sent(arrived_c, sum_sems.at[0, 0], near)
+    all_sent(arrived_o, sum_sems.at[0, 1], near)
     gate_copy.wait()
     mixed_copy.wait()
     input_copy.wait()
@@ -867,9 +881,9 @@
             pltpu.VMEM((n_chip - 1, packed_rows - piece, LANES), BF16),
             pltpu.VMEM((piece, proj), F32),
             (
-                dma((5,)), dma((3,)), gather_sems(n_chip, n_dp), dma((6,)), dma((2,)), dma((2, 2)), dma((4,)),
+                dma((5,)), dma((3,)), gather_sems(n_chip, n_dp), dma((6,)), dma((2,)), dma((2, 3)), dma((4,)),
                 dma((2,)), dma((n_chip // 2,)), dma((2,)), chips, chips, dma((n_chip // GROUP,)), dma((2,)),
-                dma((2,)), dma((2, n_dp - 1)), dma((4, 2)), dma((2,)),
+                dma((2,)), dma((3, n_dp - 1)), dma((2, 3)), dma((3,)), dma((2, 2)),
             ),
         ],
         compiler_params=pltpu.CompilerParams(

time: 132 us -> 131 us (level)
  no operation moved by 1% of the time
where the time goes in v7:
time: 131 us
  Pallas kernels  131 us (100%)
    pallas_call x1, Pallas kernels, layer_grads(): pl.pallas_call(functools.partial(layer_kernel, n_chip, n_dp), out_shape=(...  128 us
    pallas_call x1, Pallas kernels, deliver(): pl.pallas_call(functools.partial(deliver_kernel, cuts), out_shape=tuple((...  2.82 us

profile of v7, /device:TPU:1, one launch (start us, length us, event | category | flops | bytes accessed | tf_op | source)
XLA Modules:
  0.0 131.3 jit_solution(4223458335826948817)
XLA Ops:
  0.6 127.8 %shard_map.129 = (bf16[128,4096]{1,0:T(8,128)(2,1)}, bf16[128,4096]{1,0:T(8,128)(2,1)}, bf16[128,4096]{1,0:T(8,128)(2,1)}, f32[32,320]{1,0:T(8,128)}) custom-call(bf16[32,320]{1,0:T(8,128)(2,1)} %bitcast.15, bf16[128,4096]{1,0:T(8,128)(2,1)} %bitcast.11, bf16[128,4096]{1,0:T(8,128)(2,1)} %bitcast.12, bf16[128,4096]{1,0:T(8,128)(2,1)} %bitcast.13, ...), custom_call_target="tpu_custom_call" | custom-call | tf_op jit(solution)/shard_map/pallas_call | solution.py:840
  128.5 2.8 %shard_map.130 = (bf16[128,4096]{1,0:T(8,128)(2,1)}, bf16[128,4096]{1,0:T(8,128)(2,1)}, bf16[128,4096]{1,0:T(8,128)(2,1)}, f32[32,320]{1,0:T(8,128)}) custom-call(bf16[128,4096]{1,0:T(8,128)(2,1)} %get-tuple-element.12.refs_0_, bf16[128,4096]{1,0:T(8,128)(2,1)} %get-tuple-element.13.refs_1_, bf16[128,4096]{1,0:T(8,128)(2,1)} %get-tuple-element.14.refs_2_, ...), custom_call_target="tpu_custom_call" | custom-call | tf_op jit(solution)/shard_map/pallas_call | solution.py:919

commit v8 on v7

--- a/solution.py
+++ b/solution.py
@@ -434,17 +434,19 @@
         return by_half(turned[0:1, 0:1], turned[0:1, 1:2])
 
     loads[3].wait()
-    pass_copy.wait()
-    chip_passes[chip] = passes[0] * passes[1]
 
     def chip_pass_copy(k):
         block = chip_passes.at[chip]
         return remote(block, block, pass_sems.at[2], pass_sems.at[3], near.chip_device(k))
 
-    each(n_chip - 1, lambda k: chip_pass_copy(k).start())
+    def spread_passes():
+        pass_copy.wait()
+        chip_passes[chip] = passes[0] * passes[1]
+        each(n_chip - 1, lambda k: chip_pass_copy(k).start())
 
     @pl.when(pipe == 0)
     def _():
+        spread_passes()
         shard_copy.wait_recv()
         LateGather(near, one_ref, one_set).run(one_shard)
         later_copy(0).wait_recv()
@@ -522,6 +524,11 @@
         own_mine(c, couple)
 
     own_theirs(0)
+
+    @pl.when(pipe == 1)
+    def _():
+        spread_passes()
+
     each(n_chip // couple - 1, own_step)
     own_mine(n_chip // couple - 1, couple - 1)
     got[chip] = total[chip]
@@ -585,7 +592,7 @@
         gate_grad_ref[:, cols] = (g * (y + skip * x_f) * slope).astype(BF16)
         base[j] = inner + skip * grad_y
 
-    early = 12
+    early = 8
     each(early, before, UNROLL)
 
     all_here(chip_passes.at[pl.ds(0, n_chip - 1)], pass_sems.at[3], near)

time: 131 us -> 134 us (1.023)
  Pallas kernels: 131 us -> 134 us
    pallas_call x1, Pallas kernels: 128 us -> 131 us  [layer_grads(): pl.pallas_call(functools.partial(layer_kernel, n_chip, n_dp), out_shape=(...]
where the time goes in v8:
time: 134 us
  Pallas kernels  134 us (100%)
    pallas_call x1, Pallas kernels, layer_grads(): pl.pallas_call(functools.partial(layer_kernel, n_chip, n_dp), out_shape=(...  131 us
    pallas_call x1, Pallas kernels, deliver(): pl.pallas_call(functools.partial(deliver_kernel, cuts), out_shape=tuple((...  2.82 us

profile of v8, /device:TPU:1, one launch (start us, length us, event | category | flops | bytes accessed | tf_op | source)
XLA Modules:
  0.0 134.3 jit_solution(12212283056961748270)
XLA Ops:
  0.6 130.9 %shard_map.129 = (bf16[128,4096]{1,0:T(8,128)(2,1)}, bf16[128,4096]{1,0:T(8,128)(2,1)}, bf16[128,4096]{1,0:T(8,128)(2,1)}, f32[32,320]{1,0:T(8,128)}) custom-call(bf16[32,320]{1,0:T(8,128)(2,1)} %bitcast.15, bf16[128,4096]{1,0:T(8,128)(2,1)} %bitcast.11, bf16[128,4096]{1,0:T(8,128)(2,1)} %bitcast.12, bf16[128,4096]{1,0:T(8,128)(2,1)} %bitcast.13, ...), custom_call_target="tpu_custom_call" | custom-call | tf_op jit(solution)/shard_map/pallas_call | solution.py:847
  131.5 2.8 %shard_map.130 = (bf16[128,4096]{1,0:T(8,128)(2,1)}, bf16[128,4096]{1,0:T(8,128)(2,1)}, bf16[128,4096]{1,0:T(8,128)(2,1)}, f32[32,320]{1,0:T(8,128)}) custom-call(bf16[128,4096]{1,0:T(8,128)(2,1)} %get-tuple-element.12.refs_0_, bf16[128,4096]{1,0:T(8,128)(2,1)} %get-tuple-element.13.refs_1_, bf16[128,4096]{1,0:T(8,128)(2,1)} %get-tuple-element.14.refs_2_, ...), custom_call_target="tpu_custom_call" | custom-call | tf_op jit(solution)/shard_map/pallas_call | solution.py:926
